TPU v7x, 1024 devices: a whole 8x8x8 slice. The times are simulated.
1024 devices in a mesh: dp: 64 (over z_hi, y, core), tensor: 16 (over z_lo, x).
Axes of the slice: x: 8, y: 8, z: 8 (z_hi: 4, z_lo: 2; z = z_hi * 2 + z_lo), core: 2. Of those that a mesh axis runs over, the one named last changes fastest.
Arguments:
- tokens: bfloat16 [8192, 4096], P(('dp', 'tensor')), may hold values from -6 to 6
- grad_out: bfloat16 [8192, 4096], P(('dp', 'tensor')), may hold values from -6 to 6
- gate_tiles: bfloat16 [16, 16, 128, 128], P('tensor'), may hold values from -0.25 to 0.25
- up_tiles: bfloat16 [16, 16, 128, 128], P('tensor'), may hold values from -0.25 to 0.25
- down_tiles: bfloat16 [16, 16, 128, 128], P('tensor'), may hold values from -0.1875 to 0.1875
- gate_index: int32 [16, 16], P('tensor'), may hold values from -1 to 127, as said below
- up_index: int32 [16, 16], P('tensor'), may hold values from -1 to 127, as said below
- down_index: int32 [16, 16], P('tensor'), may hold values from -1 to 127, as said below
Outputs:
- input_grad: bfloat16 [8192, 4096], P(('dp', 'tensor'))
- tile_grads: float32 [16, 2048, 384], P('tensor', 'dp')
Inputs may be any that keep to these rules, and one draw needn't show every extreme that they name: `gate_index`: in each index array every row lists distinct positions in its first slots and -1 in the rest; each row uses at least 5 slots and some row uses all 16. `up_index`: as for gate_index, drawn apart. `down_index`: as for gate_index, drawn apart.
All inputs are finite; a program needn't handle non-finite values.
Results may differ from a plain program's by a relative error of at most 0.017.
Values may be sent and summed in bfloat16 or wider, within the bound.
No kernel may reach another device: no remote copies, remote signals or barrier semaphores. Data moves between devices by JAX's collectives and lax.ppermute only.
A program may use at most 32 MiB of HBM per device.

v0:
```python
import jax
import jax.numpy as jnp
from jax import lax
from jax.sharding import PartitionSpec as P

FF = 8192


def split_index(index, width):
    live = index >= 0
    safe = jnp.where(live, index, 0)
    return (safe // width, safe % width, live)


def place_add(target, slot_vals, picks, live):
    masked = jnp.where(live[None, :, None], slot_vals, 0.0)
    return target.at[:, picks].add(masked)


def product(form, left, right):
    return jnp.einsum(form, left, right, preferred_element_type=jnp.float32)


def per_device(
    tokens, grad_out, gate_tiles, up_tiles, down_tiles, gate_index, up_index, down_index
):
    whole_rows, whole_grads = (
        lax.all_gather(tokens, "tensor", axis=0, tiled=True),
        lax.all_gather(grad_out, "tensor", axis=0, tiled=True),
    )
    tile = gate_tiles.shape[-1]
    rows = whole_rows.shape[0]
    blocks = whole_rows.shape[1] // tile
    hidden_blocks = FF // tile // lax.axis_size("tensor")
    gate_w, up_w, down_w = (gate_tiles[0], up_tiles[0], down_tiles[0])
    g_row, g_col, g_live = split_index(gate_index[0], hidden_blocks)
    u_row, u_col, u_live = split_index(up_index[0], hidden_blocks)
    d_hid, d_col, d_live = split_index(down_index[0], blocks)
    x_blocks = whole_rows.reshape(rows, blocks, tile)
    dy_blocks = whole_grads.reshape(rows, blocks, tile)
    g_sel = jnp.take(x_blocks, g_row, axis=1)
    u_sel = jnp.take(x_blocks, u_row, axis=1)
    hidden_zero = jnp.zeros((rows, hidden_blocks, tile), jnp.float32)
    gate = place_add(hidden_zero, product("rsk,skn->rsn", g_sel, gate_w), g_col, g_live)
    up = place_add(hidden_zero, product("rsk,skn->rsn", u_sel, up_w), u_col, u_live)
    sig = jax.nn.sigmoid(gate)
    act = gate * sig
    hidden = (act * up).astype(jnp.bfloat16)
    dy_sel = jnp.take(dy_blocks, d_col, axis=1)
    dhidden = place_add(hidden_zero, product("rsn,skn->rsk", dy_sel, down_w), d_hid, d_live)
    h_sel = jnp.take(hidden, d_hid, axis=1)
    down_grad = product("rsk,rsn->skn", h_sel, dy_sel) * d_live[:, None, None].astype(jnp.float32)
    dgate = (dhidden * up * sig * (1.0 + gate * (1.0 - sig))).astype(jnp.bfloat16)
    dup = (dhidden * act).astype(jnp.bfloat16)
    dg_sel = jnp.take(dgate, g_col, axis=1)
    du_sel = jnp.take(dup, u_col, axis=1)
    width_zero = jnp.zeros((rows, blocks, tile), jnp.float32)
    part = place_add(width_zero, product("rsn,skn->rsk", dg_sel, gate_w), g_row, g_live)
    part = place_add(part, product("rsn,skn->rsk", du_sel, up_w), u_row, u_live)
    input_sum = lax.psum_scatter(
        part.reshape(rows, blocks * tile).astype(jnp.bfloat16),
        "tensor",
        scatter_dimension=0,
        tiled=True,
    )
    gate_grad = product("rsk,rsn->skn", g_sel, dg_sel) * g_live[:, None, None].astype(jnp.float32)
    up_grad = product("rsk,rsn->skn", u_sel, du_sel) * u_live[:, None, None].astype(jnp.float32)
    term = jnp.concatenate([gate_grad, up_grad, down_grad], axis=2).reshape(-1, 3 * tile)
    sums = lax.psum_scatter(term, "dp", scatter_dimension=0, tiled=True)
    return (input_sum, sums[None])


def solution(mesh):
    return jax.shard_map(
        per_device,
        mesh=mesh,
        in_specs=(
            P(("dp", "tensor"), None),
            P(("dp", "tensor"), None),
            P("tensor", None, None, None),
            P("tensor", None, None, None),
            P("tensor", None, None, None),
            P("tensor", None),
            P("tensor", None),
            P("tensor", None),
        ),
        out_specs=(P(("dp", "tensor"), None), P("tensor", "dp", None)),
        check_vma=False,
    )
```

profile of v0, /device:TPU:14, one launch (start us, length us, event | category | flops | bytes accessed | tf_op | source)
XLA Modules:
  0.0 451.0 jit_solution(16101580746292270558)
XLA Ops:
  8.0 0.7 all-gather.3.cloned.1.call-update
  14.8 80.3 %all-gather.5.cloned.1.call-done = bf16[128,4096]{1,0:T(8,128)(2,1)} async-done(((bf16[8,4096]{1,0:T(8,128)(2,1)}), bf16[128,4096]{1,0:T(8,128)(2,1)}) %all-gather.5.cloned.1.call-update) | async-done | bytes 1048592 | tf_op jit(solution)/shard_map/all_gather | solution.py:28
  95.1 1.6 copy.32
  98.7 71.6 %all-gather.3.cloned.1.call-done = bf16[128,4096]{1,0:T(8,128)(2,1)} async-done(((bf16[8,4096]{1,0:T(8,128)(2,1)}), bf16[128,4096]{1,0:T(8,128)(2,1)}) %all-gather.3.cloned.1.call-update) | async-done | bytes 1048592 | tf_op jit(solution)/shard_map/all_gather | solution.py:29
  170.3 1.6 copy.30
  171.9 1.3 copy.31
  173.2 1.9 gather_fusion
  175.1 1.6 convolution_select_fusion.3
  176.7 1.6 scatter_fusion.1
  178.7 1.6 scatter_fusion.2
  180.4 1.6 convolution_select_fusion.4
  181.9 1.6 scatter_fusion
  185.1 1.5 convolution_select_fusion.1
  186.6 1.5 convolution_select_fusion
  188.4 2.6 scatter_fusion.3
  191.0 2.6 scatter_fusion.4
  193.6 1.2 convert_element_type.41
  194.8 2.3 copy.35
  197.1 2.3 copy.44
  199.5 1.4 gather_fusion.5
  202.4 2.0 pad_maximum_fusion
  204.4 3.5 copy.39
  207.9 65.4 %reduce-scatter.7.cloned.1.call-done = bf16[8,4096]{1,0:T(8,128)(2,1)} async-done(((bf16[128,4096]{1,0:T(8,128)(2,1)}), bf16[8,4096]{1,0:T(8,128)(2,1)}) %reduce-scatter.7.cloned.1.call-update) | async-done | bytes 65552
  273.4 171.1 %reduce-scatter.5.cloned.1.call-done = f32[32,384]{1,0:T(8,128)} async-done(((f32[2048,384]{1,0:T(8,128)}), f32[32,384]{1,0:T(8,128)}) %reduce-scatter.5.cloned.1.call-update) | async-done | bytes 49168 | tf_op jit(solution)/shard_map/reduce_scatter | solution.py:69
  (60 shorter events, 12.5 us)
Async XLA Ops:
  7.2 171.2 %copy-start = (bf16[1,16,128,128]{3,2,1,0:T(8,128)(2,1)S(1)}, bf16[1,16,128,128]{3,2,1,0:T(8,128)(2,1)}, u32[]{:S(2)}) copy-start(bf16[1,16,128,128]{3,2,1,0:T(8,128)(2,1)} %param.14) | copy-start | bytes 1572868
  7.2 87.9 %all-gather.5.cloned.1.call-start = ((), (), s32[]{:S(2)}) async-start(), calls=%async_computation.3 | async-start | bytes 1114112 | tf_op jit(solution)/shard_map/all_gather | solution.py:28
  7.9 162.4 %all-gather.3.cloned.1.call-start = ((), (), s32[]{:S(2)}) async-start(), calls=%async_computation.2 | async-start | bytes 1114112 | tf_op jit(solution)/shard_map/all_gather | solution.py:29
  8.7 264.7 %reduce-scatter.7.cloned.1.call-start = ((), (), s32[]{:S(2)}) async-start(), calls=%async_computation.5 | async-start | bytes 1114112
  98.1 77.0 %copy-start.3 = (bf16[16,128,128]{2,1,0:T(8,128)(2,1)}, bf16[16,128,128]{2,1,0:T(8,128)(2,1)S(1)}, u32[]{:S(2)}) copy-start(bf16[16,128,128]{2,1,0:T(8,128)(2,1)S(1)} %gather_fusion.1) | copy-start | bytes 1572868
  175.1 5.3 %copy-start.1 = (bf16[16,128,128]{2,1,0:T(8,128)(2,1)}, bf16[16,128,128]{2,1,0:T(8,128)(2,1)S(1)}, u32[]{:S(2)}) copy-start(bf16[16,128,128]{2,1,0:T(8,128)(2,1)S(1)} %gather_fusion) | copy-start | bytes 1572868
  183.6 3.0 copy-start.9
  184.4 2.2 copy-start.7
  185.1 1.5 copy-start.5
  194.8 6.2 %copy-start.4 = (bf16[16,128,128]{2,1,0:T(8,128)(2,1)S(1)}, bf16[16,128,128]{2,1,0:T(8,128)(2,1)}, u32[]{:S(2)}) copy-start(bf16[16,128,128]{2,1,0:T(8,128)(2,1)} %copy-done.3) | copy-start | bytes 1572868
  194.8 6.2 %copy-start.8 = (bf16[16,128,128]{2,1,0:T(8,128)(2,1)S(1)}, bf16[16,128,128]{2,1,0:T(8,128)(2,1)}, u32[]{:S(2)}) copy-start(bf16[16,128,128]{2,1,0:T(8,128)(2,1)} %copy-done.7) | copy-start | bytes 1572868
  197.1 4.3 copy-start.6
  199.4 2.4 copy-start.2
  199.5 245.0 %reduce-scatter.5.cloned.1.call-start = ((), (), s32[]{:S(2)}) async-start(), calls=%async_computation.4 | async-start | bytes 3194880 | tf_op jit(solution)/shard_map/reduce_scatter | solution.py:69
  200.9 1.0 copy-start.10
Sparse Core Ops, SparseCore 0:
  10.7 84.3 all-gather.4
  97.8 72.4 all-gather.2
  199.6 73.7 reduce-scatter.6
  280.6 163.7 reduce-scatter.4
where the time goes:
time: 452 us; the launch traced here: 451 us
  waiting for transfers between devices  390 us (86%)
  local copies, waits for them, and re-layouts  19.7 us (4%)
  other arithmetic  19.4 us (4%)
  between operations  14.1 us (3%)
  matrix products  7.87 us (2%)
    reduce_scatter x1, waiting for transfers between devices, per_device(): sums = lax.psum_scatter(term, 'dp', scatter_dimension=0, tiled=True)  171 us
    all_gather x1, waiting for transfers between devices, per_device(): lax.all_gather(tokens, 'tensor', axis=0, tiled=True)  80.3 us
    all_gather x1, waiting for transfers between devices, per_device(): lax.all_gather(grad_out, 'tensor', axis=0, tiled=True)  71.6 us
    unnamed x5, waiting for transfers between devices  66.8 us
    scatter-add x5, other arithmetic, place_add(): return target.at[:, picks].add(masked)  10 us
  transfers between devices with their start and end apart: 4, of which 4 were waited for; matrix products, arithmetic and copies ran while one was open for 4% of the time, Pallas kernels for 0%

commit v1 on v0

v1 whole, which is shorter than its diff:
```python
import jax
import jax.numpy as jnp
from jax import lax
from jax.experimental import pallas as pl
from jax.experimental.pallas import tpu as pltpu
from jax.sharding import Mesh, PartitionSpec as P

TILE = 128
DP = ("zh", "y", "c")
TEN = ("zl", "x")
F32 = jnp.float32
BF16 = jnp.bfloat16


def lanes(ref, tile_at):
    return ref[:, pl.ds(pl.multiple_of(tile_at * TILE, TILE), TILE)]


def dot(left, right, on):
    return lax.dot_general(left, right, ((on[:1], on[1:]), ((), ())), preferred_element_type=F32)


def front(
    g_idx, u_idx, d_idx, core, xa, gw, uw, dw, mine, theirs, dgate, dup, gate, up, dhid, hid
):
    slots = gw.shape[0]
    blocks = xa.shape[1] // TILE // 2
    for acc in (gate, up, dhid):
        acc[...] = jnp.zeros_like(acc)
    for s in range(slots):
        for idx, w, acc in ((g_idx, gw, gate), (u_idx, uw, up)):
            v = idx[0, s]
            safe = jnp.maximum(v, 0)
            col = safe & 3
            val = dot(lanes(xa, safe >> 2), w[s], (1, 0))
            acc[col] += jnp.where(v >= 0, val, 0.0)
        v = d_idx[0, s]
        safe = jnp.maximum(v, 0)
        val = dot(lanes(xa, blocks + safe % blocks), dw[s], (1, 1))
        row = safe // blocks
        dhid[row] += jnp.where(v >= 0, val, 0.0)
    for b in range(gate.shape[0]):
        g, u, dh = gate[b], up[b], dhid[b]
        sig = jax.nn.sigmoid(g)
        act = g * sig
        hid[b] = (act * u).astype(BF16)
        dgate[b] = (dh * u * sig * (1.0 + g * (1.0 - sig))).astype(BF16)
        dup[b] = (dh * act).astype(BF16)
    first = core[0] == 0
    for s in range(slots):
        outs = []
        for idx, grad in ((g_idx, dgate), (u_idx, dup)):
            v = idx[0, s]
            safe = jnp.maximum(v, 0)
            val = dot(lanes(xa, safe >> 2), grad[safe & 3], (0, 0))
            outs.append(jnp.where(v >= 0, val, 0.0))
        v = d_idx[0, s]
        safe = jnp.maximum(v, 0)
        val = dot(hid[safe // blocks], lanes(xa, blocks + safe % blocks), (0, 0))
        outs.append(jnp.where(v >= 0, val, 0.0))
        for k, val in enumerate(outs):
            for half in range(2):
                even = val[64 * half : 64 * half + 32]
                odd = val[64 * half + 32 : 64 * half + 64]
                at = (2 * s + half, slice(None), slice(k * TILE, (k + 1) * TILE))
                mine[at] = jnp.where(first, even, odd)
                theirs[at] = jnp.where(first, odd, even).astype(BF16)


def back(g_idx, u_idx, dgate, dup, gw, uw, part, acc):
    acc[...] = jnp.zeros_like(acc)
    for s in range(gw.shape[0]):
        for idx, w, grad in ((g_idx, gw, dgate), (u_idx, uw, dup)):
            v = idx[0, s]
            safe = jnp.maximum(v, 0)
            val = dot(grad[safe & 3], w[s], (1, 1))
            row = safe >> 2
            acc[row] += jnp.where(v >= 0, val, 0.0)
    for b in range(acc.shape[0]):
        part[:, b * TILE : (b + 1) * TILE] = acc[b].astype(BF16)


SMEM = pl.BlockSpec(memory_space=pltpu.SMEM)
VMEM = pl.BlockSpec(memory_space=pltpu.VMEM)


def per_device(
    tokens, grad_out, gate_tiles, up_tiles, down_tiles, gate_index, up_index, down_index
):
    here, width = tokens.shape
    ten, dp = lax.axis_size(TEN), lax.axis_size(DP)
    rows, slots = here * ten, gate_tiles.shape[1]
    blocks = width // TILE
    hidden = 4
    gw, uw, dw = gate_tiles[0], up_tiles[0], down_tiles[0]
    core = lax.axis_index("c").astype(jnp.int32).reshape(1)
    with jax.named_scope("gather"):
        both = jnp.concatenate([tokens, grad_out], axis=1)
        send = jnp.broadcast_to(both[None], (ten, here, 2 * width))
        xa = lax.all_to_all(send, TEN, 0, 0, tiled=True).reshape(rows, 2 * width)
    half = dp // 2
    mine, theirs, dgate, dup = pl.pallas_call(
        front,
        out_shape=(
            jax.ShapeDtypeStruct((half, 32, 3 * TILE), F32),
            jax.ShapeDtypeStruct((half, 32, 3 * TILE), BF16),
            jax.ShapeDtypeStruct((hidden, rows, TILE), BF16),
            jax.ShapeDtypeStruct((hidden, rows, TILE), BF16),
        ),
        in_specs=[SMEM] * 4 + [VMEM] * 4,
        out_specs=(VMEM,) * 4,
        scratch_shapes=[pltpu.VMEM((hidden, rows, TILE), F32)] * 3
        + [pltpu.VMEM((hidden, rows, TILE), BF16)],
        compiler_params=pltpu.CompilerParams(vmem_limit_bytes=24 << 20),
        cost_estimate=pl.CostEstimate(
            flops=96 * 2 * TILE**3, bytes_accessed=8 << 20, transcendentals=1 << 16
        ),
        name="front",
    )(gate_index, up_index, down_index, core, xa, gw, uw, dw)
    with jax.named_scope("cores"):
        got = lax.ppermute(theirs, "c", [(0, 1), (1, 0)])
    part = pl.pallas_call(
        back,
        out_shape=jax.ShapeDtypeStruct((rows, width), BF16),
        in_specs=[SMEM] * 2 + [VMEM] * 4,
        out_specs=VMEM,
        scratch_shapes=[pltpu.VMEM((blocks, rows, TILE), F32)],
        compiler_params=pltpu.CompilerParams(vmem_limit_bytes=16 << 20),
        cost_estimate=pl.CostEstimate(
            flops=32 * 2 * TILE**3, bytes_accessed=3 << 20, transcendentals=0
        ),
        name="back",
    )(gate_index, up_index, dgate, dup, gw, uw)
    with jax.named_scope("partials"):
        parts = lax.all_to_all(part.reshape(ten, here, width), TEN, 0, 0, tiled=True)
        input_sum = jnp.sum(parts.astype(F32), axis=0).astype(BF16)
    with jax.named_scope("tile_sums"):
        pair = (mine + got.astype(F32)).astype(BF16)
        grads = lax.all_to_all(pair, ("zh", "y"), 0, 0, tiled=True)
        sums = jnp.sum(grads.astype(F32), axis=0)
    return (input_sum, sums[None])


def solution(mesh):
    fine = Mesh(mesh.devices.reshape(4, 8, 2, 2, 8), DP + TEN)
    both = P(DP + TEN, None)
    return jax.shard_map(
        per_device,
        mesh=fine,
        in_specs=(both, both)
        + (P(TEN, None, None, None),) * 3
        + (P(TEN, None),) * 3,
        out_specs=(both, P(TEN, DP, None)),
        check_vma=False,
    )
```

time: 452 us -> 147 us (0.33)
  the two profiles are of different devices: /device:TPU:14 before, /device:TPU:16 now
where the time goes in v1:
time: 147 us; the launch traced here: 146 us
  waiting for transfers between devices  96.2 us (65%)
  starting transfers between devices  38.5 us (26%)
  Pallas kernels  4.83 us (3%)
  other arithmetic  3.56 us (2%)
  local copies, waits for them, and re-layouts  2.6 us (2%)
    all_to_all x1, waiting for transfers between devices, per_device(): xa = lax.all_to_all(send, TEN, 0, 0, tiled=True).reshape(rows, 2 * width)  49 us
    all_to_all x1, waiting for transfers between devices, per_device(): grads = lax.all_to_all(pair, ('zh', 'y'), 0, 0, tiled=True)  23.1 us
    all_to_all x1, waiting for transfers between devices, per_device(): lax.all_to_all(part.reshape(ten, here, width), TEN, 0, 0, tiled=True)  21.7 us
    all_to_all x1, starting transfers between devices, per_device(): grads = lax.all_to_all(pair, ('zh', 'y'), 0, 0, tiled=True)  21.1 us
    all_to_all x1, starting transfers between devices, per_device(): xa = lax.all_to_all(send, TEN, 0, 0, tiled=True).reshape(rows, 2 * width)  9.73 us
    all_to_all x1, starting transfers between devices, per_device(): lax.all_to_all(part.reshape(ten, here, width), TEN, 0, 0, tiled=True)  5.79 us
  transfers between devices with their start and end apart: 4, of which 4 were waited for; matrix products, arithmetic and copies ran while one was open for 1% of the time, Pallas kernels for 0%

profile of v1, /device:TPU:16, one launch (start us, length us, event | category | flops | bytes accessed | tf_op | source)
XLA Modules:
  0.0 146.4 jit_solution(12222748791487455859)
XLA Ops:
  0.6 0.9 pad_maximum_fusion
  1.5 1.5 %broadcast_in_dim.4 = bf16[16,8,8192]{2,1,0:T(8,128)(2,1)} broadcast(bf16[8,8192]{1,0:T(8,128)(2,1)S(1)} %pad_maximum_fusion), dimensions={1,2} | broadcast | bytes 2228224 | tf_op jit(solution)/shard_map/gather/broadcast_in_dim | solution.py:99
  3.1 0.0 copy-start.7
  3.1 9.7 %all-to-all-start = ((bf16[16,8,8192]{2,1,0:T(8,128)(2,1)}), bf16[16,8,8192]{2,1,0:T(8,128)(2,1)S(1)}, u32[]{:S(2)}, u32[]{:S(2)}) async-start(bf16[16,8,8192]{2,1,0:T(8,128)(2,1)} %broadcast_in_dim.4), calls=%async_computation | async-start | bytes 4194304 | tf_op jit(solution)/shard_map/gather/all_to_all | solution.py:100
  12.8 49.0 %all-to-all-done = bf16[16,8,8192]{2,1,0:T(8,128)(2,1)S(1)} async-done(((bf16[16,8,8192]{2,1,0:T(8,128)(2,1)}), bf16[16,8,8192]{2,1,0:T(8,128)(2,1)S(1)}, u32[]{:S(2)}, u32[]{:S(2)}) %all-to-all-start) | async-done | bytes 2097184 | tf_op jit(solution)/shard_map/gather/all_to_all | solution.py:100
  61.8 0.0 copy-done
  61.8 0.0 copy-done.1
  61.8 0.0 copy-done.5
  61.8 0.0 copy-done.6
  61.8 0.0 copy-done.7
  61.8 0.0 copy-start.4
  61.8 1.0 copy-done.4
  62.9 2.2 %front.1 = (f32[32,32,384]{2,1,0:T(8,128)S(1)}, bf16[32,32,384]{2,1,0:T(8,128)(2,1)S(1)}, bf16[4,128,128]{2,1,0:T(8,128)(2,1)S(1)}, bf16[4,128,128]{2,1,0:T(8,128)(2,1)S(1)}) custom-call(s32[1,16]{1,0:T(1,128)S(1)} %copy-done.5, s32[1,16]{1,0:T(1,128)S(1)} %copy-done.6, s32[1,16]{1,0:T(1,128)S(1)} %copy-done.7, s32[1]{0:T(128)} %bitcast.core, ...), custom_call_target="tpu_custom_call" | custom-call | flops 402653184 | bytes 8388608 | tf_op jit(solution)/shard_map/front/pallas_call | solution.py:102
  65.1 2.6 %back.1 = bf16[128,4096]{1,0:T(8,128)(2,1)} custom-call(s32[1,16]{1,0:T(1,128)S(1)} %copy-done.5, s32[1,16]{1,0:T(1,128)S(1)} %copy-done.6, bf16[4,128,128]{2,1,0:T(8,128)(2,1)S(1)} %get-tuple-element.6.dgate, bf16[4,128,128]{2,1,0:T(8,128)(2,1)S(1)} %get-tuple-element.7.dup, bf16[16,128,128]{2,1,0:T(8,128)(2,1)S(1)} %bitcast.9, ...), custom_call_target="tpu_custom_call" | custom-call | flops 134217728 | bytes 3145728 | tf_op jit(solution)/shard_map/back/pallas_call | solution.py:122
  67.7 0.0 copy-done.8
  67.7 5.8 %all-to-all-start.1 = ((bf16[16,8,4096]{2,1,0:T(8,128)(2,1)}), bf16[16,8,4096]{2,1,0:T(8,128)(2,1)S(1)}, u32[]{:S(2)}, u32[]{:S(2)}) async-start(bf16[16,8,4096]{2,1,0:T(8,128)(2,1)} %bitcast.5), calls=%async_computation.1 | async-start | bytes 2097152 | tf_op jit(solution)/shard_map/partials/all_to_all | solution.py:135
  73.5 1.9 %collective-permute-start = (bf16[32,32,384]{2,1,0:T(8,128)(2,1)}, bf16[32,32,384]{2,1,0:T(8,128)(2,1)S(1)}, u32[]{:S(2)}, u32[]{:S(2)}) collective-permute-start(bf16[32,32,384]{2,1,0:T(8,128)(2,1)} %copy-done.8), channel_id=1, source_target_pairs={{0,16},{16,0},{1,17},{17,1},{2,18},{18,2},{3,19},{19,3},{4,20},{20... | collective-permute-start | bytes 2359304 | tf_op jit(solution)/shard_map/cores/ppermute | solution.py:121
  75.5 2.5 %collective-permute-done = bf16[32,32,384]{2,1,0:T(8,128)(2,1)S(1)} collective-permute-done((bf16[32,32,384]{2,1,0:T(8,128)(2,1)}, bf16[32,32,384]{2,1,0:T(8,128)(2,1)S(1)}, u32[]{:S(2)}, u32[]{:S(2)}) %collective-permute-start) | collective-permute-done | bytes 786464 | tf_op jit(solution)/shard_map/cores/ppermute | solution.py:121
  77.9 1.2 add_convert_fusion
  79.1 21.7 %all-to-all-done.1 = bf16[16,8,4096]{2,1,0:T(8,128)(2,1)S(1)} async-done(((bf16[16,8,4096]{2,1,0:T(8,128)(2,1)}), bf16[16,8,4096]{2,1,0:T(8,128)(2,1)S(1)}, u32[]{:S(2)}, u32[]{:S(2)}) %all-to-all-start.1) | async-done | bytes 1048608 | tf_op jit(solution)/shard_map/partials/all_to_all | solution.py:135
  100.8 21.1 %all-to-all-start.2 = ((bf16[32,32,384]{2,1,0:T(8,128)(2,1)}), bf16[32,32,384]{2,1,0:T(8,128)(2,1)S(1)}, u32[]{:S(2)}, u32[]{:S(2)}) async-start(bf16[32,32,384]{2,1,0:T(8,128)(2,1)} %add_convert_fusion), calls=%async_computation.2 | async-start | bytes 1572864 | tf_op jit(solution)/shard_map/tile_sums/all_to_all | solution.py:139
  121.8 0.8 reduce_sum.21
  122.6 23.1 %all-to-all-done.2 = bf16[32,32,384]{2,1,0:T(8,128)(2,1)S(1)} async-done(((bf16[32,32,384]{2,1,0:T(8,128)(2,1)}), bf16[32,32,384]{2,1,0:T(8,128)(2,1)S(1)}, u32[]{:S(2)}, u32[]{:S(2)}) %all-to-all-start.2) | async-done | bytes 786464 | tf_op jit(solution)/shard_map/tile_sums/all_to_all | solution.py:139
  145.7 0.7 convert_reduce_fusion
  (9 shorter events, 0.0 us)
Async XLA Ops:
  3.0 58.7 %copy-start = (bf16[1,16,128,128]{3,2,1,0:T(8,128)(2,1)S(1)}, bf16[1,16,128,128]{3,2,1,0:T(8,128)(2,1)}, u32[]{:S(2)}) copy-start(bf16[1,16,128,128]{3,2,1,0:T(8,128)(2,1)} %param.10) | copy-start | bytes 1572868
  3.1 58.7 %copy-start.1 = (bf16[1,16,128,128]{3,2,1,0:T(8,128)(2,1)S(1)}, bf16[1,16,128,128]{3,2,1,0:T(8,128)(2,1)}, u32[]{:S(2)}) copy-start(bf16[1,16,128,128]{3,2,1,0:T(8,128)(2,1)} %param.11) | copy-start | bytes 1572868
  3.1 58.7 %copy-start.5 = (s32[1,16]{1,0:T(1,128)S(1)}, s32[1,16]{1,0:T(1,128)}, u32[]{:S(2)}) copy-start(s32[1,16]{1,0:T(1,128)} %g_idx.3) | copy-start | bytes 196
  3.1 58.7 %copy-start.6 = (s32[1,16]{1,0:T(1,128)S(1)}, s32[1,16]{1,0:T(1,128)}, u32[]{:S(2)}) copy-start(s32[1,16]{1,0:T(1,128)} %u_idx.3) | copy-start | bytes 196
  3.1 58.7 %copy-start.7 = (s32[1,16]{1,0:T(1,128)S(1)}, s32[1,16]{1,0:T(1,128)}, u32[]{:S(2)}) copy-start(s32[1,16]{1,0:T(1,128)} %d_idx.1) | copy-start | bytes 196
  3.1 58.7 %all-to-all-start = ((bf16[16,8,8192]{2,1,0:T(8,128)(2,1)}), bf16[16,8,8192]{2,1,0:T(8,128)(2,1)S(1)}, u32[]{:S(2)}, u32[]{:S(2)}) async-start(bf16[16,8,8192]{2,1,0:T(8,128)(2,1)} %broadcast_in_dim.4), calls=%async_computation | async-start | bytes 4194304 | tf_op jit(solution)/shard_map/gather/all_to_all | solution.py:100
  61.8 1.0 copy-start.4
  65.1 2.6 %copy-start.2 = (f32[32,32,384]{2,1,0:T(8,128)}, f32[32,32,384]{2,1,0:T(8,128)S(1)}, u32[]{:S(2)}) copy-start(f32[32,32,384]{2,1,0:T(8,128)S(1)} %get-tuple-element.8) | copy-start | bytes 4718596
  65.1 2.6 %copy-start.8 = (bf16[32,32,384]{2,1,0:T(8,128)(2,1)}, bf16[32,32,384]{2,1,0:T(8,128)(2,1)S(1)}, u32[]{:S(2)}) copy-start(bf16[32,32,384]{2,1,0:T(8,128)(2,1)S(1)} %get-tuple-element.9) | copy-start | bytes 2359300
  67.7 10.2 %copy-start.3 = (f32[32,32,384]{2,1,0:T(8,128)S(1)}, f32[32,32,384]{2,1,0:T(8,128)}, u32[]{:S(2)}) copy-start(f32[32,32,384]{2,1,0:T(8,128)} %copy-done.2) | copy-start | bytes 4718596
  67.7 33.0 %all-to-all-start.1 = ((bf16[16,8,4096]{2,1,0:T(8,128)(2,1)}), bf16[16,8,4096]{2,1,0:T(8,128)(2,1)S(1)}, u32[]{:S(2)}, u32[]{:S(2)}) async-start(bf16[16,8,4096]{2,1,0:T(8,128)(2,1)} %bitcast.5), calls=%async_computation.1 | async-start | bytes 2097152 | tf_op jit(solution)/shard_map/partials/all_to_all | solution.py:135
  73.5 4.4 %collective-permute-start = (bf16[32,32,384]{2,1,0:T(8,128)(2,1)}, bf16[32,32,384]{2,1,0:T(8,128)(2,1)S(1)}, u32[]{:S(2)}, u32[]{:S(2)}) collective-permute-start(bf16[32,32,384]{2,1,0:T(8,128)(2,1)} %copy-done.8), channel_id=1, source_target_pairs={{0,16},{16,0},{1,17},{17,1},{2,18},{18,2},{3,19},{19,3},{4,20},{20... | collective-permute-start | bytes 2359304 | tf_op jit(solution)/shard_map/cores/ppermute | solution.py:121
  100.8 44.9 %all-to-all-start.2 = ((bf16[32,32,384]{2,1,0:T(8,128)(2,1)}), bf16[32,32,384]{2,1,0:T(8,128)(2,1)S(1)}, u32[]{:S(2)}, u32[]{:S(2)}) async-start(bf16[32,32,384]{2,1,0:T(8,128)(2,1)} %add_convert_fusion), calls=%async_computation.2 | async-start | bytes 1572864 | tf_op jit(solution)/shard_map/tile_sums/all_to_all | solution.py:139

commit v2 on v1

v2 whole, which is shorter than its diff:
```python
import jax
import jax.numpy as jnp
from jax import lax
from jax.experimental import pallas as pl
from jax.experimental.pallas import tpu as pltpu
from jax.sharding import Mesh, PartitionSpec as P

TILE = 128
DP = ("zh", "y", "c")
TEN = ("zl", "x")
F32 = jnp.float32
BF16 = jnp.bfloat16


def lanes(ref, tile_at):
    return ref[:, pl.ds(pl.multiple_of(tile_at * TILE, TILE), TILE)]


def dot(left, right, on):
    return lax.dot_general(left, right, ((on[:1], on[1:]), ((), ())), preferred_element_type=F32)


def slot_list(core, own, far, own_w, far_w):
    slots = own_w[0].shape[0]
    half = slots // 2
    for j in range(slots):
        at = [core * half + j % half, (1 - core) * half + j % half][j // half]
        k = j % half
        yield 1, at, [far[0, n * slots + at] for n in range(3)], [far_w[j // half].at[n, k] for n in range(3)]
    for s in range(slots):
        yield 0, s, [i[0, s] for i in own], [w.at[s] for w in own_w]


def front(
    g_idx, u_idx, d_idx, far, core, xa, gw, uw, dw, ra, rb,
    own_mine, own_theirs, far_mine, far_theirs, dgate, dup, gate, up, dhid, hid,
):
    blocks = xa.shape[1] // TILE // 2
    hidden = gate.shape[0] // 2
    slots = list(slot_list(core[0], (g_idx, u_idx, d_idx), far, (gw, uw, dw), (ra, rb)))
    for acc in (gate, up, dhid):
        acc[...] = jnp.zeros_like(acc)
    for side, _, (gv, uv, dv), (g_t, u_t, d_t) in slots:
        for v, w, acc in ((gv, g_t, gate), (uv, u_t, up)):
            safe = jnp.maximum(v, 0)
            val = dot(lanes(xa, safe >> 2), w[...], (1, 0))
            acc[side * hidden + (safe & 3)] += jnp.where(v >= 0, val, 0.0)
        safe = jnp.maximum(dv, 0)
        val = dot(lanes(xa, blocks + (safe & 31)), d_t[...], (1, 1))
        dhid[side * hidden + (safe >> 5)] += jnp.where(dv >= 0, val, 0.0)
    for b in range(gate.shape[0]):
        g, u, dh = gate[b], up[b], dhid[b]
        sig = jax.nn.sigmoid(g)
        act = g * sig
        hid[b] = (act * u).astype(BF16)
        dgate[b] = (dh * u * sig * (1.0 + g * (1.0 - sig))).astype(BF16)
        dup[b] = (dh * act).astype(BF16)
    first = core[0] == 0
    for side, slot, (gv, uv, dv), _ in slots:
        mine, theirs = ((own_mine, own_theirs), (far_mine, far_theirs))[side]
        outs = []
        for v, grad in ((gv, dgate), (uv, dup)):
            safe = jnp.maximum(v, 0)
            val = dot(lanes(xa, safe >> 2), grad[side * hidden + (safe & 3)], (0, 0))
            outs.append(jnp.where(v >= 0, val, 0.0))
        safe = jnp.maximum(dv, 0)
        val = dot(hid[side * hidden + (safe >> 5)], lanes(xa, blocks + (safe & 31)), (0, 0))
        outs.append(jnp.where(dv >= 0, val, 0.0))
        for k, val in enumerate(outs):
            for half in range(2):
                even = val[64 * half : 64 * half + 32]
                odd = val[64 * half + 32 : 64 * half + 64]
                at = (2 * slot + half, slice(None), slice(k * TILE, (k + 1) * TILE))
                mine[at] = jnp.where(first, even, odd)
                theirs[at] = jnp.where(first, odd, even).astype(BF16)


def back(g_idx, u_idx, far, core, dgate, dup, gw, uw, ra, rb, part, acc):
    hidden = dgate.shape[0] // 2
    acc[...] = jnp.zeros_like(acc)
    for side, _, vs, ws in slot_list(core[0], (g_idx, u_idx, u_idx), far, (gw, uw, uw), (ra, rb)):
        for v, w, grad in zip(vs[:2], ws[:2], (dgate, dup)):
            safe = jnp.maximum(v, 0)
            val = dot(grad[side * hidden + (safe & 3)], w[...], (1, 1))
            acc[safe >> 2] += jnp.where(v >= 0, val, 0.0)
    for b in range(acc.shape[0]):
        part[:, b * TILE : (b + 1) * TILE] = acc[b].astype(BF16)


SMEM = pl.BlockSpec(memory_space=pltpu.SMEM)
VMEM = pl.BlockSpec(memory_space=pltpu.VMEM)
SWAP = [(0, 1), (1, 0)]


def per_device(
    tokens, grad_out, gate_tiles, up_tiles, down_tiles, gate_index, up_index, down_index
):
    here, width = tokens.shape
    line = lax.axis_size("x")
    rows, slots = here * line, gate_tiles.shape[1]
    blocks, hidden = width // TILE, 8
    pairs = lax.axis_size(DP) // 2
    gw, uw, dw = gate_tiles[0], up_tiles[0], down_tiles[0]
    at_core = lax.axis_index("c").astype(jnp.int32)
    core = at_core.reshape(1)
    with jax.named_scope("gather"):
        both = jnp.concatenate([tokens, grad_out], axis=1)
        send = jnp.broadcast_to(both[None], (line, here, 2 * width))
        xa = lax.all_to_all(send, "x", 0, 0, tiled=True).reshape(rows, 2 * width)
    with jax.named_scope("weights"):
        part_of = lambda w: lax.dynamic_slice_in_dim(w, at_core * (slots // 2), slots // 2)
        far = lax.ppermute(
            jnp.concatenate([gate_index, up_index, down_index], axis=1), "zl", SWAP
        )
        ra = lax.ppermute(jnp.stack([part_of(w) for w in (gw, uw, dw)]), "zl", SWAP)
        rb = lax.ppermute(ra, "c", SWAP)
    own_mine, own_theirs, far_mine, far_theirs, dgate, dup = pl.pallas_call(
        front,
        out_shape=(
            jax.ShapeDtypeStruct((pairs, 32, 3 * TILE), F32),
            jax.ShapeDtypeStruct((pairs, 32, 3 * TILE), BF16),
        )
        * 2
        + (jax.ShapeDtypeStruct((hidden, rows, TILE), BF16),) * 2,
        in_specs=[SMEM] * 5 + [VMEM] * 6,
        out_specs=(VMEM,) * 6,
        scratch_shapes=[pltpu.VMEM((hidden, rows, TILE), F32)] * 3
        + [pltpu.VMEM((hidden, rows, TILE), BF16)],
        compiler_params=pltpu.CompilerParams(vmem_limit_bytes=24 << 20),
        cost_estimate=pl.CostEstimate(
            flops=96 * 2 * TILE**3, bytes_accessed=8 << 20, transcendentals=1 << 16
        ),
        name="front",
    )(gate_index, up_index, down_index, far, core, xa, gw, uw, dw, ra, rb)
    with jax.named_scope("cores"):
        far_got = lax.ppermute(far_theirs, "c", SWAP)
        own_got = lax.ppermute(own_theirs, "c", SWAP)
    part = pl.pallas_call(
        back,
        out_shape=jax.ShapeDtypeStruct((rows, width), BF16),
        in_specs=[SMEM] * 4 + [VMEM] * 6,
        out_specs=VMEM,
        scratch_shapes=[pltpu.VMEM((blocks, rows, TILE), F32)],
        compiler_params=pltpu.CompilerParams(vmem_limit_bytes=16 << 20),
        cost_estimate=pl.CostEstimate(
            flops=32 * 2 * TILE**3, bytes_accessed=3 << 20, transcendentals=0
        ),
        name="back",
    )(gate_index, up_index, far, core, dgate, dup, gw, uw, ra, rb)
    with jax.named_scope("layers"):
        near = lax.ppermute((far_mine + far_got.astype(F32)).astype(BF16), "zl", SWAP)
    with jax.named_scope("partials"):
        parts = lax.all_to_all(part.reshape(line, here, width), "x", 0, 0, tiled=True)
        input_sum = jnp.sum(parts.astype(F32), axis=0).astype(BF16)
    with jax.named_scope("tile_sums"):
        quad = (own_mine + own_got.astype(F32) + near.astype(F32)).astype(BF16)
        grads = lax.all_to_all(quad, ("zh", "y"), 0, 0, tiled=True)
        sums = jnp.sum(grads.astype(F32), axis=0)
    return (input_sum, sums[None])


def solution(mesh):
    fine = Mesh(mesh.devices.reshape(4, 8, 2, 2, 8), DP + TEN)
    both = P(DP + TEN, None)
    return jax.shard_map(
        per_device,
        mesh=fine,
        in_specs=(both, both)
        + (P(TEN, None, None, None),) * 3
        + (P(TEN, None),) * 3,
        out_specs=(both, P(TEN, DP, None)),
        check_vma=False,
    )
```

time: 147 us -> 131 us (0.89)
  waiting for transfers between devices: 96.2 us -> 58.3 us
  starting transfers between devices: 38.5 us -> 54.4 us
  other arithmetic: 3.56 us -> 6.62 us
  Pallas kernels: 4.83 us -> 6.86 us
    all_to_all x3, waiting for transfers between devices: 93.7 us -> 31.2 us  [the longest x1 24.9 us: per_device(): grads = lax.all_to_all(quad, ('zh', 'y'), 0, 0, tiled=True)]
    ppermute x1 -> x6, waiting for transfers between devices: 2.46 us -> 27.2 us  [the longest x1 17.2 us: per_device(): ra = lax.ppermute(jnp.stack([part_of(w) for w in (gw, uw, dw)]), 'zl', SWAP)]
    ppermute x1 -> x6, starting transfers between devices: 1.92 us -> 18.7 us  [the longest x1 5.19 us: per_device(): ra = lax.ppermute(jnp.stack([part_of(w) for w in (gw, uw, dw)]), 'zl', SWAP)]
    convert_element_type x1 -> x2, other arithmetic: 1.16 us -> 4.13 us  [the longest x1 3.03 us: per_device(): quad = (own_mine + own_got.astype(F32) + near.astype(F32)).astype(BF16)]
    pallas_call x1, Pallas kernels: 2.24 us -> 3.89 us  [per_device(): pl.pallas_call(front, out_shape=(jax.ShapeDtypeStruct((pairs, 32, 3 * TIL...]
  transfers between devices with their start and end apart: 4 -> 9, of which waited for: 4 -> 5; matrix products, arithmetic and copies ran while one was open for 1% -> 4% of each run, Pallas kernels for 0% -> 2%
where the time goes in v2:
time: 131 us; the launch traced here: 130 us
  waiting for transfers between devices  58.3 us (45%)
  starting transfers between devices  54.4 us (42%)
  Pallas kernels  6.86 us (5%)
  other arithmetic  6.62 us (5%)
  local copies, waits for them, and re-layouts  3.23 us (2%)
    all_to_all x1, waiting for transfers between devices, per_device(): grads = lax.all_to_all(quad, ('zh', 'y'), 0, 0, tiled=True)  24.9 us
    all_to_all x1, starting transfers between devices, per_device(): grads = lax.all_to_all(quad, ('zh', 'y'), 0, 0, tiled=True)  21.9 us
    ppermute x1, waiting for transfers between devices, per_device(): ra = lax.ppermute(jnp.stack([part_of(w) for w in (gw, uw, dw)]), 'zl', SWAP)  17.2 us
    ppermute x1, waiting for transfers between devices, per_device(): lax.ppermute((far_mine + far_got.astype(F32)).astype(BF16), 'zl', SWAP)  8.12 us
    all_to_all x1, starting transfers between devices, per_device(): lax.all_to_all(part.reshape(line, here, width), 'x', 0, 0, tiled=True)  6.92 us
    all_to_all x1, starting transfers between devices, per_device(): xa = lax.all_to_all(send, 'x', 0, 0, tiled=True).reshape(rows, 2 * width)  6.89 us
    all_to_all x1, waiting for transfers between devices, per_device(): lax.all_to_all(part.reshape(line, here, width), 'x', 0, 0, tiled=True)  6.23 us
    ppermute x1, starting transfers between devices, per_device(): ra = lax.ppermute(jnp.stack([part_of(w) for w in (gw, uw, dw)]), 'zl', SWAP)  5.19 us
  transfers between devices with their start and end apart: 9, of which 5 were waited for; matrix products, arithmetic and copies ran while one was open for 4% of the time, Pallas kernels for 2%

profile of v2, /device:TPU:16, one launch (start us, length us, event | category | flops | bytes accessed | tf_op | source)
XLA Modules:
  0.0 130.2 jit_solution(6681557008492971404)
XLA Ops:
  0.6 0.9 pad_maximum_fusion.1
  1.5 1.1 broadcast_in_dim.4
  2.6 6.9 %all-to-all-start = ((bf16[8,8,8192]{2,1,0:T(8,128)(2,1)}), bf16[8,8,8192]{2,1,0:T(8,128)(2,1)S(1)}, u32[]{:S(2)}, u32[]{:S(2)}) async-start(bf16[8,8,8192]{2,1,0:T(8,128)(2,1)} %broadcast_in_dim.4), calls=%async_computation | async-start | bytes 2097152 | tf_op jit(solution)/shard_map/gather/all_to_all | solution.py:109
  9.7 5.2 %collective-permute-start.1 = (bf16[3,8,128,128]{3,2,1,0:T(8,128)(2,1)S(1)}, bf16[3,8,128,128]{3,2,1,0:T(8,128)(2,1)S(1)}, u32[]{:S(2)}, u32[]{:S(2)}) collective-permute-start(bf16[3,8,128,128]{3,2,1,0:T(8,128)(2,1)S(1)} %pad_maximum_fusion), channel_id=1, source_target_pairs={{0,8},{8,0},{1,9},{9,1},{2,10},{10,2},{3,11},{11,3},{4,12},{12,4},... | collective-permute-start | bytes 2359304 | tf_op jit(solution)/shard_map/weights/ppermute | solution.py:115
  14.9 17.2 %collective-permute-done.1.ra = bf16[3,8,128,128]{3,2,1,0:T(8,128)(2,1)S(1)} collective-permute-done((bf16[3,8,128,128]{3,2,1,0:T(8,128)(2,1)S(1)}, bf16[3,8,128,128]{3,2,1,0:T(8,128)(2,1)S(1)}, u32[]{:S(2)}, u32[]{:S(2)}) %collective-permute-start.1) | collective-permute-done | bytes 786464 | tf_op jit(solution)/shard_map/weights/ppermute | solution.py:115
  32.2 1.9 %collective-permute-start.2 = (bf16[3,8,128,128]{3,2,1,0:T(8,128)(2,1)S(1)}, bf16[3,8,128,128]{3,2,1,0:T(8,128)(2,1)S(1)}, u32[]{:S(2)}, u32[]{:S(2)}) collective-permute-start(bf16[3,8,128,128]{3,2,1,0:T(8,128)(2,1)S(1)} %collective-permute-done.1.ra), channel_id=1, source_target_pairs={{0,16},{16,0},{1,17},{17,1},{2,18},{18,2},{3,19},{19,3},{4,20},{20... | collective-permute-start | bytes 2359304 | tf_op jit(solution)/shard_map/weights/ppermute | solution.py:116
  34.2 3.6 %collective-permute-start = (s32[1,48]{1,0:T(1,128)S(1)}, s32[1,48]{1,0:T(1,128)S(1)}, u32[]{:S(2)}, u32[]{:S(2)}) collective-permute-start(s32[1,48]{1,0:T(1,128)S(1)} %pad_add_fusion), channel_id=1, source_target_pairs={{0,8},{8,0},{1,9},{9,1},{2,10},{10,2},{3,11},{11,3},{4,12},{12,4},... | collective-permute-start | bytes 584 | tf_op jit(solution)/shard_map/weights/ppermute | solution.py:112
  37.8 1.8 %collective-permute-done.far = s32[1,48]{1,0:T(1,128)S(1)} collective-permute-done((s32[1,48]{1,0:T(1,128)S(1)}, s32[1,48]{1,0:T(1,128)S(1)}, u32[]{:S(2)}, u32[]{:S(2)}) %collective-permute-start) | collective-permute-done | bytes 224 | tf_op jit(solution)/shard_map/weights/ppermute | solution.py:112
  39.6 0.9 copy-done.2
  40.6 1.1 copy-done.3
  41.7 3.9 %front.1 = (f32[32,32,384]{2,1,0:T(8,128)S(1)}, bf16[32,32,384]{2,1,0:T(8,128)(2,1)}, f32[32,32,384]{2,1,0:T(8,128)S(1)}, bf16[32,32,384]{2,1,0:T(8,128)(2,1)S(1...) custom-call(s32[1,16]{1,0:T(1,128)S(1)} %copy-done.6, s32[1,16]{1,0:T(1,128)S(1)} %copy-done.7, ...), custom_call_target="tpu_custom_call" | custom-call | flops 402653184 | bytes 8388608 | tf_op jit(solution)/shard_map/front/pallas_call | solution.py:117
  45.6 1.9 %collective-permute-start.4 = (bf16[32,32,384]{2,1,0:T(8,128)(2,1)S(1)}, bf16[32,32,384]{2,1,0:T(8,128)(2,1)S(1)}, u32[]{:S(2)}, u32[]{:S(2)}) collective-permute-start(bf16[32,32,384]{2,1,0:T(8,128)(2,1)S(1)} %get-tuple-element.13), channel_id=1, source_target_pairs={{0,16},{16,0},{1,17},{17,1},{2,18},{18,2},{3,19},{19,3},{4,20},{20... | collective-permute-start | bytes 2359304 | tf_op jit(solution)/shard_map/cores/ppermute | solution.py:136
  47.5 2.4 %collective-permute-start.3 = (bf16[32,32,384]{2,1,0:T(8,128)(2,1)}, bf16[32,32,384]{2,1,0:T(8,128)(2,1)}, u32[]{:S(2)}, u32[]{:S(2)}) collective-permute-start(bf16[32,32,384]{2,1,0:T(8,128)(2,1)} %get-tuple-element.11), channel_id=1, source_target_pairs={{0,16},{16,0},{1,17},{17,1},{2,18},{18,2},{3,19},{19,3},{4,20},{20... | collective-permute-start | bytes 2359304 | tf_op jit(solution)/shard_map/cores/ppermute | solution.py:137
  49.9 1.1 add_convert_fusion.1
  51.0 3.6 %collective-permute-start.5 = (bf16[32,32,384]{2,1,0:T(8,128)(2,1)}, bf16[32,32,384]{2,1,0:T(8,128)(2,1)}, u32[]{:S(2)}, u32[]{:S(2)}) collective-permute-start(bf16[32,32,384]{2,1,0:T(8,128)(2,1)} %add_convert_fusion.1), channel_id=1, source_target_pairs={{0,8},{8,0},{1,9},{9,1},{2,10},{10,2},{3,11},{11,3},{4,12},{12,4},... | collective-permute-start | bytes 2359304 | tf_op jit(solution)/shard_map/layers/ppermute | solution.py:151
  54.7 3.0 %back.1 = bf16[64,4096]{1,0:T(8,128)(2,1)} custom-call(s32[1,16]{1,0:T(1,128)S(1)} %copy-done.6, s32[1,16]{1,0:T(1,128)S(1)} %copy-done.7, s32[1,48]{1,0:T(1,128)S(1)} %collective-permute-done.far, s32[1]{0:T(128)} %bitcast.core, bf16[8,64,128]{2,1,0:T(8,128)(2,1)S(1)} %get-tuple-element.8.dgate, bf16[8,64,128]{2,1,0:T(8,128)(2,1)S(1)} %get-tuple-element.9.dup, ...), custom_call_target="tpu_custom_call" | custom-call | flops 134217728 | bytes 3145728 | tf_op jit(solution)/shard_map/back/pallas_call | solution.py:138
  57.6 6.9 %all-to-all-start.1 = ((bf16[8,8,4096]{2,1,0:T(8,128)(2,1)}), bf16[8,8,4096]{2,1,0:T(8,128)(2,1)S(1)}, u32[]{:S(2)}, u32[]{:S(2)}) async-start(bf16[8,8,4096]{2,1,0:T(8,128)(2,1)} %bitcast.5), calls=%async_computation.1 | async-start | bytes 1048576 | tf_op jit(solution)/shard_map/partials/all_to_all | solution.py:153
  64.6 8.1 %collective-permute-done.5 = bf16[32,32,384]{2,1,0:T(8,128)(2,1)} collective-permute-done((bf16[32,32,384]{2,1,0:T(8,128)(2,1)}, bf16[32,32,384]{2,1,0:T(8,128)(2,1)}, u32[]{:S(2)}, u32[]{:S(2)}) %collective-permute-start.5) | collective-permute-done | bytes 786464 | tf_op jit(solution)/shard_map/layers/ppermute | solution.py:151
  72.7 3.0 %add_convert_fusion = bf16[32,32,384]{2,1,0:T(8,128)(2,1)} fusion(bf16[32,32,384]{2,1,0:T(8,128)(2,1)} %collective-permute-done.5, f32[32,32,384]{2,1,0:T(8,128)} %copy-done.4, bf16[32,32,384]{2,1,0:T(8,128)(2,1)} %collective-permute-done.3), kind=kLoop, calls=%fused_computation.1 | loop fusion | flops 1966080 | bytes 3932160 | tf_op jit(solution)/shard_map/tile_sums/convert_element_type | solution.py:156
  75.7 6.2 %all-to-all-done.1 = bf16[8,8,4096]{2,1,0:T(8,128)(2,1)S(1)} async-done(((bf16[8,8,4096]{2,1,0:T(8,128)(2,1)}), bf16[8,8,4096]{2,1,0:T(8,128)(2,1)S(1)}, u32[]{:S(2)}, u32[]{:S(2)}) %all-to-all-start.1) | async-done | bytes 524320 | tf_op jit(solution)/shard_map/partials/all_to_all | solution.py:153
  81.9 21.9 %all-to-all-start.2 = ((bf16[32,32,384]{2,1,0:T(8,128)(2,1)}), bf16[32,32,384]{2,1,0:T(8,128)(2,1)S(1)}, u32[]{:S(2)}, u32[]{:S(2)}) async-start(bf16[32,32,384]{2,1,0:T(8,128)(2,1)} %add_convert_fusion), calls=%async_computation.2 | async-start | bytes 1572864 | tf_op jit(solution)/shard_map/tile_sums/all_to_all | solution.py:157
  103.8 0.7 reduce_sum.21
  104.5 24.9 %all-to-all-done.2 = bf16[32,32,384]{2,1,0:T(8,128)(2,1)S(1)} async-done(((bf16[32,32,384]{2,1,0:T(8,128)(2,1)}), bf16[32,32,384]{2,1,0:T(8,128)(2,1)S(1)}, u32[]{:S(2)}, u32[]{:S(2)}) %all-to-all-start.2) | async-done | bytes 786464 | tf_op jit(solution)/shard_map/tile_sums/all_to_all | solution.py:157
  129.5 0.7 convert_reduce_fusion
  (24 shorter events, 0.3 us)
Async XLA Ops:
  1.5 8.0 %copy-start = (bf16[1,16,128,128]{3,2,1,0:T(8,128)(2,1)S(1)}, bf16[1,16,128,128]{3,2,1,0:T(8,128)(2,1)}, u32[]{:S(2)}) copy-start(bf16[1,16,128,128]{3,2,1,0:T(8,128)(2,1)} %param.10) | copy-start | bytes 1572868
  2.6 7.0 %copy-start.1 = (bf16[1,16,128,128]{3,2,1,0:T(8,128)(2,1)S(1)}, bf16[1,16,128,128]{3,2,1,0:T(8,128)(2,1)}, u32[]{:S(2)}) copy-start(bf16[1,16,128,128]{3,2,1,0:T(8,128)(2,1)} %param.11) | copy-start | bytes 1572868
  2.6 7.0 %copy-start.5 = (bf16[1,16,128,128]{3,2,1,0:T(8,128)(2,1)S(1)}, bf16[1,16,128,128]{3,2,1,0:T(8,128)(2,1)}, u32[]{:S(2)}) copy-start(bf16[1,16,128,128]{3,2,1,0:T(8,128)(2,1)} %param.12) | copy-start | bytes 1572868
  2.6 38.0 %all-to-all-start = ((bf16[8,8,8192]{2,1,0:T(8,128)(2,1)}), bf16[8,8,8192]{2,1,0:T(8,128)(2,1)S(1)}, u32[]{:S(2)}, u32[]{:S(2)}) async-start(bf16[8,8,8192]{2,1,0:T(8,128)(2,1)} %broadcast_in_dim.4), calls=%async_computation | async-start | bytes 2097152 | tf_op jit(solution)/shard_map/gather/all_to_all | solution.py:109
  9.5 24.6 %copy-start.6 = (s32[1,16]{1,0:T(1,128)S(1)}, s32[1,16]{1,0:T(1,128)}, u32[]{:S(2)}) copy-start(s32[1,16]{1,0:T(1,128)} %g_idx.3) | copy-start | bytes 196
  9.5 24.6 %copy-start.7 = (s32[1,16]{1,0:T(1,128)S(1)}, s32[1,16]{1,0:T(1,128)}, u32[]{:S(2)}) copy-start(s32[1,16]{1,0:T(1,128)} %u_idx.3) | copy-start | bytes 196
  9.5 24.6 %copy-start.8 = (s32[1,16]{1,0:T(1,128)S(1)}, s32[1,16]{1,0:T(1,128)}, u32[]{:S(2)}) copy-start(s32[1,16]{1,0:T(1,128)} %d_idx.1) | copy-start | bytes 196
  9.7 22.4 %collective-permute-start.1 = (bf16[3,8,128,128]{3,2,1,0:T(8,128)(2,1)S(1)}, bf16[3,8,128,128]{3,2,1,0:T(8,128)(2,1)S(1)}, u32[]{:S(2)}, u32[]{:S(2)}) collective-permute-start(bf16[3,8,128,128]{3,2,1,0:T(8,128)(2,1)S(1)} %pad_maximum_fusion), channel_id=1, source_target_pairs={{0,8},{8,0},{1,9},{9,1},{2,10},{10,2},{3,11},{11,3},{4,12},{12,4},... | collective-permute-start | bytes 2359304 | tf_op jit(solution)/shard_map/weights/ppermute | solution.py:115
  32.2 7.5 %collective-permute-start.2 = (bf16[3,8,128,128]{3,2,1,0:T(8,128)(2,1)S(1)}, bf16[3,8,128,128]{3,2,1,0:T(8,128)(2,1)S(1)}, u32[]{:S(2)}, u32[]{:S(2)}) collective-permute-start(bf16[3,8,128,128]{3,2,1,0:T(8,128)(2,1)S(1)} %collective-permute-done.1.ra), channel_id=1, source_target_pairs={{0,16},{16,0},{1,17},{17,1},{2,18},{18,2},{3,19},{19,3},{4,20},{20... | collective-permute-start | bytes 2359304 | tf_op jit(solution)/shard_map/weights/ppermute | solution.py:116
  34.2 5.4 %collective-permute-start = (s32[1,48]{1,0:T(1,128)S(1)}, s32[1,48]{1,0:T(1,128)S(1)}, u32[]{:S(2)}, u32[]{:S(2)}) collective-permute-start(s32[1,48]{1,0:T(1,128)S(1)} %pad_add_fusion), channel_id=1, source_target_pairs={{0,8},{8,0},{1,9},{9,1},{2,10},{10,2},{3,11},{11,3},{4,12},{12,4},... | collective-permute-start | bytes 584 | tf_op jit(solution)/shard_map/weights/ppermute | solution.py:112
  39.6 0.9 copy-start.2
  40.6 1.1 copy-start.3
  45.6 5.4 %copy-start.4 = (f32[32,32,384]{2,1,0:T(8,128)}, f32[32,32,384]{2,1,0:T(8,128)S(1)}, u32[]{:S(2)}) copy-start(f32[32,32,384]{2,1,0:T(8,128)S(1)} %get-tuple-element.10) | copy-start | bytes 4718596
  45.6 4.3 %collective-permute-start.4 = (bf16[32,32,384]{2,1,0:T(8,128)(2,1)S(1)}, bf16[32,32,384]{2,1,0:T(8,128)(2,1)S(1)}, u32[]{:S(2)}, u32[]{:S(2)}) collective-permute-start(bf16[32,32,384]{2,1,0:T(8,128)(2,1)S(1)} %get-tuple-element.13), channel_id=1, source_target_pairs={{0,16},{16,0},{1,17},{17,1},{2,18},{18,2},{3,19},{19,3},{4,20},{20... | collective-permute-start | bytes 2359304 | tf_op jit(solution)/shard_map/cores/ppermute | solution.py:136
  47.5 17.1 %collective-permute-start.3 = (bf16[32,32,384]{2,1,0:T(8,128)(2,1)}, bf16[32,32,384]{2,1,0:T(8,128)(2,1)}, u32[]{:S(2)}, u32[]{:S(2)}) collective-permute-start(bf16[32,32,384]{2,1,0:T(8,128)(2,1)} %get-tuple-element.11), channel_id=1, source_target_pairs={{0,16},{16,0},{1,17},{17,1},{2,18},{18,2},{3,19},{19,3},{4,20},{20... | collective-permute-start | bytes 2359304 | tf_op jit(solution)/shard_map/cores/ppermute | solution.py:137
  51.0 21.7 %collective-permute-start.5 = (bf16[32,32,384]{2,1,0:T(8,128)(2,1)}, bf16[32,32,384]{2,1,0:T(8,128)(2,1)}, u32[]{:S(2)}, u32[]{:S(2)}) collective-permute-start(bf16[32,32,384]{2,1,0:T(8,128)(2,1)} %add_convert_fusion.1), channel_id=1, source_target_pairs={{0,8},{8,0},{1,9},{9,1},{2,10},{10,2},{3,11},{11,3},{4,12},{12,4},... | collective-permute-start | bytes 2359304 | tf_op jit(solution)/shard_map/layers/ppermute | solution.py:151
  57.6 24.3 %all-to-all-start.1 = ((bf16[8,8,4096]{2,1,0:T(8,128)(2,1)}), bf16[8,8,4096]{2,1,0:T(8,128)(2,1)S(1)}, u32[]{:S(2)}, u32[]{:S(2)}) async-start(bf16[8,8,4096]{2,1,0:T(8,128)(2,1)} %bitcast.5), calls=%async_computation.1 | async-start | bytes 1048576 | tf_op jit(solution)/shard_map/partials/all_to_all | solution.py:153
  81.9 47.5 %all-to-all-start.2 = ((bf16[32,32,384]{2,1,0:T(8,128)(2,1)}), bf16[32,32,384]{2,1,0:T(8,128)(2,1)S(1)}, u32[]{:S(2)}, u32[]{:S(2)}) async-start(bf16[32,32,384]{2,1,0:T(8,128)(2,1)} %add_convert_fusion), calls=%async_computation.2 | async-start | bytes 1572864 | tf_op jit(solution)/shard_map/tile_sums/all_to_all | solution.py:157

commit v3 on v2

v3 whole, which is shorter than its diff:
```python
import jax
import jax.numpy as jnp
from jax import lax
from jax.experimental import pallas as pl
from jax.experimental.pallas import tpu as pltpu
from jax.sharding import Mesh, PartitionSpec as P

TILE = 128
DP = ("zh", "y", "c")
TEN = ("zl", "x")
F32 = jnp.float32
BF16 = jnp.bfloat16


def lanes(ref, tile_at):
    return ref[:, pl.ds(pl.multiple_of(tile_at * TILE, TILE), TILE)]


def dot(left, right, on):
    return lax.dot_general(left, right, ((on[:1], on[1:]), ((), ())), preferred_element_type=F32)


def fetch(halves, held, sems):
    copies = [pltpu.make_async_copy(r, held.at[h], sems.at[h]) for h, r in enumerate(halves)]
    for copy in copies:
        copy.start()
    return copies


def slot_list(core, own, far, own_w, held, copies):
    slots = own_w[0].shape[0]
    half = slots // 2
    for s in range(slots):
        yield 0, [i[0, s] for i in own], [w.at[s] for w in own_w]
    for j in range(slots):
        h, k = divmod(j, half)
        if k == 0:
            copies[h].wait()
        at = (core if h == 0 else 1 - core) * half + k
        yield 1, [far[0, n * slots + at] for n in range(3)], [held.at[h, n, k] for n in range(3)]


def forward(
    g_idx, u_idx, d_idx, far, core, xa, gw, uw, dw, ra, rb, dgate, dup, hid, held, sems, gate, up, dhid
):
    copies = fetch((ra, rb), held, sems)
    blocks = xa.shape[1] // TILE // 2
    hidden = gate.shape[0] // 2
    for acc in (gate, up, dhid):
        acc[...] = jnp.zeros_like(acc)
    slots = slot_list(core[0], (g_idx, u_idx, d_idx), far, (gw, uw, dw), held, copies)
    for side, (gv, uv, dv), (g_t, u_t, d_t) in slots:
        for v, w, acc in ((gv, g_t, gate), (uv, u_t, up)):
            safe = jnp.maximum(v, 0)
            val = dot(lanes(xa, safe >> 2), w[...], (1, 0))
            acc[side * hidden + (safe & 3)] += jnp.where(v >= 0, val, 0.0)
        safe = jnp.maximum(dv, 0)
        val = dot(lanes(xa, blocks + (safe & 31)), d_t[...], (1, 1))
        dhid[side * hidden + (safe >> 5)] += jnp.where(dv >= 0, val, 0.0)
    for b in range(gate.shape[0]):
        g, u, dh = gate[b], up[b], dhid[b]
        sig = jax.nn.sigmoid(g)
        act = g * sig
        hid[b] = (act * u).astype(BF16)
        dgate[b] = (dh * u * sig * (1.0 + g * (1.0 - sig))).astype(BF16)
        dup[b] = (dh * act).astype(BF16)


def back(g_idx, u_idx, far, core, dgate, dup, gw, uw, ra, rb, part, held, sems, acc):
    copies = fetch((ra, rb), held, sems)
    hidden = dgate.shape[0] // 2
    acc[...] = jnp.zeros_like(acc)
    slots = slot_list(core[0], (g_idx, u_idx, u_idx), far, (gw, uw, uw), held, copies)
    for side, vs, ws in slots:
        for v, w, grad in zip(vs[:2], ws[:2], (dgate, dup)):
            safe = jnp.maximum(v, 0)
            val = dot(grad[side * hidden + (safe & 3)], w[...], (1, 1))
            acc[safe >> 2] += jnp.where(v >= 0, val, 0.0)
    for b in range(acc.shape[0]):
        part[:, b * TILE : (b + 1) * TILE] = acc[b]


def tile_terms(
    g_idx, u_idx, d_idx, far, core, xa, dgate, dup, hid, own_mine, own_theirs, far_mine, far_theirs
):
    blocks = xa.shape[1] // TILE // 2
    hidden = dgate.shape[0] // 2
    first = core[0] == 0
    sets = (
        (1, lambda n, s: far[0, n * CAP + s], far_mine, far_theirs),
        (0, lambda n, s: (g_idx, u_idx, d_idx)[n][0, s], own_mine, own_theirs),
    )
    for side, index, mine, theirs in sets:
        for slot in range(CAP):
            outs = []
            for n, grad in ((0, dgate), (1, dup)):
                v = index(n, slot)
                safe = jnp.maximum(v, 0)
                val = dot(lanes(xa, safe >> 2), grad[side * hidden + (safe & 3)], (0, 0))
                outs.append(jnp.where(v >= 0, val, 0.0))
            v = index(2, slot)
            safe = jnp.maximum(v, 0)
            val = dot(hid[side * hidden + (safe >> 5)], lanes(xa, blocks + (safe & 31)), (0, 0))
            outs.append(jnp.where(v >= 0, val, 0.0))
            for k, val in enumerate(outs):
                for half in range(2):
                    even = val[64 * half : 64 * half + 32]
                    odd = val[64 * half + 32 : 64 * half + 64]
                    at = (2 * slot + half, slice(None), slice(k * TILE, (k + 1) * TILE))
                    mine[at] = jnp.where(first, even, odd).astype(BF16)
                    theirs[at] = jnp.where(first, odd, even).astype(BF16)


def beside():
    pairs = []
    for zh in range(4):
        for c in range(2):
            for zl in range(2):
                to = (zh if c == 0 else (zh + (1 if zl else -1)) % 4, c, 1 - zl)
                pairs.append(((zh * 2 + c) * 2 + zl, (to[0] * 2 + to[1]) * 2 + to[2]))
    return pairs


CAP = 16

SMEM = pl.BlockSpec(memory_space=pltpu.SMEM)
VMEM = pl.BlockSpec(memory_space=pltpu.VMEM)
HBM = pl.BlockSpec(memory_space=pltpu.HBM)
SWAP = [(0, 1), (1, 0)]
LAYERS = ("zh", "c", "zl")


def call(kernel, flops, out_shape, scalars, arrays, halves=(), scratch=(), mib=16):
    if halves:
        held = pltpu.VMEM((len(halves), *halves[0].shape), BF16)
        scratch = (held, pltpu.SemaphoreType.DMA((len(halves),)), *scratch)
    return pl.pallas_call(
        kernel,
        out_shape=out_shape,
        in_specs=[SMEM] * len(scalars) + [VMEM] * len(arrays) + [HBM] * len(halves),
        out_specs=(VMEM,) * len(out_shape),
        scratch_shapes=list(scratch),
        compiler_params=pltpu.CompilerParams(vmem_limit_bytes=mib << 20),
        cost_estimate=pl.CostEstimate(flops=flops, bytes_accessed=6 << 20, transcendentals=0),
        name=kernel.__name__,
    )(*scalars, *arrays, *halves)


def per_device(
    tokens, grad_out, gate_tiles, up_tiles, down_tiles, gate_index, up_index, down_index
):
    here, width = tokens.shape
    line = lax.axis_size("x")
    rows, slots = here * line, gate_tiles.shape[1]
    blocks, hidden = width // TILE, 8
    pairs = lax.axis_size(DP) // 2
    gw, uw, dw = gate_tiles[0], up_tiles[0], down_tiles[0]
    at_core = lax.axis_index("c").astype(jnp.int32)
    core = at_core.reshape(1)
    with jax.named_scope("gather"):
        both = jnp.concatenate([tokens, grad_out], axis=1)
        send = jnp.broadcast_to(both[None], (line, here, 2 * width))
        xa = lax.all_to_all(send, "x", 0, 0, tiled=True).reshape(rows, 2 * width)
    with jax.named_scope("weights"):
        part_of = lambda w: lax.dynamic_slice_in_dim(w, at_core * (slots // 2), slots // 2)
        stack = jnp.stack([part_of(w) for w in (gw, uw, dw)])
        index = jnp.concatenate([gate_index, up_index, down_index], axis=1)
        stack, index = lax.optimization_barrier((stack, index))
        far = lax.ppermute(index, "zl", SWAP)
        ra = lax.ppermute(stack, LAYERS, beside())
        ra, far = lax.optimization_barrier((ra, far))
        rb = lax.ppermute(ra, "c", SWAP)
    own = (gate_index, up_index, down_index)
    work = 2 * rows * TILE * TILE * 2 * slots
    shape = lambda *dims: jax.ShapeDtypeStruct(dims, BF16)
    dgate, dup, hid = call(
        forward,
        3 * work,
        (shape(hidden, rows, TILE),) * 3,
        (*own, far, core),
        (xa, gw, uw, dw),
        (ra, rb),
        [pltpu.VMEM((hidden, rows, TILE), F32)] * 3,
    )
    (part,) = call(
        back,
        2 * work,
        (jax.ShapeDtypeStruct((rows, width), F32),),
        (*own[:2], far, core),
        (dgate, dup, gw, uw),
        (ra, rb),
        [pltpu.VMEM((blocks, rows, TILE), F32)],
    )
    own_mine, own_theirs, far_mine, far_theirs = call(
        tile_terms,
        3 * work,
        (shape(pairs, 32, 3 * TILE),) * 4,
        (*own, far, core),
        (xa, dgate, dup, hid),
    )
    own_mine, _ = lax.optimization_barrier((own_mine, part))
    with jax.named_scope("partials"):
        input_sum = lax.psum_scatter(part, "x", scatter_dimension=0, tiled=True).astype(BF16)
    add = lambda *terms: sum(t.astype(F32) for t in terms).astype(BF16)
    with jax.named_scope("cores"):
        far_got = lax.ppermute(far_theirs, "c", SWAP)
        own_got = lax.ppermute(own_theirs, "c", SWAP)
    with jax.named_scope("layers"):
        near = lax.ppermute(add(far_mine, far_got), LAYERS, beside())
    with jax.named_scope("tile_sums"):
        grads = lax.all_to_all(add(own_mine, own_got, near), ("zh", "y"), 0, 0, tiled=True)
        sums = jnp.sum(grads.astype(F32), axis=0)
    return (input_sum, sums[None])


def solution(mesh):
    fine = Mesh(mesh.devices.reshape(4, 8, 2, 2, 8), DP + TEN)
    both = P(DP + TEN, None)
    return jax.shard_map(
        per_device,
        mesh=fine,
        in_specs=(both, both)
        + (P(TEN, None, None, None),) * 3
        + (P(TEN, None),) * 3,
        out_specs=(both, P(TEN, DP, None)),
        check_vma=False,
    )
```

time: 131 us -> 128 us (0.977)
  waiting for transfers between devices: 58.3 us -> 41.1 us
  between operations: 0.81 us -> 14.2 us
  Pallas kernels: 6.86 us -> 8.37 us
    all_to_all x2 -> x1, waiting for transfers between devices: 31.2 us -> 5.16 us  [per_device(): lax.all_to_all(add(own_mine, own_got, near), ('zh', 'y'), 0, 0, tiled=True)]
    reduce_scatter x0 -> x1, waiting for transfers between devices: none -> 18 us  [per_device(): lax.psum_scatter(part, 'x', scatter_dimension=0, tiled=True).astype(BF16)]
    ppermute x3, waiting for transfers between devices: 27.1 us -> 16.1 us  [the longest x1 8.09 us: per_device(): far = lax.ppermute(index, 'zl', SWAP)]
    ppermute x1, starting transfers between devices: 1.91 us -> 12.9 us  [per_device(): rb = lax.ppermute(ra, 'c', SWAP)]
    all_to_all x2 -> x1, starting transfers between devices: 28.8 us -> 19.8 us  [per_device(): lax.all_to_all(add(own_mine, own_got, near), ('zh', 'y'), 0, 0, tiled=True)]
    ppermute x3, starting transfers between devices: 12.5 us -> 9.75 us  [the longest x1 5.19 us: per_device(): ra = lax.ppermute(stack, LAYERS, beside())]
    ppermute x1, waiting for transfers between devices: 0.01 us -> 1.89 us  [per_device(): rb = lax.ppermute(ra, 'c', SWAP)]
    pallas_call x2 -> x3, Pallas kernels: 6.86 us -> 8.37 us  [call(): pl.pallas_call(kernel, out_shape=out_shape, in_specs=[SMEM] * len(scalars...]
  transfers between devices with their start and end apart: 9 -> 9, of which waited for: 5 -> 5; matrix products, arithmetic and copies ran while one was open for 4% -> 4% of each run, Pallas kernels for 2% -> 3%
where the time goes in v3:
time: 128 us; the launch traced here: 127 us
  starting transfers between devices  53.7 us (42%)
  waiting for transfers between devices  41.1 us (32%)
  between operations  14.2 us (11%)
  Pallas kernels  8.37 us (7%)
  other arithmetic  6.75 us (5%)
  local copies, waits for them, and re-layouts  3.18 us (2%)
    all_to_all x1, starting transfers between devices, per_device(): lax.all_to_all(add(own_mine, own_got, near), ('zh', 'y'), 0, 0, tiled=True)  19.8 us
    reduce_scatter x1, waiting for transfers between devices, per_device(): lax.psum_scatter(part, 'x', scatter_dimension=0, tiled=True).astype(BF16)  18 us
    ppermute x1, starting transfers between devices, per_device(): rb = lax.ppermute(ra, 'c', SWAP)  12.9 us
    pallas_call x3, Pallas kernels, call(): pl.pallas_call(kernel, out_shape=out_shape, in_specs=[SMEM] * len(scalars...  8.37 us
    ppermute x1, waiting for transfers between devices, per_device(): far = lax.ppermute(index, 'zl', SWAP)  8.09 us
    ppermute x1, waiting for transfers between devices, per_device(): near = lax.ppermute(add(far_mine, far_got), LAYERS, beside())  7.98 us
    all_to_all x1, starting transfers between devices, per_device(): xa = lax.all_to_all(send, 'x', 0, 0, tiled=True).reshape(rows, 2 * width)  6.9 us
    ppermute x1, starting transfers between devices, per_device(): ra = lax.ppermute(stack, LAYERS, beside())  5.19 us
  transfers between devices with their start and end apart: 9, of which 5 were waited for; matrix products, arithmetic and copies ran while one was open for 4% of the time, Pallas kernels for 3%

profile of v3, /device:TPU:16, one launch (start us, length us, event | category | flops | bytes accessed | tf_op | source)
XLA Modules:
  0.0 127.4 jit_solution(14435894698976669898)
XLA Ops:
  7.2 0.9 pad_maximum_fusion.1
  8.0 1.1 broadcast_in_dim.4
  9.1 6.9 %all-to-all-start = ((bf16[8,8,8192]{2,1,0:T(8,128)(2,1)}), bf16[8,8,8192]{2,1,0:T(8,128)(2,1)S(1)}, u32[]{:S(2)}, u32[]{:S(2)}) async-start(bf16[8,8,8192]{2,1,0:T(8,128)(2,1)} %broadcast_in_dim.4), calls=%async_computation | async-start | bytes 2097152 | tf_op jit(solution)/shard_map/gather/all_to_all | solution.py:163
  16.4 5.2 %collective-permute-start = (bf16[3,8,128,128]{3,2,1,0:T(8,128)(2,1)S(1)}, bf16[3,8,128,128]{3,2,1,0:T(8,128)(2,1)S(1)}, u32[]{:S(2)}, u32[]{:S(2)}) collective-permute-start(bf16[3,8,128,128]{3,2,1,0:T(8,128)(2,1)S(1)} %pad_maximum_fusion), channel_id=1, source_target_pairs={{0,8},{8,0},{16,792},{24,272},{256,264},{264,256},{272,24},{280,52... | collective-permute-start | bytes 2359304 | tf_op jit(solution)/shard_map/weights/ppermute | solution.py:170
  21.6 1.9 %collective-permute-start.1 = (s32[1,48]{1,0:T(1,128)S(1)}, s32[1,48]{1,0:T(1,128)S(1)}, u32[]{:S(2)}, u32[]{:S(2)}) collective-permute-start(s32[1,48]{1,0:T(1,128)S(1)} %pad_add_fusion), channel_id=1, source_target_pairs={{0,8},{8,0},{1,9},{9,1},{2,10},{10,2},{3,11},{11,3},{4,12},{12,4},... | collective-permute-start | bytes 584 | tf_op jit(solution)/shard_map/weights/ppermute | solution.py:169
  23.5 8.1 %collective-permute-done.1.far = s32[1,48]{1,0:T(1,128)S(1)} collective-permute-done((s32[1,48]{1,0:T(1,128)S(1)}, s32[1,48]{1,0:T(1,128)S(1)}, u32[]{:S(2)}, u32[]{:S(2)}) %collective-permute-start.1) | collective-permute-done | bytes 224 | tf_op jit(solution)/shard_map/weights/ppermute | solution.py:169
  31.6 12.9 %collective-permute-start.2 = (bf16[3,8,128,128]{3,2,1,0:T(8,128)(2,1)S(1)}, bf16[3,8,128,128]{3,2,1,0:T(8,128)(2,1)S(1)}, u32[]{:S(2)}, u32[]{:S(2)}) collective-permute-start(bf16[3,8,128,128]{3,2,1,0:T(8,128)(2,1)S(1)} %collective-permute-done.ra), channel_id=1, source_target_pairs={{0,16},{16,0},{1,17},{17,1},{2,18},{18,2},{3,19},{19,3},{4,20},{20... | collective-permute-start | bytes 2359304 | tf_op jit(solution)/shard_map/weights/ppermute | solution.py:172
  44.6 1.9 %collective-permute-done.2.rb = bf16[3,8,128,128]{3,2,1,0:T(8,128)(2,1)S(1)} collective-permute-done((bf16[3,8,128,128]{3,2,1,0:T(8,128)(2,1)S(1)}, bf16[3,8,128,128]{3,2,1,0:T(8,128)(2,1)S(1)}, u32[]{:S(2)}, u32[]{:S(2)}) %collective-permute-start.2) | collective-permute-done | bytes 786464 | tf_op jit(solution)/shard_map/weights/ppermute | solution.py:172
  46.4 0.9 copy-done.2
  47.3 1.1 copy-done.3
  48.5 2.3 %forward.1 = (bf16[8,64,128]{2,1,0:T(8,128)(2,1)S(1)}, bf16[8,64,128]{2,1,0:T(8,128)(2,1)S(1)}, bf16[8,64,128]{2,1,0:T(8,128)(2,1)S(1)}) custom-call(s32[1,16]{1,0:T(1,128)S(1)} %copy-done.8, s32[1,16]{1,0:T(1,128)S(1)} %copy-done.9, s32[1,16]{1,0:T(1,128)S(1)} %copy-done.10, s32[1,48]{1,0:T(1,128)S(1)} %collective-permute-done.1.far, s32[1]{0:T(128)} %bitcast.core, ...), custom_call_target="tpu_custom_call" | custom-call | flops 201326592 | bytes 6291456 | tf_op jit(solution)/shard_map/forward/pallas_call | solution.py:137
  50.8 2.6 %tile_terms.1 = (bf16[32,32,384]{2,1,0:T(8,128)(2,1)S(1)}, bf16[32,32,384]{2,1,0:T(8,128)(2,1)}, bf16[32,32,384]{2,1,0:T(8,128)(2,1)S(1)}, bf16[32,32,384]{2,1,0:T(8,128)(2,1)S(1)}) custom-call(s32[1,16]{1,0:T(1,128)S(1)} %copy-done.8, s32[1,16]{1,0:T(1,128)S(1)} %copy-done.9, s32[1,16]{1,0:T(1,128)S(1)} %copy-done.10, ...), custom_call_target="tpu_custom_call" | custom-call | flops 201326592 | bytes 6291456 | tf_op jit(solution)/shard_map/tile_terms/pallas_call | solution.py:137
  53.3 2.3 %collective-permute-start.4 = (bf16[32,32,384]{2,1,0:T(8,128)(2,1)S(1)}, bf16[32,32,384]{2,1,0:T(8,128)(2,1)S(1)}, u32[]{:S(2)}, u32[]{:S(2)}) collective-permute-start(bf16[32,32,384]{2,1,0:T(8,128)(2,1)S(1)} %get-tuple-element.25), channel_id=1, source_target_pairs={{0,16},{16,0},{1,17},{17,1},{2,18},{18,2},{3,19},{19,3},{4,20},{20... | collective-permute-start | bytes 2359304 | tf_op jit(solution)/shard_map/cores/ppermute | solution.py:206
  55.6 2.0 %collective-permute-start.3 = (bf16[32,32,384]{2,1,0:T(8,128)(2,1)}, bf16[32,32,384]{2,1,0:T(8,128)(2,1)S(1)}, u32[]{:S(2)}, u32[]{:S(2)}) collective-permute-start(bf16[32,32,384]{2,1,0:T(8,128)(2,1)} %get-tuple-element.23), channel_id=1, source_target_pairs={{0,16},{16,0},{1,17},{17,1},{2,18},{18,2},{3,19},{19,3},{4,20},{20... | collective-permute-start | bytes 2359304 | tf_op jit(solution)/shard_map/cores/ppermute | solution.py:207
  57.7 1.1 add_convert_fusion.1
  58.8 2.6 %collective-permute-start.5 = (bf16[32,32,384]{2,1,0:T(8,128)(2,1)}, bf16[32,32,384]{2,1,0:T(8,128)(2,1)}, u32[]{:S(2)}, u32[]{:S(2)}) collective-permute-start(bf16[32,32,384]{2,1,0:T(8,128)(2,1)} %add_convert_fusion.1), channel_id=1, source_target_pairs={{0,8},{8,0},{16,792},{24,272},{256,264},{264,256},{272,24},{280,52... | collective-permute-start | bytes 2359304 | tf_op jit(solution)/shard_map/layers/ppermute | solution.py:209
  61.4 3.5 %back.1 = f32[64,4096]{1,0:T(8,128)} custom-call(s32[1,16]{1,0:T(1,128)S(1)} %copy-done.8, s32[1,16]{1,0:T(1,128)S(1)} %copy-done.9, s32[1,48]{1,0:T(1,128)S(1)} %collective-permute-done.1.far, s32[1]{0:T(128)} %bitcast.core, bf16[8,64,128]{2,1,0:T(8,128)(2,1)S(1)} %get-tuple-element.18.dgate, bf16[8,64,128]{2,1,0:T(8,128)(2,1)S(1)} %get-tuple-element.19.dup, ...), custom_call_target="tpu_custom_call" | custom-call | flops 134217728 | bytes 6291456 | tf_op jit(solution)/shard_map/back/pallas_call | solution.py:137
  65.0 8.0 %collective-permute-done.5 = bf16[32,32,384]{2,1,0:T(8,128)(2,1)} collective-permute-done((bf16[32,32,384]{2,1,0:T(8,128)(2,1)}, bf16[32,32,384]{2,1,0:T(8,128)(2,1)}, u32[]{:S(2)}, u32[]{:S(2)}) %collective-permute-start.5) | collective-permute-done | bytes 786464 | tf_op jit(solution)/shard_map/layers/ppermute | solution.py:209
  73.0 2.3 %add_convert_fusion = bf16[32,32,384]{2,1,0:T(8,128)(2,1)} fusion(bf16[32,32,384]{2,1,0:T(8,128)(2,1)} %collective-permute-done.5, bf16[32,32,384]{2,1,0:T(8,128)(2,1)S(1)} %collective-permute-done.3, bf16[32,32,384]{2,1,0:T(8,128)(2,1)S(1)} %copy-done.7), kind=kLoop, calls=%fused_computation.1 | loop fusion | flops 2359296 | bytes 3145728 | tf_op jit(solution)/shard_map/tile_sums/convert_element_type | solution.py:204
  75.3 19.8 %all-to-all-start.1 = ((bf16[32,32,384]{2,1,0:T(8,128)(2,1)}), bf16[32,32,384]{2,1,0:T(8,128)(2,1)S(1)}, u32[]{:S(2)}, u32[]{:S(2)}) async-start(bf16[32,32,384]{2,1,0:T(8,128)(2,1)} %add_convert_fusion), calls=%async_computation.2 | async-start | bytes 1572864 | tf_op jit(solution)/shard_map/tile_sums/all_to_all | solution.py:211
  95.1 18.0 %reduce-scatter.2.cloned.1.call-done = f32[8,4096]{1,0:T(8,128)} async-done(((f32[64,4096]{1,0:T(8,128)}), f32[8,4096]{1,0:T(8,128)}) %reduce-scatter.2.cloned.1.call-update) | async-done | bytes 131088 | tf_op jit(solution)/shard_map/partials/reduce_scatter | solution.py:203
  113.1 1.5 %convert_element_type.27 = bf16[8,4096]{1,0:T(8,128)(2,1)} convert(f32[8,4096]{1,0:T(8,128)} %reduce-scatter.2.cloned.1.call-done) | non-fusion elementwise | flops 32768 | bytes 196608 | tf_op jit(solution)/shard_map/partials/convert_element_type | solution.py:203
  114.6 5.2 %all-to-all-done.1 = bf16[32,32,384]{2,1,0:T(8,128)(2,1)S(1)} async-done(((bf16[32,32,384]{2,1,0:T(8,128)(2,1)}), bf16[32,32,384]{2,1,0:T(8,128)(2,1)S(1)}, u32[]{:S(2)}, u32[]{:S(2)}) %all-to-all-start.1) | async-done | bytes 786464 | tf_op jit(solution)/shard_map/tile_sums/all_to_all | solution.py:211
  119.8 0.7 convert_reduce_fusion
  (30 shorter events, 0.3 us)
Async XLA Ops:
  9.1 7.0 %copy-start = (bf16[1,16,128,128]{3,2,1,0:T(8,128)(2,1)S(1)}, bf16[1,16,128,128]{3,2,1,0:T(8,128)(2,1)}, u32[]{:S(2)}) copy-start(bf16[1,16,128,128]{3,2,1,0:T(8,128)(2,1)} %param.10) | copy-start | bytes 1572868
  9.1 7.0 %copy-start.8 = (s32[1,16]{1,0:T(1,128)S(1)}, s32[1,16]{1,0:T(1,128)}, u32[]{:S(2)}) copy-start(s32[1,16]{1,0:T(1,128)} %g_idx.5) | copy-start | bytes 196
  9.1 7.0 %copy-start.9 = (s32[1,16]{1,0:T(1,128)S(1)}, s32[1,16]{1,0:T(1,128)}, u32[]{:S(2)}) copy-start(s32[1,16]{1,0:T(1,128)} %u_idx.5) | copy-start | bytes 196
  9.1 7.0 %copy-start.10 = (s32[1,16]{1,0:T(1,128)S(1)}, s32[1,16]{1,0:T(1,128)}, u32[]{:S(2)}) copy-start(s32[1,16]{1,0:T(1,128)} %d_idx.3) | copy-start | bytes 196
  9.1 7.1 %copy-start.1 = (bf16[1,16,128,128]{3,2,1,0:T(8,128)(2,1)S(1)}, bf16[1,16,128,128]{3,2,1,0:T(8,128)(2,1)}, u32[]{:S(2)}) copy-start(bf16[1,16,128,128]{3,2,1,0:T(8,128)(2,1)} %param.11) | copy-start | bytes 1572868
  9.1 7.1 %copy-start.5 = (bf16[1,16,128,128]{3,2,1,0:T(8,128)(2,1)S(1)}, bf16[1,16,128,128]{3,2,1,0:T(8,128)(2,1)}, u32[]{:S(2)}) copy-start(bf16[1,16,128,128]{3,2,1,0:T(8,128)(2,1)} %param.12) | copy-start | bytes 1572868
  9.1 38.2 %all-to-all-start = ((bf16[8,8,8192]{2,1,0:T(8,128)(2,1)}), bf16[8,8,8192]{2,1,0:T(8,128)(2,1)S(1)}, u32[]{:S(2)}, u32[]{:S(2)}) async-start(bf16[8,8,8192]{2,1,0:T(8,128)(2,1)} %broadcast_in_dim.4), calls=%async_computation | async-start | bytes 2097152 | tf_op jit(solution)/shard_map/gather/all_to_all | solution.py:163
  16.0 97.0 %reduce-scatter.2.cloned.1.call-start = ((), (), s32[]{:S(2)}) async-start(), calls=%async_computation.3 | async-start | bytes 1179648 | tf_op jit(solution)/shard_map/partials/reduce_scatter | solution.py:203
  16.4 15.2 %collective-permute-start = (bf16[3,8,128,128]{3,2,1,0:T(8,128)(2,1)S(1)}, bf16[3,8,128,128]{3,2,1,0:T(8,128)(2,1)S(1)}, u32[]{:S(2)}, u32[]{:S(2)}) collective-permute-start(bf16[3,8,128,128]{3,2,1,0:T(8,128)(2,1)S(1)} %pad_maximum_fusion), channel_id=1, source_target_pairs={{0,8},{8,0},{16,792},{24,272},{256,264},{264,256},{272,24},{280,52... | collective-permute-start | bytes 2359304 | tf_op jit(solution)/shard_map/weights/ppermute | solution.py:170
  21.6 10.0 %collective-permute-start.1 = (s32[1,48]{1,0:T(1,128)S(1)}, s32[1,48]{1,0:T(1,128)S(1)}, u32[]{:S(2)}, u32[]{:S(2)}) collective-permute-start(s32[1,48]{1,0:T(1,128)S(1)} %pad_add_fusion), channel_id=1, source_target_pairs={{0,8},{8,0},{1,9},{9,1},{2,10},{10,2},{3,11},{11,3},{4,12},{12,4},... | collective-permute-start | bytes 584 | tf_op jit(solution)/shard_map/weights/ppermute | solution.py:169
  31.6 14.8 %collective-permute-start.2 = (bf16[3,8,128,128]{3,2,1,0:T(8,128)(2,1)S(1)}, bf16[3,8,128,128]{3,2,1,0:T(8,128)(2,1)S(1)}, u32[]{:S(2)}, u32[]{:S(2)}) collective-permute-start(bf16[3,8,128,128]{3,2,1,0:T(8,128)(2,1)S(1)} %collective-permute-done.ra), channel_id=1, source_target_pairs={{0,16},{16,0},{1,17},{17,1},{2,18},{18,2},{3,19},{19,3},{4,20},{20... | collective-permute-start | bytes 2359304 | tf_op jit(solution)/shard_map/weights/ppermute | solution.py:172
  46.4 0.9 copy-start.2
  47.3 1.1 copy-start.3
  53.3 5.4 %copy-start.6 = (bf16[32,32,384]{2,1,0:T(8,128)(2,1)}, bf16[32,32,384]{2,1,0:T(8,128)(2,1)S(1)}, u32[]{:S(2)}) copy-start(bf16[32,32,384]{2,1,0:T(8,128)(2,1)S(1)} %get-tuple-element.22) | copy-start | bytes 2359300
  53.3 4.3 %collective-permute-start.4 = (bf16[32,32,384]{2,1,0:T(8,128)(2,1)S(1)}, bf16[32,32,384]{2,1,0:T(8,128)(2,1)S(1)}, u32[]{:S(2)}, u32[]{:S(2)}) collective-permute-start(bf16[32,32,384]{2,1,0:T(8,128)(2,1)S(1)} %get-tuple-element.25), channel_id=1, source_target_pairs={{0,16},{16,0},{1,17},{17,1},{2,18},{18,2},{3,19},{19,3},{4,20},{20... | collective-permute-start | bytes 2359304 | tf_op jit(solution)/shard_map/cores/ppermute | solution.py:206
  55.6 9.3 %collective-permute-start.3 = (bf16[32,32,384]{2,1,0:T(8,128)(2,1)}, bf16[32,32,384]{2,1,0:T(8,128)(2,1)S(1)}, u32[]{:S(2)}, u32[]{:S(2)}) collective-permute-start(bf16[32,32,384]{2,1,0:T(8,128)(2,1)} %get-tuple-element.23), channel_id=1, source_target_pairs={{0,16},{16,0},{1,17},{17,1},{2,18},{18,2},{3,19},{19,3},{4,20},{20... | collective-permute-start | bytes 2359304 | tf_op jit(solution)/shard_map/cores/ppermute | solution.py:207
  57.7 3.7 %copy-start.4 = (bf16[3,8,128,128]{3,2,1,0:T(8,128)(2,1)S(1)}, bf16[3,8,128,128]{3,2,1,0:T(8,128)(2,1)}, u32[]{:S(2)}) copy-start(bf16[3,8,128,128]{3,2,1,0:T(8,128)(2,1)} %copy-done.2) | copy-start | bytes 2359300
  58.8 14.2 %collective-permute-start.5 = (bf16[32,32,384]{2,1,0:T(8,128)(2,1)}, bf16[32,32,384]{2,1,0:T(8,128)(2,1)}, u32[]{:S(2)}, u32[]{:S(2)}) collective-permute-start(bf16[32,32,384]{2,1,0:T(8,128)(2,1)} %add_convert_fusion.1), channel_id=1, source_target_pairs={{0,8},{8,0},{16,792},{24,272},{256,264},{264,256},{272,24},{280,52... | collective-permute-start | bytes 2359304 | tf_op jit(solution)/shard_map/layers/ppermute | solution.py:209
  64.9 8.0 %copy-start.7 = (bf16[32,32,384]{2,1,0:T(8,128)(2,1)S(1)}, bf16[32,32,384]{2,1,0:T(8,128)(2,1)}, u32[]{:S(2)}) copy-start(bf16[32,32,384]{2,1,0:T(8,128)(2,1)} %copy-done.6) | copy-start | bytes 2359300
  75.3 44.5 %all-to-all-start.1 = ((bf16[32,32,384]{2,1,0:T(8,128)(2,1)}), bf16[32,32,384]{2,1,0:T(8,128)(2,1)S(1)}, u32[]{:S(2)}, u32[]{:S(2)}) async-start(bf16[32,32,384]{2,1,0:T(8,128)(2,1)} %add_convert_fusion), calls=%async_computation.2 | async-start | bytes 1572864 | tf_op jit(solution)/shard_map/tile_sums/all_to_all | solution.py:211
Sparse Core Ops, SparseCore 0:
  65.1 47.9 reduce-scatter.1

commit v4 on v3

--- a/solution.py
+++ b/solution.py
@@ -66,7 +66,8 @@
         dup[b] = (dh * act).astype(BF16)
 
 
-def back(g_idx, u_idx, far, core, dgate, dup, gw, uw, ra, rb, part, held, sems, acc):
+def back(g_idx, u_idx, far, core, place, dgate, dup, gw, uw, ra, rb, *rest):
+    parts, (held, sems, acc) = rest[:-3], rest[-3:]
     copies = fetch((ra, rb), held, sems)
     hidden = dgate.shape[0] // 2
     acc[...] = jnp.zeros_like(acc)
@@ -76,8 +77,11 @@
             safe = jnp.maximum(v, 0)
             val = dot(grad[side * hidden + (safe & 3)], w[...], (1, 1))
             acc[safe >> 2] += jnp.where(v >= 0, val, 0.0)
-    for b in range(acc.shape[0]):
-        part[:, b * TILE : (b + 1) * TILE] = acc[b]
+    here = parts[0].shape[0]
+    for d, part in enumerate(parts):
+        at = pl.multiple_of(((place[0] + d) & (len(parts) - 1)) * here, here)
+        for b in range(acc.shape[0]):
+            part[:, b * TILE : (b + 1) * TILE] = acc[b, pl.ds(at, here), :].astype(BF16)
 
 
 def tile_terms(
@@ -182,11 +186,11 @@
         (ra, rb),
         [pltpu.VMEM((hidden, rows, TILE), F32)] * 3,
     )
-    (part,) = call(
+    parts = call(
         back,
         2 * work,
-        (jax.ShapeDtypeStruct((rows, width), F32),),
-        (*own[:2], far, core),
+        (shape(here, width),) * line,
+        (*own[:2], far, core, lax.axis_index("x").astype(jnp.int32).reshape(1)),
         (dgate, dup, gw, uw),
         (ra, rb),
         [pltpu.VMEM((blocks, rows, TILE), F32)],
@@ -198,10 +202,12 @@
         (*own, far, core),
         (xa, dgate, dup, hid),
     )
-    own_mine, _ = lax.optimization_barrier((own_mine, part))
+    own_mine, _ = lax.optimization_barrier((own_mine, parts[0]))
+    add = lambda *terms: sum(t.astype(F32) for t in terms).astype(BF16)
     with jax.named_scope("partials"):
-        input_sum = lax.psum_scatter(part, "x", scatter_dimension=0, tiled=True).astype(BF16)
-    add = lambda *terms: sum(t.astype(F32) for t in terms).astype(BF16)
+        ring = lambda d: [(i, (i + d) % line) for i in range(line)]
+        came = [lax.ppermute(parts[d], "x", ring(d)) for d in range(1, line)]
+        input_sum = add(parts[0], *came)
     with jax.named_scope("cores"):
         far_got = lax.ppermute(far_theirs, "c", SWAP)
         own_got = lax.ppermute(own_theirs, "c", SWAP)

time: 128 us -> 121 us (0.945)
  the two profiles are of different devices: /device:TPU:16 before, /device:TPU:22 now
where the time goes in v4:
time: 121 us; the launch traced here: 120 us
  starting transfers between devices  77.5 us (64%)
  waiting for transfers between devices  24.2 us (20%)
  Pallas kernels  7.45 us (6%)
  other arithmetic  6.19 us (5%)
  local copies, waits for them, and re-layouts  4.13 us (3%)
    ppermute x7, starting transfers between devices, per_device(): came = [lax.ppermute(parts[d], 'x', ring(d)) for d in range(1, line)]  28.4 us
    all_to_all x1, starting transfers between devices, per_device(): lax.all_to_all(add(own_mine, own_got, near), ('zh', 'y'), 0, 0, tiled=True)  15.9 us
    ppermute x1, starting transfers between devices, per_device(): rb = lax.ppermute(ra, 'c', SWAP)  12.5 us
    ppermute x1, waiting for transfers between devices, per_device(): near = lax.ppermute(add(far_mine, far_got), LAYERS, beside())  8.76 us
    ppermute x1, waiting for transfers between devices, per_device(): far = lax.ppermute(index, 'zl', SWAP)  8.09 us
    pallas_call x3, Pallas kernels, call(): pl.pallas_call(kernel, out_shape=out_shape, in_specs=[SMEM] * len(scalars...  7.45 us
    all_to_all x1, starting transfers between devices, per_device(): xa = lax.all_to_all(send, 'x', 0, 0, tiled=True).reshape(rows, 2 * width)  7.38 us
    ppermute x7, waiting for transfers between devices, per_device(): came = [lax.ppermute(parts[d], 'x', ring(d)) for d in range(1, line)]  5.42 us
  transfers between devices with their start and end apart: 15, of which 5 were waited for; matrix products, arithmetic and copies ran while one was open for 2% of the time, Pallas kernels for 2%

profile of v4, /device:TPU:22, one launch (start us, length us, event | category | flops | bytes accessed | tf_op | source)
XLA Modules:
  0.0 120.4 jit_solution(6648879333262648257)
XLA Ops:
  2.6 7.4 %all-to-all-start = ((bf16[8,8,8192]{2,1,0:T(8,128)(2,1)}), bf16[8,8,8192]{2,1,0:T(8,128)(2,1)S(1)}, u32[]{:S(2)}, u32[]{:S(2)}) async-start(bf16[8,8,8192]{2,1,0:T(8,128)(2,1)} %broadcast_in_dim.4), calls=%async_computation | async-start | bytes 2097152 | tf_op jit(solution)/shard_map/gather/all_to_all | solution.py:167
  10.3 5.2 %collective-permute-start = (bf16[3,8,128,128]{3,2,1,0:T(8,128)(2,1)S(1)}, bf16[3,8,128,128]{3,2,1,0:T(8,128)(2,1)S(1)}, u32[]{:S(2)}, u32[]{:S(2)}) collective-permute-start(bf16[3,8,128,128]{3,2,1,0:T(8,128)(2,1)S(1)} %pad_maximum_fusion), channel_id=1, source_target_pairs={{0,8},{8,0},{16,792},{24,272},{256,264},{264,256},{272,24},{280,52... | collective-permute-start | bytes 2359304 | tf_op jit(solution)/shard_map/weights/ppermute | solution.py:174
  15.5 1.9 %collective-permute-start.1 = (s32[1,48]{1,0:T(1,128)S(1)}, s32[1,48]{1,0:T(1,128)S(1)}, u32[]{:S(2)}, u32[]{:S(2)}) collective-permute-start(s32[1,48]{1,0:T(1,128)S(1)} %pad_add_fusion), channel_id=1, source_target_pairs={{0,8},{8,0},{1,9},{9,1},{2,10},{10,2},{3,11},{11,3},{4,12},{12,4},... | collective-permute-start | bytes 584 | tf_op jit(solution)/shard_map/weights/ppermute | solution.py:173
  17.4 8.1 %collective-permute-done.1.far = s32[1,48]{1,0:T(1,128)S(1)} collective-permute-done((s32[1,48]{1,0:T(1,128)S(1)}, s32[1,48]{1,0:T(1,128)S(1)}, u32[]{:S(2)}, u32[]{:S(2)}) %collective-permute-start.1) | collective-permute-done | bytes 224 | tf_op jit(solution)/shard_map/weights/ppermute | solution.py:173
  25.5 12.5 %collective-permute-start.2 = (bf16[3,8,128,128]{3,2,1,0:T(8,128)(2,1)S(1)}, bf16[3,8,128,128]{3,2,1,0:T(8,128)(2,1)S(1)}, u32[]{:S(2)}, u32[]{:S(2)}) collective-permute-start(bf16[3,8,128,128]{3,2,1,0:T(8,128)(2,1)S(1)} %collective-permute-done.ra), channel_id=1, source_target_pairs={{0,16},{16,0},{1,17},{17,1},{2,18},{18,2},{3,19},{19,3},{4,20},{20... | collective-permute-start | bytes 2359304 | tf_op jit(solution)/shard_map/weights/ppermute | solution.py:176
  38.0 1.9 %collective-permute-done.2.rb = bf16[3,8,128,128]{3,2,1,0:T(8,128)(2,1)S(1)} collective-permute-done((bf16[3,8,128,128]{3,2,1,0:T(8,128)(2,1)S(1)}, bf16[3,8,128,128]{3,2,1,0:T(8,128)(2,1)S(1)}, u32[]{:S(2)}, u32[]{:S(2)}) %collective-permute-start.2) | collective-permute-done | bytes 786464 | tf_op jit(solution)/shard_map/weights/ppermute | solution.py:176
  42.0 2.3 %forward.1 = (bf16[8,64,128]{2,1,0:T(8,128)(2,1)S(1)}, bf16[8,64,128]{2,1,0:T(8,128)(2,1)S(1)}, bf16[8,64,128]{2,1,0:T(8,128)(2,1)S(1)}) custom-call(s32[1,16]{1,0:T(1,128)S(1)} %copy-done.10, s32[1,16]{1,0:T(1,128)S(1)} %copy-done.11, s32[1,16]{1,0:T(1,128)S(1)} %copy-done.12, s32[1,48]{1,0:T(1,128)S(1)} %collective-permute-done.1.far, s32[1]{0:T(128)} %bitcast.core, ...), custom_call_target="tpu_custom_call" | custom-call | flops 201326592 | bytes 6291456 | tf_op jit(solution)/shard_map/forward/pallas_call | solution.py:141
  44.3 2.6 %tile_terms.1 = (bf16[32,32,384]{2,1,0:T(8,128)(2,1)S(1)}, bf16[32,32,384]{2,1,0:T(8,128)(2,1)}, bf16[32,32,384]{2,1,0:T(8,128)(2,1)S(1)}, bf16[32,32,384]{2,1,0:T(8,128)(2,1)S(1)}) custom-call(s32[1,16]{1,0:T(1,128)S(1)} %copy-done.10, s32[1,16]{1,0:T(1,128)S(1)} %copy-done.11, s32[1,16]{1,0:T(1,128)S(1)} %copy-done.12, ...), custom_call_target="tpu_custom_call" | custom-call | flops 201326592 | bytes 6291456 | tf_op jit(solution)/shard_map/tile_terms/pallas_call | solution.py:141
  46.9 2.3 %collective-permute-start.11 = (bf16[32,32,384]{2,1,0:T(8,128)(2,1)S(1)}, bf16[32,32,384]{2,1,0:T(8,128)(2,1)S(1)}, u32[]{:S(2)}, u32[]{:S(2)}) collective-permute-start(bf16[32,32,384]{2,1,0:T(8,128)(2,1)S(1)} %get-tuple-element.41), channel_id=1, source_target_pairs={{0,16},{16,0},{1,17},{17,1},{2,18},{18,2},{3,19},{19,3},{4,20},{20... | collective-permute-start | bytes 2359304 | tf_op jit(solution)/shard_map/cores/ppermute | solution.py:212
  49.1 2.0 %collective-permute-start.10 = (bf16[32,32,384]{2,1,0:T(8,128)(2,1)}, bf16[32,32,384]{2,1,0:T(8,128)(2,1)}, u32[]{:S(2)}, u32[]{:S(2)}) collective-permute-start(bf16[32,32,384]{2,1,0:T(8,128)(2,1)} %get-tuple-element.39), channel_id=1, source_target_pairs={{0,16},{16,0},{1,17},{17,1},{2,18},{18,2},{3,19},{19,3},{4,20},{20... | collective-permute-start | bytes 2359304 | tf_op jit(solution)/shard_map/cores/ppermute | solution.py:213
  52.3 1.9 %collective-permute-start.12 = (bf16[32,32,384]{2,1,0:T(8,128)(2,1)}, bf16[32,32,384]{2,1,0:T(8,128)(2,1)}, u32[]{:S(2)}, u32[]{:S(2)}) collective-permute-start(bf16[32,32,384]{2,1,0:T(8,128)(2,1)} %add_convert_fusion.1), channel_id=1, source_target_pairs={{0,8},{8,0},{16,792},{24,272},{256,264},{264,256},{272,24},{280,52... | collective-permute-start | bytes 2359304 | tf_op jit(solution)/shard_map/layers/ppermute | solution.py:215
  55.1 2.6 %back.1 = (bf16[8,4096]{1,0:T(8,128)(2,1)S(1)}, bf16[8,4096]{1,0:T(8,128)(2,1)S(1)}, bf16[8,4096]{1,0:T(8,128)(2,1)S(1)}, bf16[8,4096]{1,0:T(8,128)(2,1)S(1)}, b...) custom-call(s32[1,16]{1,0:T(1,128)S(1)} %copy-done.10, ...), custom_call_target="tpu_custom_call" | custom-call | flops 134217728 | bytes 6291456 | tf_op jit(solution)/shard_map/back/pallas_call | solution.py:141
  57.7 8.8 %collective-permute-done.12 = bf16[32,32,384]{2,1,0:T(8,128)(2,1)} collective-permute-done((bf16[32,32,384]{2,1,0:T(8,128)(2,1)}, bf16[32,32,384]{2,1,0:T(8,128)(2,1)}, u32[]{:S(2)}, u32[]{:S(2)}) %collective-permute-start.12) | collective-permute-done | bytes 786464 | tf_op jit(solution)/shard_map/layers/ppermute | solution.py:215
  66.5 2.6 %add_convert_fusion = bf16[32,32,384]{2,1,0:T(8,128)(2,1)} fusion(bf16[32,32,384]{2,1,0:T(8,128)(2,1)} %collective-permute-done.12, bf16[32,32,384]{2,1,0:T(8,128)(2,1)} %collective-permute-done.10, bf16[32,32,384]{2,1,0:T(8,128)(2,1)S(1)} %copy-done.7), kind=kLoop, calls=%fused_computation.1 | loop fusion | flops 2359296 | bytes 3145728 | tf_op jit(solution)/shard_map/tile_sums/convert_element_type | solution.py:206
  69.1 15.9 %all-to-all-start.1 = ((bf16[32,32,384]{2,1,0:T(8,128)(2,1)}), bf16[32,32,384]{2,1,0:T(8,128)(2,1)S(1)}, u32[]{:S(2)}, u32[]{:S(2)}) async-start(bf16[32,32,384]{2,1,0:T(8,128)(2,1)} %add_convert_fusion), calls=%async_computation.1 | async-start | bytes 1572864 | tf_op jit(solution)/shard_map/tile_sums/all_to_all | solution.py:217
  85.0 3.7 %collective-permute-start.3 = (bf16[8,4096]{1,0:T(8,128)(2,1)S(1)}, bf16[8,4096]{1,0:T(8,128)(2,1)S(1)}, u32[]{:S(2)}, u32[]{:S(2)}) collective-permute-start(bf16[8,4096]{1,0:T(8,128)(2,1)S(1)} %get-tuple-element.29), channel_id=1, source_target_pairs={{0,1},{1,2},{2,3},{3,4},{4,5},{5,6},{6,7},{7,0},{8,9},{9,10},{10,1... | collective-permute-start | bytes 196616 | tf_op jit(solution)/shard_map/partials/ppermute | solution.py:209
  88.6 4.1 %collective-permute-start.4 = (bf16[8,4096]{1,0:T(8,128)(2,1)S(1)}, bf16[8,4096]{1,0:T(8,128)(2,1)S(1)}, u32[]{:S(2)}, u32[]{:S(2)}) collective-permute-start(bf16[8,4096]{1,0:T(8,128)(2,1)S(1)} %get-tuple-element.30), channel_id=1, source_target_pairs={{0,2},{1,3},{2,4},{3,5},{4,6},{5,7},{6,0},{7,1},{8,10},{9,11},{10,... | collective-permute-start | bytes 196616 | tf_op jit(solution)/shard_map/partials/ppermute | solution.py:209
  92.8 5.6 %collective-permute-start.5 = (bf16[8,4096]{1,0:T(8,128)(2,1)S(1)}, bf16[8,4096]{1,0:T(8,128)(2,1)S(1)}, u32[]{:S(2)}, u32[]{:S(2)}) collective-permute-start(bf16[8,4096]{1,0:T(8,128)(2,1)S(1)} %get-tuple-element.31), channel_id=1, source_target_pairs={{0,3},{1,4},{2,5},{3,6},{4,7},{5,0},{6,1},{7,2},{8,11},{9,12},{10,... | collective-permute-start | bytes 196616 | tf_op jit(solution)/shard_map/partials/ppermute | solution.py:209
  98.4 3.4 %collective-permute-start.6 = (bf16[8,4096]{1,0:T(8,128)(2,1)S(1)}, bf16[8,4096]{1,0:T(8,128)(2,1)S(1)}, u32[]{:S(2)}, u32[]{:S(2)}) collective-permute-start(bf16[8,4096]{1,0:T(8,128)(2,1)S(1)} %get-tuple-element.32), channel_id=1, source_target_pairs={{0,4},{1,5},{2,6},{3,7},{4,0},{5,1},{6,2},{7,3},{8,12},{9,13},{10,... | collective-permute-start | bytes 196616 | tf_op jit(solution)/shard_map/partials/ppermute | solution.py:209
  101.8 4.2 %collective-permute-start.7 = (bf16[8,4096]{1,0:T(8,128)(2,1)S(1)}, bf16[8,4096]{1,0:T(8,128)(2,1)S(1)}, u32[]{:S(2)}, u32[]{:S(2)}) collective-permute-start(bf16[8,4096]{1,0:T(8,128)(2,1)S(1)} %get-tuple-element.33), channel_id=1, source_target_pairs={{0,5},{1,6},{2,7},{3,0},{4,1},{5,2},{6,3},{7,4},{8,13},{9,14},{10,... | collective-permute-start | bytes 196616 | tf_op jit(solution)/shard_map/partials/ppermute | solution.py:209
  106.0 5.6 %collective-permute-start.8 = (bf16[8,4096]{1,0:T(8,128)(2,1)S(1)}, bf16[8,4096]{1,0:T(8,128)(2,1)S(1)}, u32[]{:S(2)}, u32[]{:S(2)}) collective-permute-start(bf16[8,4096]{1,0:T(8,128)(2,1)S(1)} %get-tuple-element.34), channel_id=1, source_target_pairs={{0,6},{1,7},{2,0},{3,1},{4,2},{5,3},{6,4},{7,5},{8,14},{9,15},{10,... | collective-permute-start | bytes 196616 | tf_op jit(solution)/shard_map/partials/ppermute | solution.py:209
  111.6 1.9 %collective-permute-start.9 = (bf16[8,4096]{1,0:T(8,128)(2,1)S(1)}, bf16[8,4096]{1,0:T(8,128)(2,1)S(1)}, u32[]{:S(2)}, u32[]{:S(2)}) collective-permute-start(bf16[8,4096]{1,0:T(8,128)(2,1)S(1)} %get-tuple-element.35), channel_id=1, source_target_pairs={{0,7},{1,0},{2,1},{3,2},{4,3},{5,4},{6,5},{7,6},{8,15},{9,8},{10,9... | collective-permute-start | bytes 196616 | tf_op jit(solution)/shard_map/partials/ppermute | solution.py:209
  113.5 1.9 %collective-permute-done.8 = bf16[8,4096]{1,0:T(8,128)(2,1)S(1)} collective-permute-done((bf16[8,4096]{1,0:T(8,128)(2,1)S(1)}, bf16[8,4096]{1,0:T(8,128)(2,1)S(1)}, u32[]{:S(2)}, u32[]{:S(2)}) %collective-permute-start.8) | collective-permute-done | bytes 65568 | tf_op jit(solution)/shard_map/partials/ppermute | solution.py:209
  115.4 3.6 %collective-permute-done.9 = bf16[8,4096]{1,0:T(8,128)(2,1)S(1)} collective-permute-done((bf16[8,4096]{1,0:T(8,128)(2,1)S(1)}, bf16[8,4096]{1,0:T(8,128)(2,1)S(1)}, u32[]{:S(2)}, u32[]{:S(2)}) %collective-permute-start.9) | collective-permute-done | bytes 65568 | tf_op jit(solution)/shard_map/partials/ppermute | solution.py:209
  (45 shorter events, 7.7 us)
Async XLA Ops:
  2.6 7.4 %copy-start = (bf16[1,16,128,128]{3,2,1,0:T(8,128)(2,1)S(1)}, bf16[1,16,128,128]{3,2,1,0:T(8,128)(2,1)}, u32[]{:S(2)}) copy-start(bf16[1,16,128,128]{3,2,1,0:T(8,128)(2,1)} %param.10) | copy-start | bytes 1572868
  2.6 7.4 %copy-start.10 = (s32[1,16]{1,0:T(1,128)S(1)}, s32[1,16]{1,0:T(1,128)}, u32[]{:S(2)}) copy-start(s32[1,16]{1,0:T(1,128)} %g_idx.5) | copy-start | bytes 196
  2.6 7.4 %copy-start.11 = (s32[1,16]{1,0:T(1,128)S(1)}, s32[1,16]{1,0:T(1,128)}, u32[]{:S(2)}) copy-start(s32[1,16]{1,0:T(1,128)} %u_idx.5) | copy-start | bytes 196
  2.6 7.5 %copy-start.12 = (s32[1,16]{1,0:T(1,128)S(1)}, s32[1,16]{1,0:T(1,128)}, u32[]{:S(2)}) copy-start(s32[1,16]{1,0:T(1,128)} %d_idx.3) | copy-start | bytes 196
  2.6 7.5 %copy-start.1 = (bf16[1,16,128,128]{3,2,1,0:T(8,128)(2,1)S(1)}, bf16[1,16,128,128]{3,2,1,0:T(8,128)(2,1)}, u32[]{:S(2)}) copy-start(bf16[1,16,128,128]{3,2,1,0:T(8,128)(2,1)} %param.11) | copy-start | bytes 1572868
  2.6 7.5 %copy-start.5 = (bf16[1,16,128,128]{3,2,1,0:T(8,128)(2,1)S(1)}, bf16[1,16,128,128]{3,2,1,0:T(8,128)(2,1)}, u32[]{:S(2)}) copy-start(bf16[1,16,128,128]{3,2,1,0:T(8,128)(2,1)} %param.12) | copy-start | bytes 1572868
  2.6 38.2 %all-to-all-start = ((bf16[8,8,8192]{2,1,0:T(8,128)(2,1)}), bf16[8,8,8192]{2,1,0:T(8,128)(2,1)S(1)}, u32[]{:S(2)}, u32[]{:S(2)}) async-start(bf16[8,8,8192]{2,1,0:T(8,128)(2,1)} %broadcast_in_dim.4), calls=%async_computation | async-start | bytes 2097152 | tf_op jit(solution)/shard_map/gather/all_to_all | solution.py:167
  10.3 15.2 %collective-permute-start = (bf16[3,8,128,128]{3,2,1,0:T(8,128)(2,1)S(1)}, bf16[3,8,128,128]{3,2,1,0:T(8,128)(2,1)S(1)}, u32[]{:S(2)}, u32[]{:S(2)}) collective-permute-start(bf16[3,8,128,128]{3,2,1,0:T(8,128)(2,1)S(1)} %pad_maximum_fusion), channel_id=1, source_target_pairs={{0,8},{8,0},{16,792},{24,272},{256,264},{264,256},{272,24},{280,52... | collective-permute-start | bytes 2359304 | tf_op jit(solution)/shard_map/weights/ppermute | solution.py:174
  15.5 10.0 %collective-permute-start.1 = (s32[1,48]{1,0:T(1,128)S(1)}, s32[1,48]{1,0:T(1,128)S(1)}, u32[]{:S(2)}, u32[]{:S(2)}) collective-permute-start(s32[1,48]{1,0:T(1,128)S(1)} %pad_add_fusion), channel_id=1, source_target_pairs={{0,8},{8,0},{1,9},{9,1},{2,10},{10,2},{3,11},{11,3},{4,12},{12,4},... | collective-permute-start | bytes 584 | tf_op jit(solution)/shard_map/weights/ppermute | solution.py:173
  25.5 14.4 %collective-permute-start.2 = (bf16[3,8,128,128]{3,2,1,0:T(8,128)(2,1)S(1)}, bf16[3,8,128,128]{3,2,1,0:T(8,128)(2,1)S(1)}, u32[]{:S(2)}, u32[]{:S(2)}) collective-permute-start(bf16[3,8,128,128]{3,2,1,0:T(8,128)(2,1)S(1)} %collective-permute-done.ra), channel_id=1, source_target_pairs={{0,16},{16,0},{1,17},{17,1},{2,18},{18,2},{3,19},{19,3},{4,20},{20... | collective-permute-start | bytes 2359304 | tf_op jit(solution)/shard_map/weights/ppermute | solution.py:176
  44.3 8.0 %copy-start.8 = (bf16[8,64,128]{2,1,0:T(8,128)(2,1)}, bf16[8,64,128]{2,1,0:T(8,128)(2,1)S(1)}, u32[]{:S(2)}) copy-start(bf16[8,64,128]{2,1,0:T(8,128)(2,1)S(1)} %get-tuple-element.27.dup) | copy-start | bytes 393220
  46.9 5.4 %copy-start.6 = (bf16[32,32,384]{2,1,0:T(8,128)(2,1)}, bf16[32,32,384]{2,1,0:T(8,128)(2,1)S(1)}, u32[]{:S(2)}) copy-start(bf16[32,32,384]{2,1,0:T(8,128)(2,1)S(1)} %get-tuple-element.38) | copy-start | bytes 2359300
  46.9 4.3 %collective-permute-start.11 = (bf16[32,32,384]{2,1,0:T(8,128)(2,1)S(1)}, bf16[32,32,384]{2,1,0:T(8,128)(2,1)S(1)}, u32[]{:S(2)}, u32[]{:S(2)}) collective-permute-start(bf16[32,32,384]{2,1,0:T(8,128)(2,1)S(1)} %get-tuple-element.41), channel_id=1, source_target_pairs={{0,16},{16,0},{1,17},{17,1},{2,18},{18,2},{3,19},{19,3},{4,20},{20... | collective-permute-start | bytes 2359304 | tf_op jit(solution)/shard_map/cores/ppermute | solution.py:212
  49.1 8.6 %collective-permute-start.10 = (bf16[32,32,384]{2,1,0:T(8,128)(2,1)}, bf16[32,32,384]{2,1,0:T(8,128)(2,1)}, u32[]{:S(2)}, u32[]{:S(2)}) collective-permute-start(bf16[32,32,384]{2,1,0:T(8,128)(2,1)} %get-tuple-element.39), channel_id=1, source_target_pairs={{0,16},{16,0},{1,17},{17,1},{2,18},{18,2},{3,19},{19,3},{4,20},{20... | collective-permute-start | bytes 2359304 | tf_op jit(solution)/shard_map/cores/ppermute | solution.py:213
  52.3 14.2 %collective-permute-start.12 = (bf16[32,32,384]{2,1,0:T(8,128)(2,1)}, bf16[32,32,384]{2,1,0:T(8,128)(2,1)}, u32[]{:S(2)}, u32[]{:S(2)}) collective-permute-start(bf16[32,32,384]{2,1,0:T(8,128)(2,1)} %add_convert_fusion.1), channel_id=1, source_target_pairs={{0,8},{8,0},{16,792},{24,272},{256,264},{264,256},{272,24},{280,52... | collective-permute-start | bytes 2359304 | tf_op jit(solution)/shard_map/layers/ppermute | solution.py:215
  55.1 11.4 %copy-start.7 = (bf16[32,32,384]{2,1,0:T(8,128)(2,1)S(1)}, bf16[32,32,384]{2,1,0:T(8,128)(2,1)}, u32[]{:S(2)}) copy-start(bf16[32,32,384]{2,1,0:T(8,128)(2,1)} %copy-done.6) | copy-start | bytes 2359300
  69.1 50.5 %all-to-all-start.1 = ((bf16[32,32,384]{2,1,0:T(8,128)(2,1)}), bf16[32,32,384]{2,1,0:T(8,128)(2,1)S(1)}, u32[]{:S(2)}, u32[]{:S(2)}) async-start(bf16[32,32,384]{2,1,0:T(8,128)(2,1)} %add_convert_fusion), calls=%async_computation.1 | async-start | bytes 1572864 | tf_op jit(solution)/shard_map/tile_sums/all_to_all | solution.py:217
  85.0 21.0 %collective-permute-start.3 = (bf16[8,4096]{1,0:T(8,128)(2,1)S(1)}, bf16[8,4096]{1,0:T(8,128)(2,1)S(1)}, u32[]{:S(2)}, u32[]{:S(2)}) collective-permute-start(bf16[8,4096]{1,0:T(8,128)(2,1)S(1)} %get-tuple-element.29), channel_id=1, source_target_pairs={{0,1},{1,2},{2,3},{3,4},{4,5},{5,6},{6,7},{7,0},{8,9},{9,10},{10,1... | collective-permute-start | bytes 196616 | tf_op jit(solution)/shard_map/partials/ppermute | solution.py:209
  88.6 22.9 %collective-permute-start.4 = (bf16[8,4096]{1,0:T(8,128)(2,1)S(1)}, bf16[8,4096]{1,0:T(8,128)(2,1)S(1)}, u32[]{:S(2)}, u32[]{:S(2)}) collective-permute-start(bf16[8,4096]{1,0:T(8,128)(2,1)S(1)} %get-tuple-element.30), channel_id=1, source_target_pairs={{0,2},{1,3},{2,4},{3,5},{4,6},{5,7},{6,0},{7,1},{8,10},{9,11},{10,... | collective-permute-start | bytes 196616 | tf_op jit(solution)/shard_map/partials/ppermute | solution.py:209
  92.8 20.7 %collective-permute-start.5 = (bf16[8,4096]{1,0:T(8,128)(2,1)S(1)}, bf16[8,4096]{1,0:T(8,128)(2,1)S(1)}, u32[]{:S(2)}, u32[]{:S(2)}) collective-permute-start(bf16[8,4096]{1,0:T(8,128)(2,1)S(1)} %get-tuple-element.31), channel_id=1, source_target_pairs={{0,3},{1,4},{2,5},{3,6},{4,7},{5,0},{6,1},{7,2},{8,11},{9,12},{10,... | collective-permute-start | bytes 196616 | tf_op jit(solution)/shard_map/partials/ppermute | solution.py:209
  98.4 15.1 %collective-permute-start.6 = (bf16[8,4096]{1,0:T(8,128)(2,1)S(1)}, bf16[8,4096]{1,0:T(8,128)(2,1)S(1)}, u32[]{:S(2)}, u32[]{:S(2)}) collective-permute-start(bf16[8,4096]{1,0:T(8,128)(2,1)S(1)} %get-tuple-element.32), channel_id=1, source_target_pairs={{0,4},{1,5},{2,6},{3,7},{4,0},{5,1},{6,2},{7,3},{8,12},{9,13},{10,... | collective-permute-start | bytes 196616 | tf_op jit(solution)/shard_map/partials/ppermute | solution.py:209
  101.8 11.7 %collective-permute-start.7 = (bf16[8,4096]{1,0:T(8,128)(2,1)S(1)}, bf16[8,4096]{1,0:T(8,128)(2,1)S(1)}, u32[]{:S(2)}, u32[]{:S(2)}) collective-permute-start(bf16[8,4096]{1,0:T(8,128)(2,1)S(1)} %get-tuple-element.33), channel_id=1, source_target_pairs={{0,5},{1,6},{2,7},{3,0},{4,1},{5,2},{6,3},{7,4},{8,13},{9,14},{10,... | collective-permute-start | bytes 196616 | tf_op jit(solution)/shard_map/partials/ppermute | solution.py:209
  106.0 9.4 %collective-permute-start.8 = (bf16[8,4096]{1,0:T(8,128)(2,1)S(1)}, bf16[8,4096]{1,0:T(8,128)(2,1)S(1)}, u32[]{:S(2)}, u32[]{:S(2)}) collective-permute-start(bf16[8,4096]{1,0:T(8,128)(2,1)S(1)} %get-tuple-element.34), channel_id=1, source_target_pairs={{0,6},{1,7},{2,0},{3,1},{4,2},{5,3},{6,4},{7,5},{8,14},{9,15},{10,... | collective-permute-start | bytes 196616 | tf_op jit(solution)/shard_map/partials/ppermute | solution.py:209
  111.6 7.4 %collective-permute-start.9 = (bf16[8,4096]{1,0:T(8,128)(2,1)S(1)}, bf16[8,4096]{1,0:T(8,128)(2,1)S(1)}, u32[]{:S(2)}, u32[]{:S(2)}) collective-permute-start(bf16[8,4096]{1,0:T(8,128)(2,1)S(1)} %get-tuple-element.35), channel_id=1, source_target_pairs={{0,7},{1,0},{2,1},{3,2},{4,3},{5,4},{6,5},{7,6},{8,15},{9,8},{10,9... | collective-permute-start | bytes 196616 | tf_op jit(solution)/shard_map/partials/ppermute | solution.py:209
  (4 other events, 6.0 us)

commit v5 on v4

--- a/solution.py
+++ b/solution.py
@@ -66,8 +66,8 @@
         dup[b] = (dh * act).astype(BF16)
 
 
-def back(g_idx, u_idx, far, core, place, dgate, dup, gw, uw, ra, rb, *rest):
-    parts, (held, sems, acc) = rest[:-3], rest[-3:]
+def back(g_idx, u_idx, far, core, place, dgate, dup, gw, uw, ra, rb, give, *rest):
+    keep, (held, sems, acc) = rest[:-3], rest[-3:]
     copies = fetch((ra, rb), held, sems)
     hidden = dgate.shape[0] // 2
     acc[...] = jnp.zeros_like(acc)
@@ -77,11 +77,15 @@
             safe = jnp.maximum(v, 0)
             val = dot(grad[side * hidden + (safe & 3)], w[...], (1, 1))
             acc[safe >> 2] += jnp.where(v >= 0, val, 0.0)
-    here = parts[0].shape[0]
-    for d, part in enumerate(parts):
-        at = pl.multiple_of(((place[0] + d) & (len(parts) - 1)) * here, here)
+    here = keep[0].shape[0]
+    me = place[0]
+    near = me + 1 - 2 * (me & 1)
+    for k in range(len(keep)):
+        row = lambda x: pl.ds(pl.multiple_of(((x + 2 * k) & (2 * len(keep) - 1)) * here, here), here)
         for b in range(acc.shape[0]):
-            part[:, b * TILE : (b + 1) * TILE] = acc[b, pl.ds(at, here), :].astype(BF16)
+            at = slice(b * TILE, (b + 1) * TILE)
+            give[k, :, at] = acc[b, row(near), :].astype(BF16)
+            keep[k][:, at] = acc[b, row(me), :].astype(BF16)
 
 
 def tile_terms(
@@ -186,10 +190,10 @@
         (ra, rb),
         [pltpu.VMEM((hidden, rows, TILE), F32)] * 3,
     )
-    parts = call(
+    give, *keep = call(
         back,
         2 * work,
-        (shape(here, width),) * line,
+        (shape(line // 2, here, width),) + (shape(here, width),) * (line // 2),
         (*own[:2], far, core, lax.axis_index("x").astype(jnp.int32).reshape(1)),
         (dgate, dup, gw, uw),
         (ra, rb),
@@ -202,12 +206,14 @@
         (*own, far, core),
         (xa, dgate, dup, hid),
     )
-    own_mine, _ = lax.optimization_barrier((own_mine, parts[0]))
     add = lambda *terms: sum(t.astype(F32) for t in terms).astype(BF16)
     with jax.named_scope("partials"):
+        got = lax.ppermute(give, "x", [(i, i ^ 1) for i in range(line)])
+        pair = [add(keep[k], got[k]) for k in range(line // 2)]
         ring = lambda d: [(i, (i + d) % line) for i in range(line)]
-        came = [lax.ppermute(parts[d], "x", ring(d)) for d in range(1, line)]
-        input_sum = add(parts[0], *came)
+        came = [lax.ppermute(pair[k], "x", ring(2 * k)) for k in (1, 3, 2)]
+        input_sum = add(*[t.astype(F32) for t in (keep[0], got[0])], *came)
+    own_mine, got = lax.optimization_barrier((own_mine, got))
     with jax.named_scope("cores"):
         far_got = lax.ppermute(far_theirs, "c", SWAP)
         own_got = lax.ppermute(own_theirs, "c", SWAP)

time: 121 us -> 115 us (0.950)
  the two profiles are of different devices: /device:TPU:22 before, /device:TPU:16 now
where the time goes in v5:
time: 115 us
  starting transfers between devices  68.5 us (60%)
  waiting for transfers between devices  27.6 us (24%)
  Pallas kernels  7.41 us (6%)
  other arithmetic  6.23 us (5%)
  local copies, waits for them, and re-layouts  4.14 us (4%)
    all_to_all x1, starting transfers between devices, per_device(): lax.all_to_all(add(own_mine, own_got, near), ('zh', 'y'), 0, 0, tiled=True)  21.1 us
    ppermute x1, starting transfers between devices, per_device(): rb = lax.ppermute(ra, 'c', SWAP)  13.1 us
    ppermute x3, starting transfers between devices, per_device(): came = [lax.ppermute(pair[k], 'x', ring(2 * k)) for k in (1, 3, 2)]  10.4 us
    ppermute x1, waiting for transfers between devices, per_device(): far = lax.ppermute(index, 'zl', SWAP)  8.09 us
    all_to_all x1, waiting for transfers between devices, per_device(): lax.all_to_all(add(own_mine, own_got, near), ('zh', 'y'), 0, 0, tiled=True)  7.7 us
    pallas_call x3, Pallas kernels, call(): pl.pallas_call(kernel, out_shape=out_shape, in_specs=[SMEM] * len(scalars...  7.41 us
    all_to_all x1, starting transfers between devices, per_device(): xa = lax.all_to_all(send, 'x', 0, 0, tiled=True).reshape(rows, 2 * width)  6.9 us
    ppermute x1, waiting for transfers between devices, per_device(): got = lax.ppermute(give, 'x', [(i, i ^ 1) for i in range(line)])  5.21 us
  transfers between devices with their start and end apart: 12, of which 6 were waited for; matrix products, arithmetic and copies ran while one was open for 2% of the time, Pallas kernels for 2%

profile of v5, /device:TPU:16, one launch (start us, length us, event | category | flops | bytes accessed | tf_op | source)
XLA Modules:
  0.0 114.7 jit_solution(8775617206169872180)
XLA Ops:
  2.6 6.9 %all-to-all-start = ((bf16[8,8,8192]{2,1,0:T(8,128)(2,1)}), bf16[8,8,8192]{2,1,0:T(8,128)(2,1)S(1)}, u32[]{:S(2)}, u32[]{:S(2)}) async-start(bf16[8,8,8192]{2,1,0:T(8,128)(2,1)} %broadcast_in_dim.4), calls=%async_computation | async-start | bytes 2097152 | tf_op jit(solution)/shard_map/gather/all_to_all | solution.py:171
  9.8 5.2 %collective-permute-start = (bf16[3,8,128,128]{3,2,1,0:T(8,128)(2,1)S(1)}, bf16[3,8,128,128]{3,2,1,0:T(8,128)(2,1)S(1)}, u32[]{:S(2)}, u32[]{:S(2)}) collective-permute-start(bf16[3,8,128,128]{3,2,1,0:T(8,128)(2,1)S(1)} %pad_maximum_fusion), channel_id=1, source_target_pairs={{0,8},{8,0},{16,792},{24,272},{256,264},{264,256},{272,24},{280,52... | collective-permute-start | bytes 2359304 | tf_op jit(solution)/shard_map/weights/ppermute | solution.py:178
  15.0 1.9 %collective-permute-start.1 = (s32[1,48]{1,0:T(1,128)S(1)}, s32[1,48]{1,0:T(1,128)S(1)}, u32[]{:S(2)}, u32[]{:S(2)}) collective-permute-start(s32[1,48]{1,0:T(1,128)S(1)} %pad_add_fusion), channel_id=1, source_target_pairs={{0,8},{8,0},{1,9},{9,1},{2,10},{10,2},{3,11},{11,3},{4,12},{12,4},... | collective-permute-start | bytes 584 | tf_op jit(solution)/shard_map/weights/ppermute | solution.py:177
  16.9 8.1 %collective-permute-done.1.far = s32[1,48]{1,0:T(1,128)S(1)} collective-permute-done((s32[1,48]{1,0:T(1,128)S(1)}, s32[1,48]{1,0:T(1,128)S(1)}, u32[]{:S(2)}, u32[]{:S(2)}) %collective-permute-start.1) | collective-permute-done | bytes 224 | tf_op jit(solution)/shard_map/weights/ppermute | solution.py:177
  25.0 13.1 %collective-permute-start.2 = (bf16[3,8,128,128]{3,2,1,0:T(8,128)(2,1)S(1)}, bf16[3,8,128,128]{3,2,1,0:T(8,128)(2,1)S(1)}, u32[]{:S(2)}, u32[]{:S(2)}) collective-permute-start(bf16[3,8,128,128]{3,2,1,0:T(8,128)(2,1)S(1)} %collective-permute-done.ra), channel_id=1, source_target_pairs={{0,16},{16,0},{1,17},{17,1},{2,18},{18,2},{3,19},{19,3},{4,20},{20... | collective-permute-start | bytes 2359304 | tf_op jit(solution)/shard_map/weights/ppermute | solution.py:180
  38.1 1.9 %collective-permute-done.2.rb = bf16[3,8,128,128]{3,2,1,0:T(8,128)(2,1)S(1)} collective-permute-done((bf16[3,8,128,128]{3,2,1,0:T(8,128)(2,1)S(1)}, bf16[3,8,128,128]{3,2,1,0:T(8,128)(2,1)S(1)}, u32[]{:S(2)}, u32[]{:S(2)}) %collective-permute-start.2) | collective-permute-done | bytes 786464 | tf_op jit(solution)/shard_map/weights/ppermute | solution.py:180
  40.9 1.1 copy-done.3
  42.1 2.3 %forward.1 = (bf16[8,64,128]{2,1,0:T(8,128)(2,1)S(1)}, bf16[8,64,128]{2,1,0:T(8,128)(2,1)S(1)}, bf16[8,64,128]{2,1,0:T(8,128)(2,1)S(1)}) custom-call(s32[1,16]{1,0:T(1,128)S(1)} %copy-done.10, s32[1,16]{1,0:T(1,128)S(1)} %copy-done.11, s32[1,16]{1,0:T(1,128)S(1)} %copy-done.12, s32[1,48]{1,0:T(1,128)S(1)} %collective-permute-done.1.far, s32[1]{0:T(128)} %bitcast.core, ...), custom_call_target="tpu_custom_call" | custom-call | flops 201326592 | bytes 6291456 | tf_op jit(solution)/shard_map/forward/pallas_call | solution.py:145
  44.4 2.6 %tile_terms.1 = (bf16[32,32,384]{2,1,0:T(8,128)(2,1)S(1)}, bf16[32,32,384]{2,1,0:T(8,128)(2,1)}, bf16[32,32,384]{2,1,0:T(8,128)(2,1)S(1)}, bf16[32,32,384]{2,1,0:T(8,128)(2,1)S(1)}) custom-call(s32[1,16]{1,0:T(1,128)S(1)} %copy-done.10, s32[1,16]{1,0:T(1,128)S(1)} %copy-done.11, s32[1,16]{1,0:T(1,128)S(1)} %copy-done.12, ...), custom_call_target="tpu_custom_call" | custom-call | flops 201326592 | bytes 6291456 | tf_op jit(solution)/shard_map/tile_terms/pallas_call | solution.py:145
  46.9 2.3 %collective-permute-start.8 = (bf16[32,32,384]{2,1,0:T(8,128)(2,1)S(1)}, bf16[32,32,384]{2,1,0:T(8,128)(2,1)S(1)}, u32[]{:S(2)}, u32[]{:S(2)}) collective-permute-start(bf16[32,32,384]{2,1,0:T(8,128)(2,1)S(1)} %get-tuple-element.35), channel_id=1, source_target_pairs={{0,16},{16,0},{1,17},{17,1},{2,18},{18,2},{3,19},{19,3},{4,20},{20... | collective-permute-start | bytes 2359304 | tf_op jit(solution)/shard_map/cores/ppermute | solution.py:218
  49.2 2.0 %collective-permute-start.7 = (bf16[32,32,384]{2,1,0:T(8,128)(2,1)}, bf16[32,32,384]{2,1,0:T(8,128)(2,1)}, u32[]{:S(2)}, u32[]{:S(2)}) collective-permute-start(bf16[32,32,384]{2,1,0:T(8,128)(2,1)} %get-tuple-element.33), channel_id=1, source_target_pairs={{0,16},{16,0},{1,17},{17,1},{2,18},{18,2},{3,19},{19,3},{4,20},{20... | collective-permute-start | bytes 2359304 | tf_op jit(solution)/shard_map/cores/ppermute | solution.py:219
  51.3 1.1 add_convert_fusion.1
  52.4 2.5 %collective-permute-start.9 = (bf16[32,32,384]{2,1,0:T(8,128)(2,1)}, bf16[32,32,384]{2,1,0:T(8,128)(2,1)}, u32[]{:S(2)}, u32[]{:S(2)}) collective-permute-start(bf16[32,32,384]{2,1,0:T(8,128)(2,1)} %add_convert_fusion.1), channel_id=1, source_target_pairs={{0,8},{8,0},{16,792},{24,272},{256,264},{264,256},{272,24},{280,52... | collective-permute-start | bytes 2359304 | tf_op jit(solution)/shard_map/layers/ppermute | solution.py:221
  55.8 2.6 %back.1 = (bf16[4,8,4096]{2,1,0:T(8,128)(2,1)S(1)}, bf16[8,4096]{1,0:T(8,128)(2,1)S(1)}, bf16[8,4096]{1,0:T(8,128)(2,1)S(1)}, bf16[8,4096]{1,0:T(8,128)(2,1)S(1)}, bf16[8,4096]{1,0:T(8,128)(2,1)S(1)}) custom-call(s32[1,16]{1,0:T(1,128)S(1)} %copy-done.10, s32[1,16]{1,0:T(1,128)S(1)} %copy-done.11, s32[1,48]{1,0:T(1,128)S(1)} %collective-permute-done.1.far, ...), custom_call_target="tpu_custom_call" | custom-call | flops 134217728 | bytes 6291456 | tf_op jit(solution)/shard_map/back/pallas_call | solution.py:145
  58.4 3.0 %collective-permute-start.3 = (bf16[4,8,4096]{2,1,0:T(8,128)(2,1)S(1)}, bf16[4,8,4096]{2,1,0:T(8,128)(2,1)S(1)}, u32[]{:S(2)}, u32[]{:S(2)}) collective-permute-start(bf16[4,8,4096]{2,1,0:T(8,128)(2,1)S(1)} %get-tuple-element.26), channel_id=1, source_target_pairs={{0,1},{1,0},{2,3},{3,2},{4,5},{5,4},{6,7},{7,6},{8,9},{9,8},{10,11... | collective-permute-start | bytes 786440 | tf_op jit(solution)/shard_map/partials/ppermute | solution.py:211
  61.5 5.2 %collective-permute-done.3 = bf16[4,8,4096]{2,1,0:T(8,128)(2,1)S(1)} collective-permute-done((bf16[4,8,4096]{2,1,0:T(8,128)(2,1)S(1)}, bf16[4,8,4096]{2,1,0:T(8,128)(2,1)S(1)}, u32[]{:S(2)}, u32[]{:S(2)}) %collective-permute-start.3) | collective-permute-done | bytes 262176 | tf_op jit(solution)/shard_map/partials/ppermute | solution.py:211
  66.7 2.6 %add_convert_fusion = bf16[32,32,384]{2,1,0:T(8,128)(2,1)} fusion(bf16[32,32,384]{2,1,0:T(8,128)(2,1)} %collective-permute-done.9, bf16[32,32,384]{2,1,0:T(8,128)(2,1)} %collective-permute-done.7, bf16[32,32,384]{2,1,0:T(8,128)(2,1)S(1)} %copy-done.7), kind=kLoop, calls=%fused_computation.1 | loop fusion | flops 2359296 | bytes 3145728 | tf_op jit(solution)/shard_map/tile_sums/convert_element_type | solution.py:209
  69.3 21.1 %all-to-all-start.1 = ((bf16[32,32,384]{2,1,0:T(8,128)(2,1)}), bf16[32,32,384]{2,1,0:T(8,128)(2,1)S(1)}, u32[]{:S(2)}, u32[]{:S(2)}) async-start(bf16[32,32,384]{2,1,0:T(8,128)(2,1)} %add_convert_fusion), calls=%async_computation.1 | async-start | bytes 1572864 | tf_op jit(solution)/shard_map/tile_sums/all_to_all | solution.py:223
  90.5 2.4 %collective-permute-start.4 = (bf16[8,4096]{1,0:T(8,128)(2,1)S(1)}, bf16[8,4096]{1,0:T(8,128)(2,1)S(1)}, u32[]{:S(2)}, u32[]{:S(2)}) collective-permute-start(bf16[8,4096]{1,0:T(8,128)(2,1)S(1)} %get-tuple-element.36), channel_id=1, source_target_pairs={{0,2},{1,3},{2,4},{3,5},{4,6},{5,7},{6,0},{7,1},{8,10},{9,11},{10,... | collective-permute-start | bytes 196616 | tf_op jit(solution)/shard_map/partials/ppermute | solution.py:214
  92.9 4.2 %collective-permute-start.6 = (bf16[8,4096]{1,0:T(8,128)(2,1)S(1)}, bf16[8,4096]{1,0:T(8,128)(2,1)S(1)}, u32[]{:S(2)}, u32[]{:S(2)}) collective-permute-start(bf16[8,4096]{1,0:T(8,128)(2,1)S(1)} %get-tuple-element.37), channel_id=1, source_target_pairs={{0,4},{1,5},{2,6},{3,7},{4,0},{5,1},{6,2},{7,3},{8,12},{9,13},{10,... | collective-permute-start | bytes 196616 | tf_op jit(solution)/shard_map/partials/ppermute | solution.py:214
  97.1 3.8 %collective-permute-start.5 = (bf16[8,4096]{1,0:T(8,128)(2,1)S(1)}, bf16[8,4096]{1,0:T(8,128)(2,1)S(1)}, u32[]{:S(2)}, u32[]{:S(2)}) collective-permute-start(bf16[8,4096]{1,0:T(8,128)(2,1)S(1)} %get-tuple-element.38), channel_id=1, source_target_pairs={{0,6},{1,7},{2,0},{3,1},{4,2},{5,3},{6,4},{7,5},{8,14},{9,15},{10,... | collective-permute-start | bytes 196616 | tf_op jit(solution)/shard_map/partials/ppermute | solution.py:214
  101.0 2.0 %collective-permute-done.6 = bf16[8,4096]{1,0:T(8,128)(2,1)S(1)} collective-permute-done((bf16[8,4096]{1,0:T(8,128)(2,1)S(1)}, bf16[8,4096]{1,0:T(8,128)(2,1)S(1)}, u32[]{:S(2)}, u32[]{:S(2)}) %collective-permute-start.6) | collective-permute-done | bytes 65568 | tf_op jit(solution)/shard_map/partials/ppermute | solution.py:214
  103.0 2.7 %collective-permute-done.5 = bf16[8,4096]{1,0:T(8,128)(2,1)S(1)} collective-permute-done((bf16[8,4096]{1,0:T(8,128)(2,1)S(1)}, bf16[8,4096]{1,0:T(8,128)(2,1)S(1)}, u32[]{:S(2)}, u32[]{:S(2)}) %collective-permute-start.5) | collective-permute-done | bytes 65568 | tf_op jit(solution)/shard_map/partials/ppermute | solution.py:214
  106.3 7.7 %all-to-all-done.1 = bf16[32,32,384]{2,1,0:T(8,128)(2,1)S(1)} async-done(((bf16[32,32,384]{2,1,0:T(8,128)(2,1)}), bf16[32,32,384]{2,1,0:T(8,128)(2,1)S(1)}, u32[]{:S(2)}, u32[]{:S(2)}) %all-to-all-start.1) | async-done | bytes 786464 | tf_op jit(solution)/shard_map/tile_sums/all_to_all | solution.py:223
  (40 shorter events, 5.5 us)
Async XLA Ops:
  2.6 6.9 %copy-start = (bf16[1,16,128,128]{3,2,1,0:T(8,128)(2,1)S(1)}, bf16[1,16,128,128]{3,2,1,0:T(8,128)(2,1)}, u32[]{:S(2)}) copy-start(bf16[1,16,128,128]{3,2,1,0:T(8,128)(2,1)} %param.10) | copy-start | bytes 1572868
  2.6 7.0 %copy-start.10 = (s32[1,16]{1,0:T(1,128)S(1)}, s32[1,16]{1,0:T(1,128)}, u32[]{:S(2)}) copy-start(s32[1,16]{1,0:T(1,128)} %g_idx.5) | copy-start | bytes 196
  2.6 7.0 %copy-start.11 = (s32[1,16]{1,0:T(1,128)S(1)}, s32[1,16]{1,0:T(1,128)}, u32[]{:S(2)}) copy-start(s32[1,16]{1,0:T(1,128)} %u_idx.5) | copy-start | bytes 196
  2.6 7.0 %copy-start.12 = (s32[1,16]{1,0:T(1,128)S(1)}, s32[1,16]{1,0:T(1,128)}, u32[]{:S(2)}) copy-start(s32[1,16]{1,0:T(1,128)} %d_idx.3) | copy-start | bytes 196
  2.6 7.1 %copy-start.1 = (bf16[1,16,128,128]{3,2,1,0:T(8,128)(2,1)S(1)}, bf16[1,16,128,128]{3,2,1,0:T(8,128)(2,1)}, u32[]{:S(2)}) copy-start(bf16[1,16,128,128]{3,2,1,0:T(8,128)(2,1)} %param.11) | copy-start | bytes 1572868
  2.6 7.1 %copy-start.5 = (bf16[1,16,128,128]{3,2,1,0:T(8,128)(2,1)S(1)}, bf16[1,16,128,128]{3,2,1,0:T(8,128)(2,1)}, u32[]{:S(2)}) copy-start(bf16[1,16,128,128]{3,2,1,0:T(8,128)(2,1)} %param.12) | copy-start | bytes 1572868
  2.6 38.3 %all-to-all-start = ((bf16[8,8,8192]{2,1,0:T(8,128)(2,1)}), bf16[8,8,8192]{2,1,0:T(8,128)(2,1)S(1)}, u32[]{:S(2)}, u32[]{:S(2)}) async-start(bf16[8,8,8192]{2,1,0:T(8,128)(2,1)} %broadcast_in_dim.4), calls=%async_computation | async-start | bytes 2097152 | tf_op jit(solution)/shard_map/gather/all_to_all | solution.py:171
  9.8 15.2 %collective-permute-start = (bf16[3,8,128,128]{3,2,1,0:T(8,128)(2,1)S(1)}, bf16[3,8,128,128]{3,2,1,0:T(8,128)(2,1)S(1)}, u32[]{:S(2)}, u32[]{:S(2)}) collective-permute-start(bf16[3,8,128,128]{3,2,1,0:T(8,128)(2,1)S(1)} %pad_maximum_fusion), channel_id=1, source_target_pairs={{0,8},{8,0},{16,792},{24,272},{256,264},{264,256},{272,24},{280,52... | collective-permute-start | bytes 2359304 | tf_op jit(solution)/shard_map/weights/ppermute | solution.py:178
  15.0 10.0 %collective-permute-start.1 = (s32[1,48]{1,0:T(1,128)S(1)}, s32[1,48]{1,0:T(1,128)S(1)}, u32[]{:S(2)}, u32[]{:S(2)}) collective-permute-start(s32[1,48]{1,0:T(1,128)S(1)} %pad_add_fusion), channel_id=1, source_target_pairs={{0,8},{8,0},{1,9},{9,1},{2,10},{10,2},{3,11},{11,3},{4,12},{12,4},... | collective-permute-start | bytes 584 | tf_op jit(solution)/shard_map/weights/ppermute | solution.py:177
  25.0 15.0 %collective-permute-start.2 = (bf16[3,8,128,128]{3,2,1,0:T(8,128)(2,1)S(1)}, bf16[3,8,128,128]{3,2,1,0:T(8,128)(2,1)S(1)}, u32[]{:S(2)}, u32[]{:S(2)}) collective-permute-start(bf16[3,8,128,128]{3,2,1,0:T(8,128)(2,1)S(1)} %collective-permute-done.ra), channel_id=1, source_target_pairs={{0,16},{16,0},{1,17},{17,1},{2,18},{18,2},{3,19},{19,3},{4,20},{20... | collective-permute-start | bytes 2359304 | tf_op jit(solution)/shard_map/weights/ppermute | solution.py:180
  40.0 0.9 copy-start.2
  40.9 1.1 copy-start.3
  44.4 8.0 %copy-start.8 = (bf16[8,64,128]{2,1,0:T(8,128)(2,1)}, bf16[8,64,128]{2,1,0:T(8,128)(2,1)S(1)}, u32[]{:S(2)}) copy-start(bf16[8,64,128]{2,1,0:T(8,128)(2,1)S(1)} %get-tuple-element.24.dup) | copy-start | bytes 393220
  46.9 5.5 %copy-start.6 = (bf16[32,32,384]{2,1,0:T(8,128)(2,1)}, bf16[32,32,384]{2,1,0:T(8,128)(2,1)S(1)}, u32[]{:S(2)}) copy-start(bf16[32,32,384]{2,1,0:T(8,128)(2,1)S(1)} %get-tuple-element.32) | copy-start | bytes 2359300
  46.9 4.3 %collective-permute-start.8 = (bf16[32,32,384]{2,1,0:T(8,128)(2,1)S(1)}, bf16[32,32,384]{2,1,0:T(8,128)(2,1)S(1)}, u32[]{:S(2)}, u32[]{:S(2)}) collective-permute-start(bf16[32,32,384]{2,1,0:T(8,128)(2,1)S(1)} %get-tuple-element.35), channel_id=1, source_target_pairs={{0,16},{16,0},{1,17},{17,1},{2,18},{18,2},{3,19},{19,3},{4,20},{20... | collective-permute-start | bytes 2359304 | tf_op jit(solution)/shard_map/cores/ppermute | solution.py:218
  49.2 17.5 %collective-permute-start.7 = (bf16[32,32,384]{2,1,0:T(8,128)(2,1)}, bf16[32,32,384]{2,1,0:T(8,128)(2,1)}, u32[]{:S(2)}, u32[]{:S(2)}) collective-permute-start(bf16[32,32,384]{2,1,0:T(8,128)(2,1)} %get-tuple-element.33), channel_id=1, source_target_pairs={{0,16},{16,0},{1,17},{17,1},{2,18},{18,2},{3,19},{19,3},{4,20},{20... | collective-permute-start | bytes 2359304 | tf_op jit(solution)/shard_map/cores/ppermute | solution.py:219
  51.3 3.6 %copy-start.4 = (bf16[3,8,128,128]{3,2,1,0:T(8,128)(2,1)S(1)}, bf16[3,8,128,128]{3,2,1,0:T(8,128)(2,1)}, u32[]{:S(2)}) copy-start(bf16[3,8,128,128]{3,2,1,0:T(8,128)(2,1)} %copy-done.2) | copy-start | bytes 2359300
  52.4 14.3 %collective-permute-start.9 = (bf16[32,32,384]{2,1,0:T(8,128)(2,1)}, bf16[32,32,384]{2,1,0:T(8,128)(2,1)}, u32[]{:S(2)}, u32[]{:S(2)}) collective-permute-start(bf16[32,32,384]{2,1,0:T(8,128)(2,1)} %add_convert_fusion.1), channel_id=1, source_target_pairs={{0,8},{8,0},{16,792},{24,272},{256,264},{264,256},{272,24},{280,52... | collective-permute-start | bytes 2359304 | tf_op jit(solution)/shard_map/layers/ppermute | solution.py:221
  55.8 10.9 %copy-start.7 = (bf16[32,32,384]{2,1,0:T(8,128)(2,1)S(1)}, bf16[32,32,384]{2,1,0:T(8,128)(2,1)}, u32[]{:S(2)}) copy-start(bf16[32,32,384]{2,1,0:T(8,128)(2,1)} %copy-done.6) | copy-start | bytes 2359300
  58.4 8.3 %collective-permute-start.3 = (bf16[4,8,4096]{2,1,0:T(8,128)(2,1)S(1)}, bf16[4,8,4096]{2,1,0:T(8,128)(2,1)S(1)}, u32[]{:S(2)}, u32[]{:S(2)}) collective-permute-start(bf16[4,8,4096]{2,1,0:T(8,128)(2,1)S(1)} %get-tuple-element.26), channel_id=1, source_target_pairs={{0,1},{1,0},{2,3},{3,2},{4,5},{5,4},{6,7},{7,6},{8,9},{9,8},{10,11... | collective-permute-start | bytes 786440 | tf_op jit(solution)/shard_map/partials/ppermute | solution.py:211
  69.3 44.7 %all-to-all-start.1 = ((bf16[32,32,384]{2,1,0:T(8,128)(2,1)}), bf16[32,32,384]{2,1,0:T(8,128)(2,1)S(1)}, u32[]{:S(2)}, u32[]{:S(2)}) async-start(bf16[32,32,384]{2,1,0:T(8,128)(2,1)} %add_convert_fusion), calls=%async_computation.1 | async-start | bytes 1572864 | tf_op jit(solution)/shard_map/tile_sums/all_to_all | solution.py:223
  90.5 10.5 %collective-permute-start.4 = (bf16[8,4096]{1,0:T(8,128)(2,1)S(1)}, bf16[8,4096]{1,0:T(8,128)(2,1)S(1)}, u32[]{:S(2)}, u32[]{:S(2)}) collective-permute-start(bf16[8,4096]{1,0:T(8,128)(2,1)S(1)} %get-tuple-element.36), channel_id=1, source_target_pairs={{0,2},{1,3},{2,4},{3,5},{4,6},{5,7},{6,0},{7,1},{8,10},{9,11},{10,... | collective-permute-start | bytes 196616 | tf_op jit(solution)/shard_map/partials/ppermute | solution.py:214
  92.9 10.1 %collective-permute-start.6 = (bf16[8,4096]{1,0:T(8,128)(2,1)S(1)}, bf16[8,4096]{1,0:T(8,128)(2,1)S(1)}, u32[]{:S(2)}, u32[]{:S(2)}) collective-permute-start(bf16[8,4096]{1,0:T(8,128)(2,1)S(1)} %get-tuple-element.37), channel_id=1, source_target_pairs={{0,4},{1,5},{2,6},{3,7},{4,0},{5,1},{6,2},{7,3},{8,12},{9,13},{10,... | collective-permute-start | bytes 196616 | tf_op jit(solution)/shard_map/partials/ppermute | solution.py:214
  97.1 8.5 %collective-permute-start.5 = (bf16[8,4096]{1,0:T(8,128)(2,1)S(1)}, bf16[8,4096]{1,0:T(8,128)(2,1)S(1)}, u32[]{:S(2)}, u32[]{:S(2)}) collective-permute-start(bf16[8,4096]{1,0:T(8,128)(2,1)S(1)} %get-tuple-element.38), channel_id=1, source_target_pairs={{0,6},{1,7},{2,0},{3,1},{4,2},{5,3},{6,4},{7,5},{8,14},{9,15},{10,... | collective-permute-start | bytes 196616 | tf_op jit(solution)/shard_map/partials/ppermute | solution.py:214
  (1 other events, 0.9 us)

commit v6 on v5

--- a/solution.py
+++ b/solution.py
@@ -88,35 +88,45 @@
             keep[k][:, at] = acc[b, row(me), :].astype(BF16)
 
 
-def tile_terms(
-    g_idx, u_idx, d_idx, far, core, xa, dgate, dup, hid, own_mine, own_theirs, far_mine, far_theirs
-):
+def terms(side, index, core, xa, dgate, dup, hid, mine, theirs):
     blocks = xa.shape[1] // TILE // 2
     hidden = dgate.shape[0] // 2
     first = core[0] == 0
-    sets = (
-        (1, lambda n, s: far[0, n * CAP + s], far_mine, far_theirs),
-        (0, lambda n, s: (g_idx, u_idx, d_idx)[n][0, s], own_mine, own_theirs),
-    )
-    for side, index, mine, theirs in sets:
-        for slot in range(CAP):
-            outs = []
-            for n, grad in ((0, dgate), (1, dup)):
-                v = index(n, slot)
-                safe = jnp.maximum(v, 0)
-                val = dot(lanes(xa, safe >> 2), grad[side * hidden + (safe & 3)], (0, 0))
-                outs.append(jnp.where(v >= 0, val, 0.0))
-            v = index(2, slot)
+    for slot in range(CAP):
+        outs = []
+        for n, grad in ((0, dgate), (1, dup)):
+            v = index(n, slot)
             safe = jnp.maximum(v, 0)
-            val = dot(hid[side * hidden + (safe >> 5)], lanes(xa, blocks + (safe & 31)), (0, 0))
+            val = dot(lanes(xa, safe >> 2), grad[side * hidden + (safe & 3)], (0, 0))
             outs.append(jnp.where(v >= 0, val, 0.0))
-            for k, val in enumerate(outs):
-                for half in range(2):
-                    even = val[64 * half : 64 * half + 32]
-                    odd = val[64 * half + 32 : 64 * half + 64]
-                    at = (2 * slot + half, slice(None), slice(k * TILE, (k + 1) * TILE))
-                    mine[at] = jnp.where(first, even, odd).astype(BF16)
-                    theirs[at] = jnp.where(first, odd, even).astype(BF16)
+        v = index(2, slot)
+        safe = jnp.maximum(v, 0)
+        val = dot(hid[side * hidden + (safe >> 5)], lanes(xa, blocks + (safe & 31)), (0, 0))
+        outs.append(jnp.where(v >= 0, val, 0.0))
+        for k, val in enumerate(outs):
+            for half in range(2):
+                even = val[64 * half : 64 * half + 32]
+                odd = val[64 * half + 32 : 64 * half + 64]
+                at = (2 * slot + half, slice(None), slice(k * TILE, (k + 1) * TILE))
+                mine[at] = jnp.where(first, even, odd).astype(BF16)
+                theirs[at] = jnp.where(first, odd, even).astype(BF16)
+
+
+def far_terms(far, core, *refs):
+    terms(1, lambda n, s: far[0, n * CAP + s], core, *refs)
+
+
+def own_terms(g_idx, u_idx, d_idx, core, *refs):
+    terms(0, lambda n, s: (g_idx, u_idx, d_idx)[n][0, s], core, *refs)
+
+
+def total(*refs):
+    *parts, out = refs
+    for k in range(out.shape[0]):
+        val = parts[0][k].astype(F32)
+        for t in parts[1:]:
+            val += t[k].astype(F32)
+        out[k] = val.astype(BF16)
 
 
 def beside():
@@ -190,6 +200,19 @@
         (ra, rb),
         [pltpu.VMEM((hidden, rows, TILE), F32)] * 3,
     )
+    half_terms = (shape(pairs, 32, 3 * TILE),) * 2
+    far_mine, far_theirs = call(
+        far_terms, 3 * work // 2, half_terms, (far, core), (xa, dgate, dup, hid)
+    )
+    with jax.named_scope("cores"):
+        far_got = lax.ppermute(far_theirs, "c", SWAP)
+    own_mine, own_theirs = call(
+        own_terms, 3 * work // 2, half_terms, (*own, core), (xa, dgate, dup, hid)
+    )
+    own_mine, far_got = lax.optimization_barrier((own_mine, far_got))
+    with jax.named_scope("layers"):
+        (far_sum,) = call(total, 0, half_terms[:1], (), (far_mine, far_got))
+        near = lax.ppermute(far_sum, LAYERS, beside())
     give, *keep = call(
         back,
         2 * work,
@@ -199,28 +222,18 @@
         (ra, rb),
         [pltpu.VMEM((blocks, rows, TILE), F32)],
     )
-    own_mine, own_theirs, far_mine, far_theirs = call(
-        tile_terms,
-        3 * work,
-        (shape(pairs, 32, 3 * TILE),) * 4,
-        (*own, far, core),
-        (xa, dgate, dup, hid),
-    )
-    add = lambda *terms: sum(t.astype(F32) for t in terms).astype(BF16)
+    add = lambda *addends: sum(t.astype(F32) for t in addends).astype(BF16)
     with jax.named_scope("partials"):
         got = lax.ppermute(give, "x", [(i, i ^ 1) for i in range(line)])
         pair = [add(keep[k], got[k]) for k in range(line // 2)]
         ring = lambda d: [(i, (i + d) % line) for i in range(line)]
         came = [lax.ppermute(pair[k], "x", ring(2 * k)) for k in (1, 3, 2)]
-        input_sum = add(*[t.astype(F32) for t in (keep[0], got[0])], *came)
-    own_mine, got = lax.optimization_barrier((own_mine, got))
-    with jax.named_scope("cores"):
-        far_got = lax.ppermute(far_theirs, "c", SWAP)
+        input_sum = add(keep[0], got[0], *came)
+    with jax.named_scope("tile_sums"):
         own_got = lax.ppermute(own_theirs, "c", SWAP)
-    with jax.named_scope("layers"):
-        near = lax.ppermute(add(far_mine, far_got), LAYERS, beside())
-    with jax.named_scope("tile_sums"):
-        grads = lax.all_to_all(add(own_mine, own_got, near), ("zh", "y"), 0, 0, tiled=True)
+        own_mine, got = lax.optimization_barrier((own_mine, got))
+        (all_sum,) = call(total, 0, half_terms[:1], (), (own_mine, own_got, near))
+        grads = lax.all_to_all(all_sum, ("zh", "y"), 0, 0, tiled=True)
         sums = jnp.sum(grads.astype(F32), axis=0)
     return (input_sum, sums[None])
 

time: 115 us -> 118 us (1.026)
  Pallas kernels: 7.41 us -> 11.9 us
  other arithmetic: 6.23 us -> 2.51 us
  waiting for transfers between devices: 27.6 us -> 28.9 us
    pallas_call x3 -> x6, Pallas kernels: 7.41 us -> 11.9 us  [call(): pl.pallas_call(kernel, out_shape=out_shape, in_specs=[SMEM] * len(scalars...]
    convert_element_type x4 -> x2, other arithmetic: 4.45 us -> 0.72 us  [per_device(): add = lambda *addends: sum((t.astype(F32) for t in addends)).astype(BF16)]
    unnamed x26 -> x24, local copies, waits for them, and re-layouts: 3.01 us -> 4.05 us
  transfers between devices with their start and end apart: 12 -> 12, of which waited for: 6 -> 7; matrix products, arithmetic and copies ran while one was open for 2% -> 1% of each run, Pallas kernels for 2% -> 5%
where the time goes in v6:
time: 118 us; the launch traced here: 117 us
  starting transfers between devices  67.7 us (57%)
  waiting for transfers between devices  28.9 us (24%)
  Pallas kernels  11.9 us (10%)
  local copies, waits for them, and re-layouts  5.18 us (4%)
  other arithmetic  2.51 us (2%)
    all_to_all x1, starting transfers between devices, per_device(): grads = lax.all_to_all(all_sum, ('zh', 'y'), 0, 0, tiled=True)  20.3 us
    ppermute x1, starting transfers between devices, per_device(): rb = lax.ppermute(ra, 'c', SWAP)  13.1 us
    pallas_call x6, Pallas kernels, call(): pl.pallas_call(kernel, out_shape=out_shape, in_specs=[SMEM] * len(scalars...  11.9 us
    ppermute x3, starting transfers between devices, per_device(): came = [lax.ppermute(pair[k], 'x', ring(2 * k)) for k in (1, 3, 2)]  10.4 us
    all_to_all x1, waiting for transfers between devices, per_device(): grads = lax.all_to_all(all_sum, ('zh', 'y'), 0, 0, tiled=True)  8.15 us
    ppermute x1, waiting for transfers between devices, per_device(): far = lax.ppermute(index, 'zl', SWAP)  8.09 us
    all_to_all x1, starting transfers between devices, per_device(): xa = lax.all_to_all(send, 'x', 0, 0, tiled=True).reshape(rows, 2 * width)  6.9 us
    ppermute x1, waiting for transfers between devices, per_device(): got = lax.ppermute(give, 'x', [(i, i ^ 1) for i in range(line)])  5.19 us
  transfers between devices with their start and end apart: 12, of which 7 were waited for; matrix products, arithmetic and copies ran while one was open for 1% of the time, Pallas kernels for 5%

profile of v6, /device:TPU:16, one launch (start us, length us, event | category | flops | bytes accessed | tf_op | source)
XLA Modules:
  0.0 117.0 jit_solution(2261841444573032587)
XLA Ops:
  2.6 6.9 %all-to-all-start = ((bf16[8,8,8192]{2,1,0:T(8,128)(2,1)}), bf16[8,8,8192]{2,1,0:T(8,128)(2,1)S(1)}, u32[]{:S(2)}, u32[]{:S(2)}) async-start(bf16[8,8,8192]{2,1,0:T(8,128)(2,1)} %broadcast_in_dim.4), calls=%async_computation | async-start | bytes 2097152 | tf_op jit(solution)/shard_map/gather/all_to_all | solution.py:181
  9.8 5.2 %collective-permute-start = (bf16[3,8,128,128]{3,2,1,0:T(8,128)(2,1)S(1)}, bf16[3,8,128,128]{3,2,1,0:T(8,128)(2,1)S(1)}, u32[]{:S(2)}, u32[]{:S(2)}) collective-permute-start(bf16[3,8,128,128]{3,2,1,0:T(8,128)(2,1)S(1)} %pad_maximum_fusion), channel_id=1, source_target_pairs={{0,8},{8,0},{16,792},{24,272},{256,264},{264,256},{272,24},{280,52... | collective-permute-start | bytes 2359304 | tf_op jit(solution)/shard_map/weights/ppermute | solution.py:188
  15.0 1.9 %collective-permute-start.1 = (s32[1,48]{1,0:T(1,128)S(1)}, s32[1,48]{1,0:T(1,128)S(1)}, u32[]{:S(2)}, u32[]{:S(2)}) collective-permute-start(s32[1,48]{1,0:T(1,128)S(1)} %pad_add_fusion), channel_id=1, source_target_pairs={{0,8},{8,0},{1,9},{9,1},{2,10},{10,2},{3,11},{11,3},{4,12},{12,4},... | collective-permute-start | bytes 584 | tf_op jit(solution)/shard_map/weights/ppermute | solution.py:187
  16.9 8.1 %collective-permute-done.1.far = s32[1,48]{1,0:T(1,128)S(1)} collective-permute-done((s32[1,48]{1,0:T(1,128)S(1)}, s32[1,48]{1,0:T(1,128)S(1)}, u32[]{:S(2)}, u32[]{:S(2)}) %collective-permute-start.1) | collective-permute-done | bytes 224 | tf_op jit(solution)/shard_map/weights/ppermute | solution.py:187
  25.0 13.1 %collective-permute-start.2 = (bf16[3,8,128,128]{3,2,1,0:T(8,128)(2,1)S(1)}, bf16[3,8,128,128]{3,2,1,0:T(8,128)(2,1)S(1)}, u32[]{:S(2)}, u32[]{:S(2)}) collective-permute-start(bf16[3,8,128,128]{3,2,1,0:T(8,128)(2,1)S(1)} %collective-permute-done.ra), channel_id=1, source_target_pairs={{0,16},{16,0},{1,17},{17,1},{2,18},{18,2},{3,19},{19,3},{4,20},{20... | collective-permute-start | bytes 2359304 | tf_op jit(solution)/shard_map/weights/ppermute | solution.py:190
  38.1 1.9 %collective-permute-done.2.rb = bf16[3,8,128,128]{3,2,1,0:T(8,128)(2,1)S(1)} collective-permute-done((bf16[3,8,128,128]{3,2,1,0:T(8,128)(2,1)S(1)}, bf16[3,8,128,128]{3,2,1,0:T(8,128)(2,1)S(1)}, u32[]{:S(2)}, u32[]{:S(2)}) %collective-permute-start.2) | collective-permute-done | bytes 786464 | tf_op jit(solution)/shard_map/weights/ppermute | solution.py:190
  40.9 1.1 copy-done.3
  43.1 2.3 %forward.1 = (bf16[8,64,128]{2,1,0:T(8,128)(2,1)S(1)}, bf16[8,64,128]{2,1,0:T(8,128)(2,1)S(1)}, bf16[8,64,128]{2,1,0:T(8,128)(2,1)S(1)}) custom-call(s32[1,16]{1,0:T(1,128)S(1)} %copy-done.9, s32[1,16]{1,0:T(1,128)S(1)} %copy-done.10, s32[1,16]{1,0:T(1,128)S(1)} %copy-done.11, s32[1,48]{1,0:T(1,128)S(1)} %collective-permute-done.1.far, s32[1]{0:T(128)} %bitcast.core, ...), custom_call_target="tpu_custom_call" | custom-call | flops 201326592 | bytes 6291456 | tf_op jit(solution)/shard_map/forward/pallas_call | solution.py:155
  45.4 1.2 %far_terms.1 = (bf16[32,32,384]{2,1,0:T(8,128)(2,1)S(1)}, bf16[32,32,384]{2,1,0:T(8,128)(2,1)S(1)}) custom-call(s32[1,48]{1,0:T(1,128)S(1)} %collective-permute-done.1.far, s32[1]{0:T(128)} %bitcast.core, bf16[64,8192]{1,0:T(8,128)(2,1)S(1)} %bitcast.28, bf16[8,64,128]{2,1,0:T(8,128)(2,1)S(1)} %get-tuple-element.25.dgate.refs_1_, ...), custom_call_target="tpu_custom_call" | custom-call | flops 100663296 | bytes 6291456 | tf_op jit(solution)/shard_map/far_terms/pallas_call | solution.py:155
  46.6 2.3 %collective-permute-start.7 = (bf16[32,32,384]{2,1,0:T(8,128)(2,1)S(1)}, bf16[32,32,384]{2,1,0:T(8,128)(2,1)S(1)}, u32[]{:S(2)}, u32[]{:S(2)}) collective-permute-start(bf16[32,32,384]{2,1,0:T(8,128)(2,1)S(1)} %get-tuple-element.34), channel_id=1, source_target_pairs={{0,16},{16,0},{1,17},{17,1},{2,18},{18,2},{3,19},{19,3},{4,20},{20... | collective-permute-start | bytes 2359304 | tf_op jit(solution)/shard_map/cores/ppermute | solution.py:208
  48.9 2.1 %own_terms.1 = (bf16[32,32,384]{2,1,0:T(8,128)(2,1)S(1)}, bf16[32,32,384]{2,1,0:T(8,128)(2,1)}) custom-call(s32[1,16]{1,0:T(1,128)S(1)} %copy-done.9, s32[1,16]{1,0:T(1,128)S(1)} %copy-done.10, s32[1,16]{1,0:T(1,128)S(1)} %copy-done.11, s32[1]{0:T(128)} %bitcast.core, bf16[64,8192]{1,0:T(8,128)(2,1)S(1)} %bitcast.29, ...), custom_call_target="tpu_custom_call" | custom-call | flops 100663296 | bytes 6291456 | tf_op jit(solution)/shard_map/own_terms/pallas_call | solution.py:155
  51.9 2.0 %collective-permute-start.8 = (bf16[32,32,384]{2,1,0:T(8,128)(2,1)}, bf16[32,32,384]{2,1,0:T(8,128)(2,1)}, u32[]{:S(2)}, u32[]{:S(2)}) collective-permute-start(bf16[32,32,384]{2,1,0:T(8,128)(2,1)} %get-tuple-element.37), channel_id=1, source_target_pairs={{0,16},{16,0},{1,17},{17,1},{2,18},{18,2},{3,19},{19,3},{4,20},{20... | collective-permute-start | bytes 2359304 | tf_op jit(solution)/shard_map/tile_sums/ppermute | solution.py:233
  55.1 2.5 %collective-permute-start.9 = (bf16[32,32,384]{2,1,0:T(8,128)(2,1)}, bf16[32,32,384]{2,1,0:T(8,128)(2,1)}, u32[]{:S(2)}, u32[]{:S(2)}) collective-permute-start(bf16[32,32,384]{2,1,0:T(8,128)(2,1)} %total.2), channel_id=1, source_target_pairs={{0,8},{8,0},{16,792},{24,272},{256,264},{264,256},{272,24},{280,52... | collective-permute-start | bytes 2359304 | tf_op jit(solution)/shard_map/layers/ppermute | solution.py:215
  57.6 2.6 %back.1 = (bf16[4,8,4096]{2,1,0:T(8,128)(2,1)S(1)}, bf16[8,4096]{1,0:T(8,128)(2,1)S(1)}, bf16[8,4096]{1,0:T(8,128)(2,1)S(1)}, bf16[8,4096]{1,0:T(8,128)(2,1)S(1)}, bf16[8,4096]{1,0:T(8,128)(2,1)S(1)}) custom-call(s32[1,16]{1,0:T(1,128)S(1)} %copy-done.9, s32[1,16]{1,0:T(1,128)S(1)} %copy-done.10, s32[1,48]{1,0:T(1,128)S(1)} %collective-permute-done.1.far, ...), custom_call_target="tpu_custom_call" | custom-call | flops 134217728 | bytes 6291456 | tf_op jit(solution)/shard_map/back/pallas_call | solution.py:155
  60.2 3.1 %collective-permute-start.3 = (bf16[4,8,4096]{2,1,0:T(8,128)(2,1)S(1)}, bf16[4,8,4096]{2,1,0:T(8,128)(2,1)S(1)}, u32[]{:S(2)}, u32[]{:S(2)}) collective-permute-start(bf16[4,8,4096]{2,1,0:T(8,128)(2,1)S(1)} %get-tuple-element.28), channel_id=1, source_target_pairs={{0,1},{1,0},{2,3},{3,2},{4,5},{5,4},{6,7},{7,6},{8,9},{9,8},{10,11... | collective-permute-start | bytes 786440 | tf_op jit(solution)/shard_map/partials/ppermute | solution.py:227
  63.2 5.2 %collective-permute-done.3 = bf16[4,8,4096]{2,1,0:T(8,128)(2,1)S(1)} collective-permute-done((bf16[4,8,4096]{2,1,0:T(8,128)(2,1)S(1)}, bf16[4,8,4096]{2,1,0:T(8,128)(2,1)S(1)}, u32[]{:S(2)}, u32[]{:S(2)}) %collective-permute-start.3) | collective-permute-done | bytes 262176 | tf_op jit(solution)/shard_map/partials/ppermute | solution.py:227
  69.3 2.6 %total.3 = bf16[32,32,384]{2,1,0:T(8,128)(2,1)} custom-call(bf16[32,32,384]{2,1,0:T(8,128)(2,1)S(1)} %copy-done.8, bf16[32,32,384]{2,1,0:T(8,128)(2,1)} %collective-permute-done.8.refs_1_, bf16[32,32,384]{2,1,0:T(8,128)(2,1)} %collective-permute-done.9.refs_2_), custom_call_target="tpu_custom_call" | custom-call | bytes 6291456 | tf_op jit(solution)/shard_map/tile_sums/total/pallas_call | solution.py:155
  71.9 20.3 %all-to-all-start.1 = ((bf16[32,32,384]{2,1,0:T(8,128)(2,1)}), bf16[32,32,384]{2,1,0:T(8,128)(2,1)S(1)}, u32[]{:S(2)}, u32[]{:S(2)}) async-start(bf16[32,32,384]{2,1,0:T(8,128)(2,1)} %total.3), calls=%async_computation.1 | async-start | bytes 1572864 | tf_op jit(solution)/shard_map/tile_sums/all_to_all | solution.py:236
  92.3 2.4 %collective-permute-start.4 = (bf16[8,4096]{1,0:T(8,128)(2,1)S(1)}, bf16[8,4096]{1,0:T(8,128)(2,1)S(1)}, u32[]{:S(2)}, u32[]{:S(2)}) collective-permute-start(bf16[8,4096]{1,0:T(8,128)(2,1)S(1)} %get-tuple-element.40), channel_id=1, source_target_pairs={{0,2},{1,3},{2,4},{3,5},{4,6},{5,7},{6,0},{7,1},{8,10},{9,11},{10,... | collective-permute-start | bytes 196616 | tf_op jit(solution)/shard_map/partials/ppermute | solution.py:230
  94.7 4.2 %collective-permute-start.6 = (bf16[8,4096]{1,0:T(8,128)(2,1)S(1)}, bf16[8,4096]{1,0:T(8,128)(2,1)S(1)}, u32[]{:S(2)}, u32[]{:S(2)}) collective-permute-start(bf16[8,4096]{1,0:T(8,128)(2,1)S(1)} %get-tuple-element.41), channel_id=1, source_target_pairs={{0,4},{1,5},{2,6},{3,7},{4,0},{5,1},{6,2},{7,3},{8,12},{9,13},{10,... | collective-permute-start | bytes 196616 | tf_op jit(solution)/shard_map/partials/ppermute | solution.py:230
  98.9 3.8 %collective-permute-start.5 = (bf16[8,4096]{1,0:T(8,128)(2,1)S(1)}, bf16[8,4096]{1,0:T(8,128)(2,1)S(1)}, u32[]{:S(2)}, u32[]{:S(2)}) collective-permute-start(bf16[8,4096]{1,0:T(8,128)(2,1)S(1)} %get-tuple-element.42), channel_id=1, source_target_pairs={{0,6},{1,7},{2,0},{3,1},{4,2},{5,3},{6,4},{7,5},{8,14},{9,15},{10,... | collective-permute-start | bytes 196616 | tf_op jit(solution)/shard_map/partials/ppermute | solution.py:230
  102.7 2.1 %collective-permute-done.6 = bf16[8,4096]{1,0:T(8,128)(2,1)S(1)} collective-permute-done((bf16[8,4096]{1,0:T(8,128)(2,1)S(1)}, bf16[8,4096]{1,0:T(8,128)(2,1)S(1)}, u32[]{:S(2)}, u32[]{:S(2)}) %collective-permute-start.6) | collective-permute-done | bytes 65568 | tf_op jit(solution)/shard_map/partials/ppermute | solution.py:230
  104.8 2.6 %collective-permute-done.5 = bf16[8,4096]{1,0:T(8,128)(2,1)S(1)} collective-permute-done((bf16[8,4096]{1,0:T(8,128)(2,1)S(1)}, bf16[8,4096]{1,0:T(8,128)(2,1)S(1)}, u32[]{:S(2)}, u32[]{:S(2)}) %collective-permute-start.5) | collective-permute-done | bytes 65568 | tf_op jit(solution)/shard_map/partials/ppermute | solution.py:230
  108.1 8.1 %all-to-all-done.1 = bf16[32,32,384]{2,1,0:T(8,128)(2,1)S(1)} async-done(((bf16[32,32,384]{2,1,0:T(8,128)(2,1)}), bf16[32,32,384]{2,1,0:T(8,128)(2,1)S(1)}, u32[]{:S(2)}, u32[]{:S(2)}) %all-to-all-start.1) | async-done | bytes 786464 | tf_op jit(solution)/shard_map/tile_sums/all_to_all | solution.py:236
  (39 shorter events, 8.5 us)
Async XLA Ops:
  2.6 6.9 %copy-start = (bf16[1,16,128,128]{3,2,1,0:T(8,128)(2,1)S(1)}, bf16[1,16,128,128]{3,2,1,0:T(8,128)(2,1)}, u32[]{:S(2)}) copy-start(bf16[1,16,128,128]{3,2,1,0:T(8,128)(2,1)} %param.10) | copy-start | bytes 1572868
  2.6 7.0 %copy-start.9 = (s32[1,16]{1,0:T(1,128)S(1)}, s32[1,16]{1,0:T(1,128)}, u32[]{:S(2)}) copy-start(s32[1,16]{1,0:T(1,128)} %g_idx.5) | copy-start | bytes 196
  2.6 7.0 %copy-start.10 = (s32[1,16]{1,0:T(1,128)S(1)}, s32[1,16]{1,0:T(1,128)}, u32[]{:S(2)}) copy-start(s32[1,16]{1,0:T(1,128)} %u_idx.5) | copy-start | bytes 196
  2.6 7.0 %copy-start.11 = (s32[1,16]{1,0:T(1,128)S(1)}, s32[1,16]{1,0:T(1,128)}, u32[]{:S(2)}) copy-start(s32[1,16]{1,0:T(1,128)} %d_idx.3) | copy-start | bytes 196
  2.6 7.1 %copy-start.1 = (bf16[1,16,128,128]{3,2,1,0:T(8,128)(2,1)S(1)}, bf16[1,16,128,128]{3,2,1,0:T(8,128)(2,1)}, u32[]{:S(2)}) copy-start(bf16[1,16,128,128]{3,2,1,0:T(8,128)(2,1)} %param.11) | copy-start | bytes 1572868
  2.6 7.1 %copy-start.5 = (bf16[1,16,128,128]{3,2,1,0:T(8,128)(2,1)S(1)}, bf16[1,16,128,128]{3,2,1,0:T(8,128)(2,1)}, u32[]{:S(2)}) copy-start(bf16[1,16,128,128]{3,2,1,0:T(8,128)(2,1)} %param.12) | copy-start | bytes 1572868
  2.6 38.3 %all-to-all-start = ((bf16[8,8,8192]{2,1,0:T(8,128)(2,1)}), bf16[8,8,8192]{2,1,0:T(8,128)(2,1)S(1)}, u32[]{:S(2)}, u32[]{:S(2)}) async-start(bf16[8,8,8192]{2,1,0:T(8,128)(2,1)} %broadcast_in_dim.4), calls=%async_computation | async-start | bytes 2097152 | tf_op jit(solution)/shard_map/gather/all_to_all | solution.py:181
  9.8 15.2 %collective-permute-start = (bf16[3,8,128,128]{3,2,1,0:T(8,128)(2,1)S(1)}, bf16[3,8,128,128]{3,2,1,0:T(8,128)(2,1)S(1)}, u32[]{:S(2)}, u32[]{:S(2)}) collective-permute-start(bf16[3,8,128,128]{3,2,1,0:T(8,128)(2,1)S(1)} %pad_maximum_fusion), channel_id=1, source_target_pairs={{0,8},{8,0},{16,792},{24,272},{256,264},{264,256},{272,24},{280,52... | collective-permute-start | bytes 2359304 | tf_op jit(solution)/shard_map/weights/ppermute | solution.py:188
  15.0 10.0 %collective-permute-start.1 = (s32[1,48]{1,0:T(1,128)S(1)}, s32[1,48]{1,0:T(1,128)S(1)}, u32[]{:S(2)}, u32[]{:S(2)}) collective-permute-start(s32[1,48]{1,0:T(1,128)S(1)} %pad_add_fusion), channel_id=1, source_target_pairs={{0,8},{8,0},{1,9},{9,1},{2,10},{10,2},{3,11},{11,3},{4,12},{12,4},... | collective-permute-start | bytes 584 | tf_op jit(solution)/shard_map/weights/ppermute | solution.py:187
  25.0 15.0 %collective-permute-start.2 = (bf16[3,8,128,128]{3,2,1,0:T(8,128)(2,1)S(1)}, bf16[3,8,128,128]{3,2,1,0:T(8,128)(2,1)S(1)}, u32[]{:S(2)}, u32[]{:S(2)}) collective-permute-start(bf16[3,8,128,128]{3,2,1,0:T(8,128)(2,1)S(1)} %collective-permute-done.ra), channel_id=1, source_target_pairs={{0,16},{16,0},{1,17},{17,1},{2,18},{18,2},{3,19},{19,3},{4,20},{20... | collective-permute-start | bytes 2359304 | tf_op jit(solution)/shard_map/weights/ppermute | solution.py:190
  40.0 0.9 copy-start.2
  40.9 1.1 copy-start.3
  42.1 1.0 copy-start.6
  46.6 7.3 %collective-permute-start.7 = (bf16[32,32,384]{2,1,0:T(8,128)(2,1)S(1)}, bf16[32,32,384]{2,1,0:T(8,128)(2,1)S(1)}, u32[]{:S(2)}, u32[]{:S(2)}) collective-permute-start(bf16[32,32,384]{2,1,0:T(8,128)(2,1)S(1)} %get-tuple-element.34), channel_id=1, source_target_pairs={{0,16},{16,0},{1,17},{17,1},{2,18},{18,2},{3,19},{19,3},{4,20},{20... | collective-permute-start | bytes 2359304 | tf_op jit(solution)/shard_map/cores/ppermute | solution.py:208
  51.0 0.9 copy-start.7
  51.9 16.5 %collective-permute-start.8 = (bf16[32,32,384]{2,1,0:T(8,128)(2,1)}, bf16[32,32,384]{2,1,0:T(8,128)(2,1)}, u32[]{:S(2)}, u32[]{:S(2)}) collective-permute-start(bf16[32,32,384]{2,1,0:T(8,128)(2,1)} %get-tuple-element.37), channel_id=1, source_target_pairs={{0,16},{16,0},{1,17},{17,1},{2,18},{18,2},{3,19},{19,3},{4,20},{20... | collective-permute-start | bytes 2359304 | tf_op jit(solution)/shard_map/tile_sums/ppermute | solution.py:233
  54.0 3.6 %copy-start.4 = (bf16[3,8,128,128]{3,2,1,0:T(8,128)(2,1)S(1)}, bf16[3,8,128,128]{3,2,1,0:T(8,128)(2,1)}, u32[]{:S(2)}) copy-start(bf16[3,8,128,128]{3,2,1,0:T(8,128)(2,1)} %copy-done.2) | copy-start | bytes 2359300
  55.1 14.2 %collective-permute-start.9 = (bf16[32,32,384]{2,1,0:T(8,128)(2,1)}, bf16[32,32,384]{2,1,0:T(8,128)(2,1)}, u32[]{:S(2)}, u32[]{:S(2)}) collective-permute-start(bf16[32,32,384]{2,1,0:T(8,128)(2,1)} %total.2), channel_id=1, source_target_pairs={{0,8},{8,0},{16,792},{24,272},{256,264},{264,256},{272,24},{280,52... | collective-permute-start | bytes 2359304 | tf_op jit(solution)/shard_map/layers/ppermute | solution.py:215
  57.6 11.7 %copy-start.8 = (bf16[32,32,384]{2,1,0:T(8,128)(2,1)S(1)}, bf16[32,32,384]{2,1,0:T(8,128)(2,1)}, u32[]{:S(2)}) copy-start(bf16[32,32,384]{2,1,0:T(8,128)(2,1)} %copy-done.7) | copy-start | bytes 2359300
  60.2 8.3 %collective-permute-start.3 = (bf16[4,8,4096]{2,1,0:T(8,128)(2,1)S(1)}, bf16[4,8,4096]{2,1,0:T(8,128)(2,1)S(1)}, u32[]{:S(2)}, u32[]{:S(2)}) collective-permute-start(bf16[4,8,4096]{2,1,0:T(8,128)(2,1)S(1)} %get-tuple-element.28), channel_id=1, source_target_pairs={{0,1},{1,0},{2,3},{3,2},{4,5},{5,4},{6,7},{7,6},{8,9},{9,8},{10,11... | collective-permute-start | bytes 786440 | tf_op jit(solution)/shard_map/partials/ppermute | solution.py:227
  71.9 44.4 %all-to-all-start.1 = ((bf16[32,32,384]{2,1,0:T(8,128)(2,1)}), bf16[32,32,384]{2,1,0:T(8,128)(2,1)S(1)}, u32[]{:S(2)}, u32[]{:S(2)}) async-start(bf16[32,32,384]{2,1,0:T(8,128)(2,1)} %total.3), calls=%async_computation.1 | async-start | bytes 1572864 | tf_op jit(solution)/shard_map/tile_sums/all_to_all | solution.py:236
  92.3 10.5 %collective-permute-start.4 = (bf16[8,4096]{1,0:T(8,128)(2,1)S(1)}, bf16[8,4096]{1,0:T(8,128)(2,1)S(1)}, u32[]{:S(2)}, u32[]{:S(2)}) collective-permute-start(bf16[8,4096]{1,0:T(8,128)(2,1)S(1)} %get-tuple-element.40), channel_id=1, source_target_pairs={{0,2},{1,3},{2,4},{3,5},{4,6},{5,7},{6,0},{7,1},{8,10},{9,11},{10,... | collective-permute-start | bytes 196616 | tf_op jit(solution)/shard_map/partials/ppermute | solution.py:230
  94.7 10.2 %collective-permute-start.6 = (bf16[8,4096]{1,0:T(8,128)(2,1)S(1)}, bf16[8,4096]{1,0:T(8,128)(2,1)S(1)}, u32[]{:S(2)}, u32[]{:S(2)}) collective-permute-start(bf16[8,4096]{1,0:T(8,128)(2,1)S(1)} %get-tuple-element.41), channel_id=1, source_target_pairs={{0,4},{1,5},{2,6},{3,7},{4,0},{5,1},{6,2},{7,3},{8,12},{9,13},{10,... | collective-permute-start | bytes 196616 | tf_op jit(solution)/shard_map/partials/ppermute | solution.py:230
  98.9 8.5 %collective-permute-start.5 = (bf16[8,4096]{1,0:T(8,128)(2,1)S(1)}, bf16[8,4096]{1,0:T(8,128)(2,1)S(1)}, u32[]{:S(2)}, u32[]{:S(2)}) collective-permute-start(bf16[8,4096]{1,0:T(8,128)(2,1)S(1)} %get-tuple-element.42), channel_id=1, source_target_pairs={{0,6},{1,7},{2,0},{3,1},{4,2},{5,3},{6,4},{7,5},{8,14},{9,15},{10,... | collective-permute-start | bytes 196616 | tf_op jit(solution)/shard_map/partials/ppermute | solution.py:230

commit v7 on v5

--- a/solution.py
+++ b/solution.py
@@ -18,6 +18,19 @@
 
 def dot(left, right, on):
     return lax.dot_general(left, right, ((on[:1], on[1:]), ((), ())), preferred_element_type=F32)
+
+
+def spread(tokens, grad_out, out, sems):
+    width = tokens.shape[1]
+    copies = [
+        pltpu.make_async_copy(t, out.at[n, :, pl.ds(k * width, width)], sems.at[n, k])
+        for n in range(out.shape[0])
+        for k, t in enumerate((tokens, grad_out))
+    ]
+    for copy in copies:
+        copy.start()
+    for copy in copies:
+        copy.wait()
 
 
 def fetch(halves, held, sems):
@@ -166,8 +179,14 @@
     at_core = lax.axis_index("c").astype(jnp.int32)
     core = at_core.reshape(1)
     with jax.named_scope("gather"):
-        both = jnp.concatenate([tokens, grad_out], axis=1)
-        send = jnp.broadcast_to(both[None], (line, here, 2 * width))
+        send = pl.pallas_call(
+            spread,
+            out_shape=jax.ShapeDtypeStruct((line, here, 2 * width), BF16),
+            in_specs=[pl.BlockSpec(memory_space=pl.ANY)] * 2,
+            out_specs=pl.BlockSpec(memory_space=pl.ANY),
+            scratch_shapes=[pltpu.SemaphoreType.DMA((line, 2))],
+            name="spread",
+        )(tokens, grad_out)
         xa = lax.all_to_all(send, "x", 0, 0, tiled=True).reshape(rows, 2 * width)
     with jax.named_scope("weights"):
         part_of = lambda w: lax.dynamic_slice_in_dim(w, at_core * (slots // 2), slots // 2)
@@ -209,19 +228,20 @@
     add = lambda *terms: sum(t.astype(F32) for t in terms).astype(BF16)
     with jax.named_scope("partials"):
         got = lax.ppermute(give, "x", [(i, i ^ 1) for i in range(line)])
-        pair = [add(keep[k], got[k]) for k in range(line // 2)]
-        ring = lambda d: [(i, (i + d) % line) for i in range(line)]
-        came = [lax.ppermute(pair[k], "x", ring(2 * k)) for k in (1, 3, 2)]
-        input_sum = add(*[t.astype(F32) for t in (keep[0], got[0])], *came)
-    own_mine, got = lax.optimization_barrier((own_mine, got))
     with jax.named_scope("cores"):
         far_got = lax.ppermute(far_theirs, "c", SWAP)
         own_got = lax.ppermute(own_theirs, "c", SWAP)
     with jax.named_scope("layers"):
         near = lax.ppermute(add(far_mine, far_got), LAYERS, beside())
     with jax.named_scope("tile_sums"):
-        grads = lax.all_to_all(add(own_mine, own_got, near), ("zh", "y"), 0, 0, tiled=True)
+        own_sum, got = lax.optimization_barrier((add(own_mine, own_got), got))
+        grads = lax.all_to_all(add(own_sum, near), ("zh", "y"), 0, 0, tiled=True)
         sums = jnp.sum(grads.astype(F32), axis=0)
+    with jax.named_scope("partials"):
+        pair = [add(keep[k], got[k]) for k in range(line // 2)]
+        ring = lambda d: [(i, (i + d) % line) for i in range(line)]
+        came = [lax.ppermute(pair[k], "x", ring(2 * k)) for k in (1, 3, 2)]
+        input_sum = add(*[t.astype(F32) for t in (keep[0], got[0])], *came)
     return (input_sum, sums[None])
 
 

time: 115 us -> 146 us (1.27)
  Pallas kernels: 7.41 us -> 40.5 us
    pallas_call x0 -> x1, Pallas kernels: none -> 33 us  [per_device(): pl.pallas_call(spread, out_shape=jax.ShapeDtypeStruct((line, here, 2 * wi...]
    convert_element_type x4 -> x5, other arithmetic: 4.45 us -> 5.37 us  [per_device(): add = lambda *terms: sum((t.astype(F32) for t in terms)).astype(BF16)]
where the time goes in v7:
time: 146 us; the launch traced here: 145 us
  starting transfers between devices  68.3 us (47%)
  Pallas kernels  40.5 us (28%)
  waiting for transfers between devices  26.3 us (18%)
  other arithmetic  6.27 us (4%)
  local copies, waits for them, and re-layouts  3.05 us (2%)
    pallas_call x1, Pallas kernels, per_device(): pl.pallas_call(spread, out_shape=jax.ShapeDtypeStruct((line, here, 2 * wi...  33 us
    all_to_all x1, starting transfers between devices, per_device(): grads = lax.all_to_all(add(own_sum, near), ('zh', 'y'), 0, 0, tiled=True)  21.1 us
    ppermute x1, starting transfers between devices, per_device(): rb = lax.ppermute(ra, 'c', SWAP)  12.9 us
    ppermute x3, starting transfers between devices, per_device(): came = [lax.ppermute(pair[k], 'x', ring(2 * k)) for k in (1, 3, 2)]  10.5 us
    ppermute x1, waiting for transfers between devices, per_device(): far = lax.ppermute(index, 'zl', SWAP)  8.09 us
    all_to_all x1, waiting for transfers between devices, per_device(): grads = lax.all_to_all(add(own_sum, near), ('zh', 'y'), 0, 0, tiled=True)  7.71 us
    pallas_call x3, Pallas kernels, call(): pl.pallas_call(kernel, out_shape=out_shape, in_specs=[SMEM] * len(scalars...  7.46 us
    all_to_all x1, starting transfers between devices, per_device(): xa = lax.all_to_all(send, 'x', 0, 0, tiled=True).reshape(rows, 2 * width)  6.9 us
  transfers between devices with their start and end apart: 12, of which 6 were waited for; matrix products, arithmetic and copies ran while one was open for 2% of the time, Pallas kernels for 2%

profile of v7, /device:TPU:16, one launch (start us, length us, event | category | flops | bytes accessed | tf_op | source)
XLA Modules:
  0.0 145.4 jit_solution(676747315779427431)
XLA Ops:
  0.6 33.0 %spread.1 = bf16[8,8,8192]{2,1,0:T(8,128)(2,1)} custom-call(bf16[8,4096]{1,0:T(8,128)(2,1)} %tokens.1, bf16[8,4096]{1,0:T(8,128)(2,1)} %grad_out.1), custom_call_target="tpu_custom_call" | custom-call | tf_op jit(solution)/shard_map/gather/spread/pallas_call | solution.py:182
  33.7 6.9 %all-to-all-start = ((bf16[8,8,8192]{2,1,0:T(8,128)(2,1)}), bf16[8,8,8192]{2,1,0:T(8,128)(2,1)S(1)}, u32[]{:S(2)}, u32[]{:S(2)}) async-start(bf16[8,8,8192]{2,1,0:T(8,128)(2,1)} %spread.1), calls=%async_computation | async-start | bytes 2097152 | tf_op jit(solution)/shard_map/gather/all_to_all | solution.py:190
  40.9 5.2 %collective-permute-start = (bf16[3,8,128,128]{3,2,1,0:T(8,128)(2,1)S(1)}, bf16[3,8,128,128]{3,2,1,0:T(8,128)(2,1)S(1)}, u32[]{:S(2)}, u32[]{:S(2)}) collective-permute-start(bf16[3,8,128,128]{3,2,1,0:T(8,128)(2,1)S(1)} %pad_maximum_fusion), channel_id=1, source_target_pairs={{0,8},{8,0},{16,792},{24,272},{256,264},{264,256},{272,24},{280,52... | collective-permute-start | bytes 2359304 | tf_op jit(solution)/shard_map/weights/ppermute | solution.py:197
  46.1 1.9 %collective-permute-start.1 = (s32[1,48]{1,0:T(1,128)S(1)}, s32[1,48]{1,0:T(1,128)S(1)}, u32[]{:S(2)}, u32[]{:S(2)}) collective-permute-start(s32[1,48]{1,0:T(1,128)S(1)} %pad_add_fusion), channel_id=1, source_target_pairs={{0,8},{8,0},{1,9},{9,1},{2,10},{10,2},{3,11},{11,3},{4,12},{12,4},... | collective-permute-start | bytes 584 | tf_op jit(solution)/shard_map/weights/ppermute | solution.py:196
  48.0 8.1 %collective-permute-done.1.far = s32[1,48]{1,0:T(1,128)S(1)} collective-permute-done((s32[1,48]{1,0:T(1,128)S(1)}, s32[1,48]{1,0:T(1,128)S(1)}, u32[]{:S(2)}, u32[]{:S(2)}) %collective-permute-start.1) | collective-permute-done | bytes 224 | tf_op jit(solution)/shard_map/weights/ppermute | solution.py:196
  56.1 12.9 %collective-permute-start.2 = (bf16[3,8,128,128]{3,2,1,0:T(8,128)(2,1)S(1)}, bf16[3,8,128,128]{3,2,1,0:T(8,128)(2,1)S(1)}, u32[]{:S(2)}, u32[]{:S(2)}) collective-permute-start(bf16[3,8,128,128]{3,2,1,0:T(8,128)(2,1)S(1)} %collective-permute-done.ra), channel_id=1, source_target_pairs={{0,16},{16,0},{1,17},{17,1},{2,18},{18,2},{3,19},{19,3},{4,20},{20... | collective-permute-start | bytes 2359304 | tf_op jit(solution)/shard_map/weights/ppermute | solution.py:199
  69.1 1.9 %collective-permute-done.2.rb = bf16[3,8,128,128]{3,2,1,0:T(8,128)(2,1)S(1)} collective-permute-done((bf16[3,8,128,128]{3,2,1,0:T(8,128)(2,1)S(1)}, bf16[3,8,128,128]{3,2,1,0:T(8,128)(2,1)S(1)}, u32[]{:S(2)}, u32[]{:S(2)}) %collective-permute-start.2) | collective-permute-done | bytes 786464 | tf_op jit(solution)/shard_map/weights/ppermute | solution.py:199
  73.0 2.3 %forward.1 = (bf16[8,64,128]{2,1,0:T(8,128)(2,1)S(1)}, bf16[8,64,128]{2,1,0:T(8,128)(2,1)S(1)}, bf16[8,64,128]{2,1,0:T(8,128)(2,1)S(1)}) custom-call(s32[1,16]{1,0:T(1,128)S(1)} %copy-done.10, s32[1,16]{1,0:T(1,128)S(1)} %copy-done.11, s32[1,16]{1,0:T(1,128)S(1)} %copy-done.12, s32[1,48]{1,0:T(1,128)S(1)} %collective-permute-done.1.far, s32[1]{0:T(128)} %bitcast.core, ...), custom_call_target="tpu_custom_call" | custom-call | flops 201326592 | bytes 6291456 | tf_op jit(solution)/shard_map/forward/pallas_call | solution.py:158
  75.3 2.6 %tile_terms.1 = (bf16[32,32,384]{2,1,0:T(8,128)(2,1)S(1)}, bf16[32,32,384]{2,1,0:T(8,128)(2,1)}, bf16[32,32,384]{2,1,0:T(8,128)(2,1)S(1)}, bf16[32,32,384]{2,1,0:T(8,128)(2,1)S(1)}) custom-call(s32[1,16]{1,0:T(1,128)S(1)} %copy-done.10, s32[1,16]{1,0:T(1,128)S(1)} %copy-done.11, s32[1,16]{1,0:T(1,128)S(1)} %copy-done.12, ...), custom_call_target="tpu_custom_call" | custom-call | flops 201326592 | bytes 6291456 | tf_op jit(solution)/shard_map/tile_terms/pallas_call | solution.py:158
  77.9 2.3 %collective-permute-start.8 = (bf16[32,32,384]{2,1,0:T(8,128)(2,1)S(1)}, bf16[32,32,384]{2,1,0:T(8,128)(2,1)S(1)}, u32[]{:S(2)}, u32[]{:S(2)}) collective-permute-start(bf16[32,32,384]{2,1,0:T(8,128)(2,1)S(1)} %get-tuple-element.37), channel_id=1, source_target_pairs={{0,16},{16,0},{1,17},{17,1},{2,18},{18,2},{3,19},{19,3},{4,20},{20... | collective-permute-start | bytes 2359304 | tf_op jit(solution)/shard_map/cores/ppermute | solution.py:232
  80.2 2.0 %collective-permute-start.3 = (bf16[32,32,384]{2,1,0:T(8,128)(2,1)}, bf16[32,32,384]{2,1,0:T(8,128)(2,1)}, u32[]{:S(2)}, u32[]{:S(2)}) collective-permute-start(bf16[32,32,384]{2,1,0:T(8,128)(2,1)} %get-tuple-element.29), channel_id=1, source_target_pairs={{0,16},{16,0},{1,17},{17,1},{2,18},{18,2},{3,19},{19,3},{4,20},{20... | collective-permute-start | bytes 2359304 | tf_op jit(solution)/shard_map/cores/ppermute | solution.py:233
  83.3 2.7 %collective-permute-start.9 = (bf16[32,32,384]{2,1,0:T(8,128)(2,1)}, bf16[32,32,384]{2,1,0:T(8,128)(2,1)}, u32[]{:S(2)}, u32[]{:S(2)}) collective-permute-start(bf16[32,32,384]{2,1,0:T(8,128)(2,1)} %add_convert_fusion.1), channel_id=1, source_target_pairs={{0,8},{8,0},{16,792},{24,272},{256,264},{264,256},{272,24},{280,52... | collective-permute-start | bytes 2359304 | tf_op jit(solution)/shard_map/layers/ppermute | solution.py:235
  86.9 2.6 %back.1 = (bf16[4,8,4096]{2,1,0:T(8,128)(2,1)S(1)}, bf16[8,4096]{1,0:T(8,128)(2,1)S(1)}, bf16[8,4096]{1,0:T(8,128)(2,1)S(1)}, bf16[8,4096]{1,0:T(8,128)(2,1)S(1)}, bf16[8,4096]{1,0:T(8,128)(2,1)S(1)}) custom-call(s32[1,16]{1,0:T(1,128)S(1)} %copy-done.10, s32[1,16]{1,0:T(1,128)S(1)} %copy-done.11, s32[1,48]{1,0:T(1,128)S(1)} %collective-permute-done.1.far, ...), custom_call_target="tpu_custom_call" | custom-call | flops 134217728 | bytes 6291456 | tf_op jit(solution)/shard_map/back/pallas_call | solution.py:158
  89.5 2.9 %collective-permute-start.4 = (bf16[4,8,4096]{2,1,0:T(8,128)(2,1)S(1)}, bf16[4,8,4096]{2,1,0:T(8,128)(2,1)S(1)}, u32[]{:S(2)}, u32[]{:S(2)}) collective-permute-start(bf16[4,8,4096]{2,1,0:T(8,128)(2,1)S(1)} %get-tuple-element.30), channel_id=1, source_target_pairs={{0,1},{1,0},{2,3},{3,2},{4,5},{5,4},{6,7},{7,6},{8,9},{9,8},{10,11... | collective-permute-start | bytes 786440 | tf_op jit(solution)/shard_map/partials/ppermute | solution.py:230
  92.4 1.3 add_convert_fusion.2
  93.8 4.0 %collective-permute-done.4 = bf16[4,8,4096]{2,1,0:T(8,128)(2,1)S(1)} collective-permute-done((bf16[4,8,4096]{2,1,0:T(8,128)(2,1)S(1)}, bf16[4,8,4096]{2,1,0:T(8,128)(2,1)S(1)}, u32[]{:S(2)}, u32[]{:S(2)}) %collective-permute-start.4) | collective-permute-done | bytes 262176 | tf_op jit(solution)/shard_map/partials/ppermute | solution.py:230
  97.8 2.2 %add_convert_fusion = bf16[32,32,384]{2,1,0:T(8,128)(2,1)} fusion(bf16[32,32,384]{2,1,0:T(8,128)(2,1)} %collective-permute-done.9, bf16[32,32,384]{2,1,0:T(8,128)(2,1)S(1)} %add_convert_fusion.2), kind=kLoop, calls=%fused_computation.1 | loop fusion | flops 1572864 | bytes 2359296 | tf_op jit(solution)/shard_map/tile_sums/convert_element_type | solution.py:228
  100.0 21.1 %all-to-all-start.1 = ((bf16[32,32,384]{2,1,0:T(8,128)(2,1)}), bf16[32,32,384]{2,1,0:T(8,128)(2,1)S(1)}, u32[]{:S(2)}, u32[]{:S(2)}) async-start(bf16[32,32,384]{2,1,0:T(8,128)(2,1)} %add_convert_fusion), calls=%async_computation.1 | async-start | bytes 1572864 | tf_op jit(solution)/shard_map/tile_sums/all_to_all | solution.py:238
  121.2 2.4 %collective-permute-start.5 = (bf16[8,4096]{1,0:T(8,128)(2,1)S(1)}, bf16[8,4096]{1,0:T(8,128)(2,1)S(1)}, u32[]{:S(2)}, u32[]{:S(2)}) collective-permute-start(bf16[8,4096]{1,0:T(8,128)(2,1)S(1)} %get-tuple-element.38), channel_id=1, source_target_pairs={{0,2},{1,3},{2,4},{3,5},{4,6},{5,7},{6,0},{7,1},{8,10},{9,11},{10,... | collective-permute-start | bytes 196616 | tf_op jit(solution)/shard_map/partials/ppermute | solution.py:243
  123.6 4.2 %collective-permute-start.7 = (bf16[8,4096]{1,0:T(8,128)(2,1)S(1)}, bf16[8,4096]{1,0:T(8,128)(2,1)S(1)}, u32[]{:S(2)}, u32[]{:S(2)}) collective-permute-start(bf16[8,4096]{1,0:T(8,128)(2,1)S(1)} %get-tuple-element.39), channel_id=1, source_target_pairs={{0,4},{1,5},{2,6},{3,7},{4,0},{5,1},{6,2},{7,3},{8,12},{9,13},{10,... | collective-permute-start | bytes 196616 | tf_op jit(solution)/shard_map/partials/ppermute | solution.py:243
  127.8 3.8 %collective-permute-start.6 = (bf16[8,4096]{1,0:T(8,128)(2,1)S(1)}, bf16[8,4096]{1,0:T(8,128)(2,1)S(1)}, u32[]{:S(2)}, u32[]{:S(2)}) collective-permute-start(bf16[8,4096]{1,0:T(8,128)(2,1)S(1)} %get-tuple-element.40), channel_id=1, source_target_pairs={{0,6},{1,7},{2,0},{3,1},{4,2},{5,3},{6,4},{7,5},{8,14},{9,15},{10,... | collective-permute-start | bytes 196616 | tf_op jit(solution)/shard_map/partials/ppermute | solution.py:243
  131.6 2.0 %collective-permute-done.7 = bf16[8,4096]{1,0:T(8,128)(2,1)S(1)} collective-permute-done((bf16[8,4096]{1,0:T(8,128)(2,1)S(1)}, bf16[8,4096]{1,0:T(8,128)(2,1)S(1)}, u32[]{:S(2)}, u32[]{:S(2)}) %collective-permute-start.7) | collective-permute-done | bytes 65568 | tf_op jit(solution)/shard_map/partials/ppermute | solution.py:243
  133.6 2.6 %collective-permute-done.6 = bf16[8,4096]{1,0:T(8,128)(2,1)S(1)} collective-permute-done((bf16[8,4096]{1,0:T(8,128)(2,1)S(1)}, bf16[8,4096]{1,0:T(8,128)(2,1)S(1)}, u32[]{:S(2)}, u32[]{:S(2)}) %collective-permute-start.6) | collective-permute-done | bytes 65568 | tf_op jit(solution)/shard_map/partials/ppermute | solution.py:243
  137.0 7.7 %all-to-all-done.1 = bf16[32,32,384]{2,1,0:T(8,128)(2,1)S(1)} async-done(((bf16[32,32,384]{2,1,0:T(8,128)(2,1)}), bf16[32,32,384]{2,1,0:T(8,128)(2,1)S(1)}, u32[]{:S(2)}, u32[]{:S(2)}) %all-to-all-start.1) | async-done | bytes 786464 | tf_op jit(solution)/shard_map/tile_sums/all_to_all | solution.py:238
  (40 shorter events, 5.8 us)
Async XLA Ops:
  33.6 7.0 %copy-start = (bf16[1,16,128,128]{3,2,1,0:T(8,128)(2,1)S(1)}, bf16[1,16,128,128]{3,2,1,0:T(8,128)(2,1)}, u32[]{:S(2)}) copy-start(bf16[1,16,128,128]{3,2,1,0:T(8,128)(2,1)} %param.10) | copy-start | bytes 1572868
  33.7 7.0 %copy-start.10 = (s32[1,16]{1,0:T(1,128)S(1)}, s32[1,16]{1,0:T(1,128)}, u32[]{:S(2)}) copy-start(s32[1,16]{1,0:T(1,128)} %g_idx.5) | copy-start | bytes 196
  33.7 7.0 %copy-start.11 = (s32[1,16]{1,0:T(1,128)S(1)}, s32[1,16]{1,0:T(1,128)}, u32[]{:S(2)}) copy-start(s32[1,16]{1,0:T(1,128)} %u_idx.5) | copy-start | bytes 196
  33.7 7.0 %copy-start.12 = (s32[1,16]{1,0:T(1,128)S(1)}, s32[1,16]{1,0:T(1,128)}, u32[]{:S(2)}) copy-start(s32[1,16]{1,0:T(1,128)} %d_idx.3) | copy-start | bytes 196
  33.7 7.1 %copy-start.1 = (bf16[1,16,128,128]{3,2,1,0:T(8,128)(2,1)S(1)}, bf16[1,16,128,128]{3,2,1,0:T(8,128)(2,1)}, u32[]{:S(2)}) copy-start(bf16[1,16,128,128]{3,2,1,0:T(8,128)(2,1)} %param.11) | copy-start | bytes 1572868
  33.7 7.1 %copy-start.5 = (bf16[1,16,128,128]{3,2,1,0:T(8,128)(2,1)S(1)}, bf16[1,16,128,128]{3,2,1,0:T(8,128)(2,1)}, u32[]{:S(2)}) copy-start(bf16[1,16,128,128]{3,2,1,0:T(8,128)(2,1)} %param.12) | copy-start | bytes 1572868
  33.7 38.1 %all-to-all-start = ((bf16[8,8,8192]{2,1,0:T(8,128)(2,1)}), bf16[8,8,8192]{2,1,0:T(8,128)(2,1)S(1)}, u32[]{:S(2)}, u32[]{:S(2)}) async-start(bf16[8,8,8192]{2,1,0:T(8,128)(2,1)} %spread.1), calls=%async_computation | async-start | bytes 2097152 | tf_op jit(solution)/shard_map/gather/all_to_all | solution.py:190
  40.9 15.2 %collective-permute-start = (bf16[3,8,128,128]{3,2,1,0:T(8,128)(2,1)S(1)}, bf16[3,8,128,128]{3,2,1,0:T(8,128)(2,1)S(1)}, u32[]{:S(2)}, u32[]{:S(2)}) collective-permute-start(bf16[3,8,128,128]{3,2,1,0:T(8,128)(2,1)S(1)} %pad_maximum_fusion), channel_id=1, source_target_pairs={{0,8},{8,0},{16,792},{24,272},{256,264},{264,256},{272,24},{280,52... | collective-permute-start | bytes 2359304 | tf_op jit(solution)/shard_map/weights/ppermute | solution.py:197
  46.1 10.0 %collective-permute-start.1 = (s32[1,48]{1,0:T(1,128)S(1)}, s32[1,48]{1,0:T(1,128)S(1)}, u32[]{:S(2)}, u32[]{:S(2)}) collective-permute-start(s32[1,48]{1,0:T(1,128)S(1)} %pad_add_fusion), channel_id=1, source_target_pairs={{0,8},{8,0},{1,9},{9,1},{2,10},{10,2},{3,11},{11,3},{4,12},{12,4},... | collective-permute-start | bytes 584 | tf_op jit(solution)/shard_map/weights/ppermute | solution.py:196
  56.1 14.8 %collective-permute-start.2 = (bf16[3,8,128,128]{3,2,1,0:T(8,128)(2,1)S(1)}, bf16[3,8,128,128]{3,2,1,0:T(8,128)(2,1)S(1)}, u32[]{:S(2)}, u32[]{:S(2)}) collective-permute-start(bf16[3,8,128,128]{3,2,1,0:T(8,128)(2,1)S(1)} %collective-permute-done.ra), channel_id=1, source_target_pairs={{0,16},{16,0},{1,17},{17,1},{2,18},{18,2},{3,19},{19,3},{4,20},{20... | collective-permute-start | bytes 2359304 | tf_op jit(solution)/shard_map/weights/ppermute | solution.py:199
  71.9 1.1 copy-start.3
  75.3 8.0 %copy-start.8 = (bf16[8,64,128]{2,1,0:T(8,128)(2,1)}, bf16[8,64,128]{2,1,0:T(8,128)(2,1)S(1)}, u32[]{:S(2)}) copy-start(bf16[8,64,128]{2,1,0:T(8,128)(2,1)S(1)} %get-tuple-element.25.dup) | copy-start | bytes 393220
  77.9 5.4 %copy-start.6 = (bf16[32,32,384]{2,1,0:T(8,128)(2,1)}, bf16[32,32,384]{2,1,0:T(8,128)(2,1)S(1)}, u32[]{:S(2)}) copy-start(bf16[32,32,384]{2,1,0:T(8,128)(2,1)S(1)} %get-tuple-element.28) | copy-start | bytes 2359300
  77.9 4.3 %collective-permute-start.8 = (bf16[32,32,384]{2,1,0:T(8,128)(2,1)S(1)}, bf16[32,32,384]{2,1,0:T(8,128)(2,1)S(1)}, u32[]{:S(2)}, u32[]{:S(2)}) collective-permute-start(bf16[32,32,384]{2,1,0:T(8,128)(2,1)S(1)} %get-tuple-element.37), channel_id=1, source_target_pairs={{0,16},{16,0},{1,17},{17,1},{2,18},{18,2},{3,19},{19,3},{4,20},{20... | collective-permute-start | bytes 2359304 | tf_op jit(solution)/shard_map/cores/ppermute | solution.py:232
  80.2 12.2 %collective-permute-start.3 = (bf16[32,32,384]{2,1,0:T(8,128)(2,1)}, bf16[32,32,384]{2,1,0:T(8,128)(2,1)}, u32[]{:S(2)}, u32[]{:S(2)}) collective-permute-start(bf16[32,32,384]{2,1,0:T(8,128)(2,1)} %get-tuple-element.29), channel_id=1, source_target_pairs={{0,16},{16,0},{1,17},{17,1},{2,18},{18,2},{3,19},{19,3},{4,20},{20... | collective-permute-start | bytes 2359304 | tf_op jit(solution)/shard_map/cores/ppermute | solution.py:233
  82.3 3.8 %copy-start.4 = (bf16[3,8,128,128]{3,2,1,0:T(8,128)(2,1)S(1)}, bf16[3,8,128,128]{3,2,1,0:T(8,128)(2,1)}, u32[]{:S(2)}) copy-start(bf16[3,8,128,128]{3,2,1,0:T(8,128)(2,1)} %copy-done.2) | copy-start | bytes 2359300
  83.3 14.4 %collective-permute-start.9 = (bf16[32,32,384]{2,1,0:T(8,128)(2,1)}, bf16[32,32,384]{2,1,0:T(8,128)(2,1)}, u32[]{:S(2)}, u32[]{:S(2)}) collective-permute-start(bf16[32,32,384]{2,1,0:T(8,128)(2,1)} %add_convert_fusion.1), channel_id=1, source_target_pairs={{0,8},{8,0},{16,792},{24,272},{256,264},{264,256},{272,24},{280,52... | collective-permute-start | bytes 2359304 | tf_op jit(solution)/shard_map/layers/ppermute | solution.py:235
  86.0 0.9 copy-start.9
  86.9 5.5 %copy-start.7 = (bf16[32,32,384]{2,1,0:T(8,128)(2,1)S(1)}, bf16[32,32,384]{2,1,0:T(8,128)(2,1)}, u32[]{:S(2)}) copy-start(bf16[32,32,384]{2,1,0:T(8,128)(2,1)} %copy-done.6) | copy-start | bytes 2359300
  89.5 8.3 %collective-permute-start.4 = (bf16[4,8,4096]{2,1,0:T(8,128)(2,1)S(1)}, bf16[4,8,4096]{2,1,0:T(8,128)(2,1)S(1)}, u32[]{:S(2)}, u32[]{:S(2)}) collective-permute-start(bf16[4,8,4096]{2,1,0:T(8,128)(2,1)S(1)} %get-tuple-element.30), channel_id=1, source_target_pairs={{0,1},{1,0},{2,3},{3,2},{4,5},{5,4},{6,7},{7,6},{8,9},{9,8},{10,11... | collective-permute-start | bytes 786440 | tf_op jit(solution)/shard_map/partials/ppermute | solution.py:230
  100.0 44.6 %all-to-all-start.1 = ((bf16[32,32,384]{2,1,0:T(8,128)(2,1)}), bf16[32,32,384]{2,1,0:T(8,128)(2,1)S(1)}, u32[]{:S(2)}, u32[]{:S(2)}) async-start(bf16[32,32,384]{2,1,0:T(8,128)(2,1)} %add_convert_fusion), calls=%async_computation.1 | async-start | bytes 1572864 | tf_op jit(solution)/shard_map/tile_sums/all_to_all | solution.py:238
  121.2 10.5 %collective-permute-start.5 = (bf16[8,4096]{1,0:T(8,128)(2,1)S(1)}, bf16[8,4096]{1,0:T(8,128)(2,1)S(1)}, u32[]{:S(2)}, u32[]{:S(2)}) collective-permute-start(bf16[8,4096]{1,0:T(8,128)(2,1)S(1)} %get-tuple-element.38), channel_id=1, source_target_pairs={{0,2},{1,3},{2,4},{3,5},{4,6},{5,7},{6,0},{7,1},{8,10},{9,11},{10,... | collective-permute-start | bytes 196616 | tf_op jit(solution)/shard_map/partials/ppermute | solution.py:243
  123.6 10.1 %collective-permute-start.7 = (bf16[8,4096]{1,0:T(8,128)(2,1)S(1)}, bf16[8,4096]{1,0:T(8,128)(2,1)S(1)}, u32[]{:S(2)}, u32[]{:S(2)}) collective-permute-start(bf16[8,4096]{1,0:T(8,128)(2,1)S(1)} %get-tuple-element.39), channel_id=1, source_target_pairs={{0,4},{1,5},{2,6},{3,7},{4,0},{5,1},{6,2},{7,3},{8,12},{9,13},{10,... | collective-permute-start | bytes 196616 | tf_op jit(solution)/shard_map/partials/ppermute | solution.py:243
  127.8 8.5 %collective-permute-start.6 = (bf16[8,4096]{1,0:T(8,128)(2,1)S(1)}, bf16[8,4096]{1,0:T(8,128)(2,1)S(1)}, u32[]{:S(2)}, u32[]{:S(2)}) collective-permute-start(bf16[8,4096]{1,0:T(8,128)(2,1)S(1)} %get-tuple-element.40), channel_id=1, source_target_pairs={{0,6},{1,7},{2,0},{3,1},{4,2},{5,3},{6,4},{7,5},{8,14},{9,15},{10,... | collective-permute-start | bytes 196616 | tf_op jit(solution)/shard_map/partials/ppermute | solution.py:243
  (1 other events, 0.9 us)

commit v8 on v7

--- a/solution.py
+++ b/solution.py
@@ -132,6 +132,10 @@
                     theirs[at] = jnp.where(first, odd, even).astype(BF16)
 
 
+def total(left, right, out):
+    out[...] = (left[...].astype(F32) + right[...].astype(F32)).astype(BF16)
+
+
 def beside():
     pairs = []
     for zh in range(4):
@@ -182,7 +186,7 @@
         send = pl.pallas_call(
             spread,
             out_shape=jax.ShapeDtypeStruct((line, here, 2 * width), BF16),
-            in_specs=[pl.BlockSpec(memory_space=pl.ANY)] * 2,
+            in_specs=[VMEM] * 2,
             out_specs=pl.BlockSpec(memory_space=pl.ANY),
             scratch_shapes=[pltpu.SemaphoreType.DMA((line, 2))],
             name="spread",
@@ -235,7 +239,17 @@
         near = lax.ppermute(add(far_mine, far_got), LAYERS, beside())
     with jax.named_scope("tile_sums"):
         own_sum, got = lax.optimization_barrier((add(own_mine, own_got), got))
-        grads = lax.all_to_all(add(own_sum, near), ("zh", "y"), 0, 0, tiled=True)
+        block = pl.BlockSpec((8, 32, 3 * TILE), lambda i: (i, 0, 0))
+        set_sum = pl.pallas_call(
+            total,
+            grid=(pairs // 8,),
+            out_shape=shape(pairs, 32, 3 * TILE),
+            in_specs=[block] * 2,
+            out_specs=block,
+            compiler_params=pltpu.CompilerParams(vmem_limit_bytes=8 << 20),
+            name="total",
+        )(own_sum, near)
+        grads = lax.all_to_all(set_sum, ("zh", "y"), 0, 0, tiled=True)
         sums = jnp.sum(grads.astype(F32), axis=0)
     with jax.named_scope("partials"):
         pair = [add(keep[k], got[k]) for k in range(line // 2)]

time: 146 us -> 116 us (0.79)
  Pallas kernels: 40.5 us -> 12.8 us
  other arithmetic: 6.27 us -> 4.05 us
    pallas_call x1, Pallas kernels: 33 us -> 2.02 us  [per_device(): pl.pallas_call(spread, out_shape=jax.ShapeDtypeStruct((line, here, 2 * wi...]
    pallas_call x0 -> x1, Pallas kernels: none -> 3.34 us  [per_device(): pl.pallas_call(total, grid=(pairs // 8,), out_shape=shape(pairs, 32, 3 *...]
    convert_element_type x5 -> x4, other arithmetic: 5.37 us -> 3.15 us  [per_device(): add = lambda *terms: sum((t.astype(F32) for t in terms)).astype(BF16)]
  transfers between devices with their start and end apart: 12 -> 12, of which waited for: 6 -> 6; matrix products, arithmetic and copies ran while one was open for 2% -> 3% of each run, Pallas kernels for 2% -> 2%
where the time goes in v8:
time: 116 us
  starting transfers between devices  68.5 us (59%)
  waiting for transfers between devices  26.3 us (23%)
  Pallas kernels  12.8 us (11%)
  other arithmetic  4.05 us (3%)
  local copies, waits for them, and re-layouts  3.05 us (3%)
    all_to_all x1, starting transfers between devices, per_device(): grads = lax.all_to_all(set_sum, ('zh', 'y'), 0, 0, tiled=True)  21.2 us
    ppermute x1, starting transfers between devices, per_device(): rb = lax.ppermute(ra, 'c', SWAP)  13.1 us
    ppermute x3, starting transfers between devices, per_device(): came = [lax.ppermute(pair[k], 'x', ring(2 * k)) for k in (1, 3, 2)]  10.4 us
    ppermute x1, waiting for transfers between devices, per_device(): far = lax.ppermute(index, 'zl', SWAP)  8.09 us
    all_to_all x1, waiting for transfers between devices, per_device(): grads = lax.all_to_all(set_sum, ('zh', 'y'), 0, 0, tiled=True)  7.69 us
    pallas_call x3, Pallas kernels, call(): pl.pallas_call(kernel, out_shape=out_shape, in_specs=[SMEM] * len(scalars...  7.46 us
    all_to_all x1, starting transfers between devices, per_device(): xa = lax.all_to_all(send, 'x', 0, 0, tiled=True).reshape(rows, 2 * width)  6.9 us
    ppermute x1, starting transfers between devices, per_device(): ra = lax.ppermute(stack, LAYERS, beside())  5.19 us
  transfers between devices with their start and end apart: 12, of which 6 were waited for; matrix products, arithmetic and copies ran while one was open for 3% of the time, Pallas kernels for 2%

profile of v8, /device:TPU:16, one launch (start us, length us, event | category | flops | bytes accessed | tf_op | source)
XLA Modules:
  0.0 115.7 jit_solution(18374391962429602263)
XLA Ops:
  0.6 2.0 %spread.1 = bf16[8,8,8192]{2,1,0:T(8,128)(2,1)} custom-call(bf16[8,4096]{1,0:T(8,128)(2,1)} %tokens.1, bf16[8,4096]{1,0:T(8,128)(2,1)} %grad_out.1), custom_call_target="tpu_custom_call" | custom-call | tf_op jit(solution)/shard_map/gather/spread/pallas_call | solution.py:186
  2.7 6.9 %all-to-all-start = ((bf16[8,8,8192]{2,1,0:T(8,128)(2,1)}), bf16[8,8,8192]{2,1,0:T(8,128)(2,1)S(1)}, u32[]{:S(2)}, u32[]{:S(2)}) async-start(bf16[8,8,8192]{2,1,0:T(8,128)(2,1)} %spread.1), calls=%async_computation | async-start | bytes 2097152 | tf_op jit(solution)/shard_map/gather/all_to_all | solution.py:194
  9.9 5.2 %collective-permute-start = (bf16[3,8,128,128]{3,2,1,0:T(8,128)(2,1)S(1)}, bf16[3,8,128,128]{3,2,1,0:T(8,128)(2,1)S(1)}, u32[]{:S(2)}, u32[]{:S(2)}) collective-permute-start(bf16[3,8,128,128]{3,2,1,0:T(8,128)(2,1)S(1)} %pad_maximum_fusion), channel_id=1, source_target_pairs={{0,8},{8,0},{16,792},{24,272},{256,264},{264,256},{272,24},{280,52... | collective-permute-start | bytes 2359304 | tf_op jit(solution)/shard_map/weights/ppermute | solution.py:201
  15.1 1.9 %collective-permute-start.1 = (s32[1,48]{1,0:T(1,128)S(1)}, s32[1,48]{1,0:T(1,128)S(1)}, u32[]{:S(2)}, u32[]{:S(2)}) collective-permute-start(s32[1,48]{1,0:T(1,128)S(1)} %pad_add_fusion), channel_id=1, source_target_pairs={{0,8},{8,0},{1,9},{9,1},{2,10},{10,2},{3,11},{11,3},{4,12},{12,4},... | collective-permute-start | bytes 584 | tf_op jit(solution)/shard_map/weights/ppermute | solution.py:200
  17.1 8.1 %collective-permute-done.1.far = s32[1,48]{1,0:T(1,128)S(1)} collective-permute-done((s32[1,48]{1,0:T(1,128)S(1)}, s32[1,48]{1,0:T(1,128)S(1)}, u32[]{:S(2)}, u32[]{:S(2)}) %collective-permute-start.1) | collective-permute-done | bytes 224 | tf_op jit(solution)/shard_map/weights/ppermute | solution.py:200
  25.1 13.1 %collective-permute-start.2 = (bf16[3,8,128,128]{3,2,1,0:T(8,128)(2,1)S(1)}, bf16[3,8,128,128]{3,2,1,0:T(8,128)(2,1)S(1)}, u32[]{:S(2)}, u32[]{:S(2)}) collective-permute-start(bf16[3,8,128,128]{3,2,1,0:T(8,128)(2,1)S(1)} %collective-permute-done.ra), channel_id=1, source_target_pairs={{0,16},{16,0},{1,17},{17,1},{2,18},{18,2},{3,19},{19,3},{4,20},{20... | collective-permute-start | bytes 2359304 | tf_op jit(solution)/shard_map/weights/ppermute | solution.py:203
  38.2 1.9 %collective-permute-done.2.rb = bf16[3,8,128,128]{3,2,1,0:T(8,128)(2,1)S(1)} collective-permute-done((bf16[3,8,128,128]{3,2,1,0:T(8,128)(2,1)S(1)}, bf16[3,8,128,128]{3,2,1,0:T(8,128)(2,1)S(1)}, u32[]{:S(2)}, u32[]{:S(2)}) %collective-permute-start.2) | collective-permute-done | bytes 786464 | tf_op jit(solution)/shard_map/weights/ppermute | solution.py:203
  42.1 2.3 %forward.1 = (bf16[8,64,128]{2,1,0:T(8,128)(2,1)S(1)}, bf16[8,64,128]{2,1,0:T(8,128)(2,1)S(1)}, bf16[8,64,128]{2,1,0:T(8,128)(2,1)S(1)}) custom-call(s32[1,16]{1,0:T(1,128)S(1)} %copy-done.10, s32[1,16]{1,0:T(1,128)S(1)} %copy-done.11, s32[1,16]{1,0:T(1,128)S(1)} %copy-done.12, s32[1,48]{1,0:T(1,128)S(1)} %collective-permute-done.1.far, s32[1]{0:T(128)} %bitcast.core, ...), custom_call_target="tpu_custom_call" | custom-call | flops 201326592 | bytes 6291456 | tf_op jit(solution)/shard_map/forward/pallas_call | solution.py:162
  44.5 2.6 %tile_terms.1 = (bf16[32,32,384]{2,1,0:T(8,128)(2,1)S(1)}, bf16[32,32,384]{2,1,0:T(8,128)(2,1)}, bf16[32,32,384]{2,1,0:T(8,128)(2,1)S(1)}, bf16[32,32,384]{2,1,0:T(8,128)(2,1)S(1)}) custom-call(s32[1,16]{1,0:T(1,128)S(1)} %copy-done.10, s32[1,16]{1,0:T(1,128)S(1)} %copy-done.11, s32[1,16]{1,0:T(1,128)S(1)} %copy-done.12, ...), custom_call_target="tpu_custom_call" | custom-call | flops 201326592 | bytes 6291456 | tf_op jit(solution)/shard_map/tile_terms/pallas_call | solution.py:162
  47.0 2.3 %collective-permute-start.8 = (bf16[32,32,384]{2,1,0:T(8,128)(2,1)S(1)}, bf16[32,32,384]{2,1,0:T(8,128)(2,1)S(1)}, u32[]{:S(2)}, u32[]{:S(2)}) collective-permute-start(bf16[32,32,384]{2,1,0:T(8,128)(2,1)S(1)} %get-tuple-element.37), channel_id=1, source_target_pairs={{0,16},{16,0},{1,17},{17,1},{2,18},{18,2},{3,19},{19,3},{4,20},{20... | collective-permute-start | bytes 2359304 | tf_op jit(solution)/shard_map/cores/ppermute | solution.py:236
  49.3 2.0 %collective-permute-start.3 = (bf16[32,32,384]{2,1,0:T(8,128)(2,1)}, bf16[32,32,384]{2,1,0:T(8,128)(2,1)}, u32[]{:S(2)}, u32[]{:S(2)}) collective-permute-start(bf16[32,32,384]{2,1,0:T(8,128)(2,1)} %get-tuple-element.29), channel_id=1, source_target_pairs={{0,16},{16,0},{1,17},{17,1},{2,18},{18,2},{3,19},{19,3},{4,20},{20... | collective-permute-start | bytes 2359304 | tf_op jit(solution)/shard_map/cores/ppermute | solution.py:237
  52.5 2.5 %collective-permute-start.9 = (bf16[32,32,384]{2,1,0:T(8,128)(2,1)}, bf16[32,32,384]{2,1,0:T(8,128)(2,1)}, u32[]{:S(2)}, u32[]{:S(2)}) collective-permute-start(bf16[32,32,384]{2,1,0:T(8,128)(2,1)} %add_convert_fusion), channel_id=1, source_target_pairs={{0,8},{8,0},{16,792},{24,272},{256,264},{264,256},{272,24},{280,52... | collective-permute-start | bytes 2359304 | tf_op jit(solution)/shard_map/layers/ppermute | solution.py:239
  56.0 2.6 %back.1 = (bf16[4,8,4096]{2,1,0:T(8,128)(2,1)S(1)}, bf16[8,4096]{1,0:T(8,128)(2,1)S(1)}, bf16[8,4096]{1,0:T(8,128)(2,1)S(1)}, bf16[8,4096]{1,0:T(8,128)(2,1)S(1)}, bf16[8,4096]{1,0:T(8,128)(2,1)S(1)}) custom-call(s32[1,16]{1,0:T(1,128)S(1)} %copy-done.10, s32[1,16]{1,0:T(1,128)S(1)} %copy-done.11, s32[1,48]{1,0:T(1,128)S(1)} %collective-permute-done.1.far, ...), custom_call_target="tpu_custom_call" | custom-call | flops 134217728 | bytes 6291456 | tf_op jit(solution)/shard_map/back/pallas_call | solution.py:162
  58.5 3.0 %collective-permute-start.4 = (bf16[4,8,4096]{2,1,0:T(8,128)(2,1)S(1)}, bf16[4,8,4096]{2,1,0:T(8,128)(2,1)S(1)}, u32[]{:S(2)}, u32[]{:S(2)}) collective-permute-start(bf16[4,8,4096]{2,1,0:T(8,128)(2,1)S(1)} %get-tuple-element.30), channel_id=1, source_target_pairs={{0,1},{1,0},{2,3},{3,2},{4,5},{5,4},{6,7},{7,6},{8,9},{9,8},{10,11... | collective-permute-start | bytes 786440 | tf_op jit(solution)/shard_map/partials/ppermute | solution.py:234
  61.6 1.3 %add_convert_fusion.1.left = bf16[32,32,384]{2,1,0:T(8,128)(2,1)S(1)} fusion(bf16[32,32,384]{2,1,0:T(8,128)(2,1)} %collective-permute-done.3, bf16[32,32,384]{2,1,0:T(8,128)(2,1)S(1)} %copy-done.7), kind=kLoop, calls=%fused_computation.2 | loop fusion | flops 1572864 | bytes 2359296 | tf_op jit(solution)/shard_map/tile_sums/convert_element_type | solution.py:232
  62.9 3.9 %collective-permute-done.4 = bf16[4,8,4096]{2,1,0:T(8,128)(2,1)S(1)} collective-permute-done((bf16[4,8,4096]{2,1,0:T(8,128)(2,1)S(1)}, bf16[4,8,4096]{2,1,0:T(8,128)(2,1)S(1)}, u32[]{:S(2)}, u32[]{:S(2)}) %collective-permute-start.4) | collective-permute-done | bytes 262176 | tf_op jit(solution)/shard_map/partials/ppermute | solution.py:234
  66.8 3.3 %total.1 = bf16[32,32,384]{2,1,0:T(8,128)(2,1)} custom-call(bf16[32,32,384]{2,1,0:T(8,128)(2,1)S(1)} %add_convert_fusion.1.left, bf16[32,32,384]{2,1,0:T(8,128)(2,1)} %collective-permute-done.9.right), custom_call_target="tpu_custom_call" | custom-call | tf_op jit(solution)/shard_map/tile_sums/total/pallas_call | solution.py:243
  70.2 21.2 %all-to-all-start.1 = ((bf16[32,32,384]{2,1,0:T(8,128)(2,1)}), bf16[32,32,384]{2,1,0:T(8,128)(2,1)S(1)}, u32[]{:S(2)}, u32[]{:S(2)}) async-start(bf16[32,32,384]{2,1,0:T(8,128)(2,1)} %total.1), calls=%async_computation.1 | async-start | bytes 1572864 | tf_op jit(solution)/shard_map/tile_sums/all_to_all | solution.py:252
  91.4 2.4 %collective-permute-start.5 = (bf16[8,4096]{1,0:T(8,128)(2,1)S(1)}, bf16[8,4096]{1,0:T(8,128)(2,1)S(1)}, u32[]{:S(2)}, u32[]{:S(2)}) collective-permute-start(bf16[8,4096]{1,0:T(8,128)(2,1)S(1)} %get-tuple-element.38), channel_id=1, source_target_pairs={{0,2},{1,3},{2,4},{3,5},{4,6},{5,7},{6,0},{7,1},{8,10},{9,11},{10,... | collective-permute-start | bytes 196616 | tf_op jit(solution)/shard_map/partials/ppermute | solution.py:257
  93.8 4.2 %collective-permute-start.7 = (bf16[8,4096]{1,0:T(8,128)(2,1)S(1)}, bf16[8,4096]{1,0:T(8,128)(2,1)S(1)}, u32[]{:S(2)}, u32[]{:S(2)}) collective-permute-start(bf16[8,4096]{1,0:T(8,128)(2,1)S(1)} %get-tuple-element.39), channel_id=1, source_target_pairs={{0,4},{1,5},{2,6},{3,7},{4,0},{5,1},{6,2},{7,3},{8,12},{9,13},{10,... | collective-permute-start | bytes 196616 | tf_op jit(solution)/shard_map/partials/ppermute | solution.py:257
  98.0 3.8 %collective-permute-start.6 = (bf16[8,4096]{1,0:T(8,128)(2,1)S(1)}, bf16[8,4096]{1,0:T(8,128)(2,1)S(1)}, u32[]{:S(2)}, u32[]{:S(2)}) collective-permute-start(bf16[8,4096]{1,0:T(8,128)(2,1)S(1)} %get-tuple-element.40), channel_id=1, source_target_pairs={{0,6},{1,7},{2,0},{3,1},{4,2},{5,3},{6,4},{7,5},{8,14},{9,15},{10,... | collective-permute-start | bytes 196616 | tf_op jit(solution)/shard_map/partials/ppermute | solution.py:257
  101.9 2.0 %collective-permute-done.7 = bf16[8,4096]{1,0:T(8,128)(2,1)S(1)} collective-permute-done((bf16[8,4096]{1,0:T(8,128)(2,1)S(1)}, bf16[8,4096]{1,0:T(8,128)(2,1)S(1)}, u32[]{:S(2)}, u32[]{:S(2)}) %collective-permute-start.7) | collective-permute-done | bytes 65568 | tf_op jit(solution)/shard_map/partials/ppermute | solution.py:257
  103.9 2.7 %collective-permute-done.6 = bf16[8,4096]{1,0:T(8,128)(2,1)S(1)} collective-permute-done((bf16[8,4096]{1,0:T(8,128)(2,1)S(1)}, bf16[8,4096]{1,0:T(8,128)(2,1)S(1)}, u32[]{:S(2)}, u32[]{:S(2)}) %collective-permute-start.6) | collective-permute-done | bytes 65568 | tf_op jit(solution)/shard_map/partials/ppermute | solution.py:257
  107.2 7.7 %all-to-all-done.1 = bf16[32,32,384]{2,1,0:T(8,128)(2,1)S(1)} async-done(((bf16[32,32,384]{2,1,0:T(8,128)(2,1)}), bf16[32,32,384]{2,1,0:T(8,128)(2,1)S(1)}, u32[]{:S(2)}, u32[]{:S(2)}) %all-to-all-start.1) | async-done | bytes 786464 | tf_op jit(solution)/shard_map/tile_sums/all_to_all | solution.py:252
  (40 shorter events, 5.8 us)
Async XLA Ops:
  2.7 7.0 %copy-start = (bf16[1,16,128,128]{3,2,1,0:T(8,128)(2,1)S(1)}, bf16[1,16,128,128]{3,2,1,0:T(8,128)(2,1)}, u32[]{:S(2)}) copy-start(bf16[1,16,128,128]{3,2,1,0:T(8,128)(2,1)} %param.10) | copy-start | bytes 1572868
  2.7 7.0 %copy-start.10 = (s32[1,16]{1,0:T(1,128)S(1)}, s32[1,16]{1,0:T(1,128)}, u32[]{:S(2)}) copy-start(s32[1,16]{1,0:T(1,128)} %g_idx.5) | copy-start | bytes 196
  2.7 7.0 %copy-start.11 = (s32[1,16]{1,0:T(1,128)S(1)}, s32[1,16]{1,0:T(1,128)}, u32[]{:S(2)}) copy-start(s32[1,16]{1,0:T(1,128)} %u_idx.5) | copy-start | bytes 196
  2.7 7.0 %copy-start.12 = (s32[1,16]{1,0:T(1,128)S(1)}, s32[1,16]{1,0:T(1,128)}, u32[]{:S(2)}) copy-start(s32[1,16]{1,0:T(1,128)} %d_idx.3) | copy-start | bytes 196
  2.7 7.1 %copy-start.1 = (bf16[1,16,128,128]{3,2,1,0:T(8,128)(2,1)S(1)}, bf16[1,16,128,128]{3,2,1,0:T(8,128)(2,1)}, u32[]{:S(2)}) copy-start(bf16[1,16,128,128]{3,2,1,0:T(8,128)(2,1)} %param.11) | copy-start | bytes 1572868
  2.7 7.1 %copy-start.5 = (bf16[1,16,128,128]{3,2,1,0:T(8,128)(2,1)S(1)}, bf16[1,16,128,128]{3,2,1,0:T(8,128)(2,1)}, u32[]{:S(2)}) copy-start(bf16[1,16,128,128]{3,2,1,0:T(8,128)(2,1)} %param.12) | copy-start | bytes 1572868
  2.7 38.3 %all-to-all-start = ((bf16[8,8,8192]{2,1,0:T(8,128)(2,1)}), bf16[8,8,8192]{2,1,0:T(8,128)(2,1)S(1)}, u32[]{:S(2)}, u32[]{:S(2)}) async-start(bf16[8,8,8192]{2,1,0:T(8,128)(2,1)} %spread.1), calls=%async_computation | async-start | bytes 2097152 | tf_op jit(solution)/shard_map/gather/all_to_all | solution.py:194
  9.9 15.2 %collective-permute-start = (bf16[3,8,128,128]{3,2,1,0:T(8,128)(2,1)S(1)}, bf16[3,8,128,128]{3,2,1,0:T(8,128)(2,1)S(1)}, u32[]{:S(2)}, u32[]{:S(2)}) collective-permute-start(bf16[3,8,128,128]{3,2,1,0:T(8,128)(2,1)S(1)} %pad_maximum_fusion), channel_id=1, source_target_pairs={{0,8},{8,0},{16,792},{24,272},{256,264},{264,256},{272,24},{280,52... | collective-permute-start | bytes 2359304 | tf_op jit(solution)/shard_map/weights/ppermute | solution.py:201
  15.1 10.0 %collective-permute-start.1 = (s32[1,48]{1,0:T(1,128)S(1)}, s32[1,48]{1,0:T(1,128)S(1)}, u32[]{:S(2)}, u32[]{:S(2)}) collective-permute-start(s32[1,48]{1,0:T(1,128)S(1)} %pad_add_fusion), channel_id=1, source_target_pairs={{0,8},{8,0},{1,9},{9,1},{2,10},{10,2},{3,11},{11,3},{4,12},{12,4},... | collective-permute-start | bytes 584 | tf_op jit(solution)/shard_map/weights/ppermute | solution.py:200
  25.1 15.0 %collective-permute-start.2 = (bf16[3,8,128,128]{3,2,1,0:T(8,128)(2,1)S(1)}, bf16[3,8,128,128]{3,2,1,0:T(8,128)(2,1)S(1)}, u32[]{:S(2)}, u32[]{:S(2)}) collective-permute-start(bf16[3,8,128,128]{3,2,1,0:T(8,128)(2,1)S(1)} %collective-permute-done.ra), channel_id=1, source_target_pairs={{0,16},{16,0},{1,17},{17,1},{2,18},{18,2},{3,19},{19,3},{4,20},{20... | collective-permute-start | bytes 2359304 | tf_op jit(solution)/shard_map/weights/ppermute | solution.py:203
  41.0 1.1 copy-start.3
  44.5 8.0 %copy-start.8 = (bf16[8,64,128]{2,1,0:T(8,128)(2,1)}, bf16[8,64,128]{2,1,0:T(8,128)(2,1)S(1)}, u32[]{:S(2)}) copy-start(bf16[8,64,128]{2,1,0:T(8,128)(2,1)S(1)} %get-tuple-element.25.dup) | copy-start | bytes 393220
  47.0 5.5 %copy-start.6 = (bf16[32,32,384]{2,1,0:T(8,128)(2,1)}, bf16[32,32,384]{2,1,0:T(8,128)(2,1)S(1)}, u32[]{:S(2)}) copy-start(bf16[32,32,384]{2,1,0:T(8,128)(2,1)S(1)} %get-tuple-element.28) | copy-start | bytes 2359300
  47.0 4.3 %collective-permute-start.8 = (bf16[32,32,384]{2,1,0:T(8,128)(2,1)S(1)}, bf16[32,32,384]{2,1,0:T(8,128)(2,1)S(1)}, u32[]{:S(2)}, u32[]{:S(2)}) collective-permute-start(bf16[32,32,384]{2,1,0:T(8,128)(2,1)S(1)} %get-tuple-element.37), channel_id=1, source_target_pairs={{0,16},{16,0},{1,17},{17,1},{2,18},{18,2},{3,19},{19,3},{4,20},{20... | collective-permute-start | bytes 2359304 | tf_op jit(solution)/shard_map/cores/ppermute | solution.py:236
  49.3 12.2 %collective-permute-start.3 = (bf16[32,32,384]{2,1,0:T(8,128)(2,1)}, bf16[32,32,384]{2,1,0:T(8,128)(2,1)}, u32[]{:S(2)}, u32[]{:S(2)}) collective-permute-start(bf16[32,32,384]{2,1,0:T(8,128)(2,1)} %get-tuple-element.29), channel_id=1, source_target_pairs={{0,16},{16,0},{1,17},{17,1},{2,18},{18,2},{3,19},{19,3},{4,20},{20... | collective-permute-start | bytes 2359304 | tf_op jit(solution)/shard_map/cores/ppermute | solution.py:237
  51.4 3.7 %copy-start.4 = (bf16[3,8,128,128]{3,2,1,0:T(8,128)(2,1)S(1)}, bf16[3,8,128,128]{3,2,1,0:T(8,128)(2,1)}, u32[]{:S(2)}) copy-start(bf16[3,8,128,128]{3,2,1,0:T(8,128)(2,1)} %copy-done.2) | copy-start | bytes 2359300
  52.5 14.3 %collective-permute-start.9 = (bf16[32,32,384]{2,1,0:T(8,128)(2,1)}, bf16[32,32,384]{2,1,0:T(8,128)(2,1)}, u32[]{:S(2)}, u32[]{:S(2)}) collective-permute-start(bf16[32,32,384]{2,1,0:T(8,128)(2,1)} %add_convert_fusion), channel_id=1, source_target_pairs={{0,8},{8,0},{16,792},{24,272},{256,264},{264,256},{272,24},{280,52... | collective-permute-start | bytes 2359304 | tf_op jit(solution)/shard_map/layers/ppermute | solution.py:239
  55.1 0.9 copy-start.9
  56.0 5.6 %copy-start.7 = (bf16[32,32,384]{2,1,0:T(8,128)(2,1)S(1)}, bf16[32,32,384]{2,1,0:T(8,128)(2,1)}, u32[]{:S(2)}) copy-start(bf16[32,32,384]{2,1,0:T(8,128)(2,1)} %copy-done.6) | copy-start | bytes 2359300
  58.5 8.3 %collective-permute-start.4 = (bf16[4,8,4096]{2,1,0:T(8,128)(2,1)S(1)}, bf16[4,8,4096]{2,1,0:T(8,128)(2,1)S(1)}, u32[]{:S(2)}, u32[]{:S(2)}) collective-permute-start(bf16[4,8,4096]{2,1,0:T(8,128)(2,1)S(1)} %get-tuple-element.30), channel_id=1, source_target_pairs={{0,1},{1,0},{2,3},{3,2},{4,5},{5,4},{6,7},{7,6},{8,9},{9,8},{10,11... | collective-permute-start | bytes 786440 | tf_op jit(solution)/shard_map/partials/ppermute | solution.py:234
  70.2 44.8 %all-to-all-start.1 = ((bf16[32,32,384]{2,1,0:T(8,128)(2,1)}), bf16[32,32,384]{2,1,0:T(8,128)(2,1)S(1)}, u32[]{:S(2)}, u32[]{:S(2)}) async-start(bf16[32,32,384]{2,1,0:T(8,128)(2,1)} %total.1), calls=%async_computation.1 | async-start | bytes 1572864 | tf_op jit(solution)/shard_map/tile_sums/all_to_all | solution.py:252
  91.4 10.4 %collective-permute-start.5 = (bf16[8,4096]{1,0:T(8,128)(2,1)S(1)}, bf16[8,4096]{1,0:T(8,128)(2,1)S(1)}, u32[]{:S(2)}, u32[]{:S(2)}) collective-permute-start(bf16[8,4096]{1,0:T(8,128)(2,1)S(1)} %get-tuple-element.38), channel_id=1, source_target_pairs={{0,2},{1,3},{2,4},{3,5},{4,6},{5,7},{6,0},{7,1},{8,10},{9,11},{10,... | collective-permute-start | bytes 196616 | tf_op jit(solution)/shard_map/partials/ppermute | solution.py:257
  93.8 10.1 %collective-permute-start.7 = (bf16[8,4096]{1,0:T(8,128)(2,1)S(1)}, bf16[8,4096]{1,0:T(8,128)(2,1)S(1)}, u32[]{:S(2)}, u32[]{:S(2)}) collective-permute-start(bf16[8,4096]{1,0:T(8,128)(2,1)S(1)} %get-tuple-element.39), channel_id=1, source_target_pairs={{0,4},{1,5},{2,6},{3,7},{4,0},{5,1},{6,2},{7,3},{8,12},{9,13},{10,... | collective-permute-start | bytes 196616 | tf_op jit(solution)/shard_map/partials/ppermute | solution.py:257
  98.0 8.5 %collective-permute-start.6 = (bf16[8,4096]{1,0:T(8,128)(2,1)S(1)}, bf16[8,4096]{1,0:T(8,128)(2,1)S(1)}, u32[]{:S(2)}, u32[]{:S(2)}) collective-permute-start(bf16[8,4096]{1,0:T(8,128)(2,1)S(1)} %get-tuple-element.40), channel_id=1, source_target_pairs={{0,6},{1,7},{2,0},{3,1},{4,2},{5,3},{6,4},{7,5},{8,14},{9,15},{10,... | collective-permute-start | bytes 196616 | tf_op jit(solution)/shard_map/partials/ppermute | solution.py:257
  (1 other events, 0.9 us)

commit v9 on v5

--- a/solution.py
+++ b/solution.py
@@ -119,6 +119,10 @@
                     theirs[at] = jnp.where(first, odd, even).astype(BF16)
 
 
+def settle(far, out):
+    out[...] = jnp.maximum(far[...], -1)
+
+
 def beside():
     pairs = []
     for zh in range(4):
@@ -177,6 +181,16 @@
         far = lax.ppermute(index, "zl", SWAP)
         ra = lax.ppermute(stack, LAYERS, beside())
         ra, far = lax.optimization_barrier((ra, far))
+        far = pl.pallas_call(
+            settle,
+            out_shape=jax.ShapeDtypeStruct(far.shape, far.dtype),
+            in_specs=[VMEM],
+            out_specs=VMEM,
+            compiler_params=pltpu.CompilerParams(vmem_limit_bytes=1 << 20),
+            cost_estimate=pl.CostEstimate(flops=10 ** 10, bytes_accessed=0, transcendentals=0),
+            name="settle",
+        )(far)
+        ra, far = lax.optimization_barrier((ra, far))
         rb = lax.ppermute(ra, "c", SWAP)
     own = (gate_index, up_index, down_index)
     work = 2 * rows * TILE * TILE * 2 * slots
@@ -209,19 +223,20 @@
     add = lambda *terms: sum(t.astype(F32) for t in terms).astype(BF16)
     with jax.named_scope("partials"):
         got = lax.ppermute(give, "x", [(i, i ^ 1) for i in range(line)])
-        pair = [add(keep[k], got[k]) for k in range(line // 2)]
-        ring = lambda d: [(i, (i + d) % line) for i in range(line)]
-        came = [lax.ppermute(pair[k], "x", ring(2 * k)) for k in (1, 3, 2)]
-        input_sum = add(*[t.astype(F32) for t in (keep[0], got[0])], *came)
-    own_mine, got = lax.optimization_barrier((own_mine, got))
     with jax.named_scope("cores"):
         far_got = lax.ppermute(far_theirs, "c", SWAP)
         own_got = lax.ppermute(own_theirs, "c", SWAP)
     with jax.named_scope("layers"):
         near = lax.ppermute(add(far_mine, far_got), LAYERS, beside())
     with jax.named_scope("tile_sums"):
-        grads = lax.all_to_all(add(own_mine, own_got, near), ("zh", "y"), 0, 0, tiled=True)
+        own_sum, got = lax.optimization_barrier((add(own_mine, own_got), got))
+        grads = lax.all_to_all(add(own_sum, near), ("zh", "y"), 0, 0, tiled=True)
         sums = jnp.sum(grads.astype(F32), axis=0)
+    with jax.named_scope("partials"):
+        pair = [add(keep[k], got[k]) for k in range(line // 2)]
+        ring = lambda d: [(i, (i + d) % line) for i in range(line)]
+        came = [lax.ppermute(pair[k], "x", ring(2 * k)) for k in (1, 3, 2)]
+        input_sum = add(*[t.astype(F32) for t in (keep[0], got[0])], *came)
     return (input_sum, sums[None])
 
 

time: 115 us -> 120 us (1.043)
  the two profiles are of different devices: /device:TPU:16 before, /device:TPU:144 now
where the time goes in v9:
time: 120 us; the launch traced here: 119 us
  starting transfers between devices  63.6 us (53%)
  waiting for transfers between devices  34.1 us (28%)
  Pallas kernels  7.46 us (6%)
  other arithmetic  7.2 us (6%)
  local copies, waits for them, and re-layouts  6.1 us (5%)
    all_to_all x1, starting transfers between devices, per_device(): grads = lax.all_to_all(add(own_sum, near), ('zh', 'y'), 0, 0, tiled=True)  18.3 us
    ppermute x1, starting transfers between devices, per_device(): rb = lax.ppermute(ra, 'c', SWAP)  12.7 us
    ppermute x3, starting transfers between devices, per_device(): came = [lax.ppermute(pair[k], 'x', ring(2 * k)) for k in (1, 3, 2)]  10.1 us
    all_to_all x1, waiting for transfers between devices, per_device(): grads = lax.all_to_all(add(own_sum, near), ('zh', 'y'), 0, 0, tiled=True)  9.55 us
    all_to_all x1, waiting for transfers between devices, per_device(): xa = lax.all_to_all(send, 'x', 0, 0, tiled=True).reshape(rows, 2 * width)  8.92 us
    pallas_call x3, Pallas kernels, call(): pl.pallas_call(kernel, out_shape=out_shape, in_specs=[SMEM] * len(scalars...  7.45 us
    ppermute x1, waiting for transfers between devices, per_device(): got = lax.ppermute(give, 'x', [(i, i ^ 1) for i in range(line)])  7.03 us
    all_to_all x1, starting transfers between devices, per_device(): xa = lax.all_to_all(send, 'x', 0, 0, tiled=True).reshape(rows, 2 * width)  6.76 us
  transfers between devices with their start and end apart: 12, of which 7 were waited for; matrix products, arithmetic and copies ran while one was open for 4% of the time, Pallas kernels for 2%

profile of v9, /device:TPU:144, one launch (start us, length us, event | category | flops | bytes accessed | tf_op | source)
XLA Modules:
  0.0 119.4 jit_solution(7623287175310703526)
XLA Ops:
  3.9 1.9 %collective-permute-start = (bf16[3,8,128,128]{3,2,1,0:T(8,128)(2,1)}, bf16[3,8,128,128]{3,2,1,0:T(8,128)(2,1)S(1)}, u32[]{:S(2)}, u32[]{:S(2)}) collective-permute-start(bf16[3,8,128,128]{3,2,1,0:T(8,128)(2,1)} %pad_maximum_fusion), channel_id=1, source_target_pairs={{0,8},{8,0},{16,792},{24,272},{256,264},{264,256},{272,24},{280,52... | collective-permute-start | bytes 2359304 | tf_op jit(solution)/shard_map/weights/ppermute | solution.py:182
  6.9 6.8 %all-to-all-start = ((bf16[8,8,8192]{2,1,0:T(8,128)(2,1)}), bf16[8,8,8192]{2,1,0:T(8,128)(2,1)S(1)}, u32[]{:S(2)}, u32[]{:S(2)}) async-start(bf16[8,8,8192]{2,1,0:T(8,128)(2,1)} %broadcast_in_dim.4), calls=%async_computation | async-start | bytes 2097152 | tf_op jit(solution)/shard_map/gather/all_to_all | solution.py:175
  13.7 4.1 %collective-permute-start.1 = (s32[1,48]{1,0:T(1,128)S(1)}, s32[1,48]{1,0:T(1,128)S(1)}, u32[]{:S(2)}, u32[]{:S(2)}) collective-permute-start(s32[1,48]{1,0:T(1,128)S(1)} %pad_add_fusion), channel_id=1, source_target_pairs={{0,8},{8,0},{1,9},{9,1},{2,10},{10,2},{3,11},{11,3},{4,12},{12,4},... | collective-permute-start | bytes 584 | tf_op jit(solution)/shard_map/weights/ppermute | solution.py:181
  17.7 1.5 %collective-permute-done.1.far = s32[1,48]{1,0:T(1,128)S(1)} collective-permute-done((s32[1,48]{1,0:T(1,128)S(1)}, s32[1,48]{1,0:T(1,128)S(1)}, u32[]{:S(2)}, u32[]{:S(2)}) %collective-permute-start.1) | collective-permute-done | bytes 224 | tf_op jit(solution)/shard_map/weights/ppermute | solution.py:181
  19.2 12.7 %collective-permute-start.2 = (bf16[3,8,128,128]{3,2,1,0:T(8,128)(2,1)S(1)}, bf16[3,8,128,128]{3,2,1,0:T(8,128)(2,1)S(1)}, u32[]{:S(2)}, u32[]{:S(2)}) collective-permute-start(bf16[3,8,128,128]{3,2,1,0:T(8,128)(2,1)S(1)} %collective-permute-done.ra), channel_id=1, source_target_pairs={{0,16},{16,0},{1,17},{17,1},{2,18},{18,2},{3,19},{19,3},{4,20},{20... | collective-permute-start | bytes 2359304 | tf_op jit(solution)/shard_map/weights/ppermute | solution.py:194
  32.0 1.9 %collective-permute-done.2.rb = bf16[3,8,128,128]{3,2,1,0:T(8,128)(2,1)S(1)} collective-permute-done((bf16[3,8,128,128]{3,2,1,0:T(8,128)(2,1)S(1)}, bf16[3,8,128,128]{3,2,1,0:T(8,128)(2,1)S(1)}, u32[]{:S(2)}, u32[]{:S(2)}) %collective-permute-start.2) | collective-permute-done | bytes 786464 | tf_op jit(solution)/shard_map/weights/ppermute | solution.py:194
  34.8 8.9 %all-to-all-done = bf16[8,8,8192]{2,1,0:T(8,128)(2,1)S(1)} async-done(((bf16[8,8,8192]{2,1,0:T(8,128)(2,1)}), bf16[8,8,8192]{2,1,0:T(8,128)(2,1)S(1)}, u32[]{:S(2)}, u32[]{:S(2)}) %all-to-all-start) | async-done | bytes 1048608 | tf_op jit(solution)/shard_map/gather/all_to_all | solution.py:175
  44.8 2.3 %forward.1 = (bf16[8,64,128]{2,1,0:T(8,128)(2,1)S(1)}, bf16[8,64,128]{2,1,0:T(8,128)(2,1)S(1)}, bf16[8,64,128]{2,1,0:T(8,128)(2,1)S(1)}) custom-call(s32[1,16]{1,0:T(1,128)S(1)} %copy-done.10, s32[1,16]{1,0:T(1,128)S(1)} %copy-done.11, s32[1,16]{1,0:T(1,128)S(1)} %copy-done.12, s32[1,48]{1,0:T(1,128)S(1)} %settle.1.far, s32[1]{0:T(128)} %bitcast.core, ...), custom_call_target="tpu_custom_call" | custom-call | flops 201326592 | bytes 6291456 | tf_op jit(solution)/shard_map/forward/pallas_call | solution.py:149
  47.1 2.6 %tile_terms.1 = (bf16[32,32,384]{2,1,0:T(8,128)(2,1)S(1)}, bf16[32,32,384]{2,1,0:T(8,128)(2,1)}, bf16[32,32,384]{2,1,0:T(8,128)(2,1)S(1)}, bf16[32,32,384]{2,1,0:T(8,128)(2,1)S(1)}) custom-call(s32[1,16]{1,0:T(1,128)S(1)} %copy-done.10, s32[1,16]{1,0:T(1,128)S(1)} %copy-done.11, s32[1,16]{1,0:T(1,128)S(1)} %copy-done.12, s32[1,48]{1,0:T(1,128)S(1)} %settle.1.far, ...), custom_call_target="tpu_custom_call" | custom-call | flops 201326592 | bytes 6291456 | tf_op jit(solution)/shard_map/tile_terms/pallas_call | solution.py:149
  49.7 2.0 %collective-permute-start.8 = (bf16[32,32,384]{2,1,0:T(8,128)(2,1)S(1)}, bf16[32,32,384]{2,1,0:T(8,128)(2,1)S(1)}, u32[]{:S(2)}, u32[]{:S(2)}) collective-permute-start(bf16[32,32,384]{2,1,0:T(8,128)(2,1)S(1)} %get-tuple-element.41), channel_id=1, source_target_pairs={{0,16},{16,0},{1,17},{17,1},{2,18},{18,2},{3,19},{19,3},{4,20},{20... | collective-permute-start | bytes 2359304 | tf_op jit(solution)/shard_map/cores/ppermute | solution.py:227
  51.7 2.3 %collective-permute-start.3 = (bf16[32,32,384]{2,1,0:T(8,128)(2,1)}, bf16[32,32,384]{2,1,0:T(8,128)(2,1)}, u32[]{:S(2)}, u32[]{:S(2)}) collective-permute-start(bf16[32,32,384]{2,1,0:T(8,128)(2,1)} %get-tuple-element.33), channel_id=1, source_target_pairs={{0,16},{16,0},{1,17},{17,1},{2,18},{18,2},{3,19},{19,3},{4,20},{20... | collective-permute-start | bytes 2359304 | tf_op jit(solution)/shard_map/cores/ppermute | solution.py:228
  55.2 3.4 %collective-permute-start.9 = (bf16[32,32,384]{2,1,0:T(8,128)(2,1)}, bf16[32,32,384]{2,1,0:T(8,128)(2,1)}, u32[]{:S(2)}, u32[]{:S(2)}) collective-permute-start(bf16[32,32,384]{2,1,0:T(8,128)(2,1)} %add_convert_fusion.1), channel_id=1, source_target_pairs={{0,8},{8,0},{16,792},{24,272},{256,264},{264,256},{272,24},{280,52... | collective-permute-start | bytes 2359304 | tf_op jit(solution)/shard_map/layers/ppermute | solution.py:230
  59.5 2.6 %back.1 = (bf16[4,8,4096]{2,1,0:T(8,128)(2,1)S(1)}, bf16[8,4096]{1,0:T(8,128)(2,1)S(1)}, bf16[8,4096]{1,0:T(8,128)(2,1)S(1)}, bf16[8,4096]{1,0:T(8,128)(2,1)S(1)}, bf16[8,4096]{1,0:T(8,128)(2,1)S(1)}) custom-call(s32[1,16]{1,0:T(1,128)S(1)} %copy-done.10, s32[1,16]{1,0:T(1,128)S(1)} %copy-done.11, s32[1,48]{1,0:T(1,128)S(1)} %settle.1.far, s32[1]{0:T(128)} %bitcast.core, ...), custom_call_target="tpu_custom_call" | custom-call | flops 134217728 | bytes 6291456 | tf_op jit(solution)/shard_map/back/pallas_call | solution.py:149
  62.1 1.9 %collective-permute-start.4 = (bf16[4,8,4096]{2,1,0:T(8,128)(2,1)S(1)}, bf16[4,8,4096]{2,1,0:T(8,128)(2,1)S(1)}, u32[]{:S(2)}, u32[]{:S(2)}) collective-permute-start(bf16[4,8,4096]{2,1,0:T(8,128)(2,1)S(1)} %get-tuple-element.34), channel_id=1, source_target_pairs={{0,1},{1,0},{2,3},{3,2},{4,5},{5,4},{6,7},{7,6},{8,9},{9,8},{10,11... | collective-permute-start | bytes 786440 | tf_op jit(solution)/shard_map/partials/ppermute | solution.py:225
  64.1 1.3 %add_convert_fusion.2 = bf16[32,32,384]{2,1,0:T(8,128)(2,1)S(1)} fusion(bf16[32,32,384]{2,1,0:T(8,128)(2,1)} %collective-permute-done.3, bf16[32,32,384]{2,1,0:T(8,128)(2,1)S(1)} %copy-done.7), kind=kLoop, calls=%fused_computation.3 | loop fusion | flops 1572864 | bytes 2359296 | tf_op jit(solution)/shard_map/tile_sums/convert_element_type | solution.py:223
  65.4 7.0 %collective-permute-done.4 = bf16[4,8,4096]{2,1,0:T(8,128)(2,1)S(1)} collective-permute-done((bf16[4,8,4096]{2,1,0:T(8,128)(2,1)S(1)}, bf16[4,8,4096]{2,1,0:T(8,128)(2,1)S(1)}, u32[]{:S(2)}, u32[]{:S(2)}) %collective-permute-start.4) | collective-permute-done | bytes 262176 | tf_op jit(solution)/shard_map/partials/ppermute | solution.py:225
  72.4 2.2 %add_convert_fusion = bf16[32,32,384]{2,1,0:T(8,128)(2,1)} fusion(bf16[32,32,384]{2,1,0:T(8,128)(2,1)} %collective-permute-done.9, bf16[32,32,384]{2,1,0:T(8,128)(2,1)S(1)} %add_convert_fusion.2), kind=kLoop, calls=%fused_computation.1 | loop fusion | flops 1572864 | bytes 2359296 | tf_op jit(solution)/shard_map/tile_sums/convert_element_type | solution.py:223
  74.7 18.3 %all-to-all-start.1 = ((bf16[32,32,384]{2,1,0:T(8,128)(2,1)}), bf16[32,32,384]{2,1,0:T(8,128)(2,1)S(1)}, u32[]{:S(2)}, u32[]{:S(2)}) async-start(bf16[32,32,384]{2,1,0:T(8,128)(2,1)} %add_convert_fusion), calls=%async_computation.1 | async-start | bytes 1572864 | tf_op jit(solution)/shard_map/tile_sums/all_to_all | solution.py:233
  93.1 2.1 %collective-permute-start.5 = (bf16[8,4096]{1,0:T(8,128)(2,1)S(1)}, bf16[8,4096]{1,0:T(8,128)(2,1)S(1)}, u32[]{:S(2)}, u32[]{:S(2)}) collective-permute-start(bf16[8,4096]{1,0:T(8,128)(2,1)S(1)} %get-tuple-element.42), channel_id=1, source_target_pairs={{0,2},{1,3},{2,4},{3,5},{4,6},{5,7},{6,0},{7,1},{8,10},{9,11},{10,... | collective-permute-start | bytes 196616 | tf_op jit(solution)/shard_map/partials/ppermute | solution.py:238
  95.2 4.4 %collective-permute-start.7 = (bf16[8,4096]{1,0:T(8,128)(2,1)S(1)}, bf16[8,4096]{1,0:T(8,128)(2,1)S(1)}, u32[]{:S(2)}, u32[]{:S(2)}) collective-permute-start(bf16[8,4096]{1,0:T(8,128)(2,1)S(1)} %get-tuple-element.43), channel_id=1, source_target_pairs={{0,4},{1,5},{2,6},{3,7},{4,0},{5,1},{6,2},{7,3},{8,12},{9,13},{10,... | collective-permute-start | bytes 196616 | tf_op jit(solution)/shard_map/partials/ppermute | solution.py:238
  99.5 3.7 %collective-permute-start.6 = (bf16[8,4096]{1,0:T(8,128)(2,1)S(1)}, bf16[8,4096]{1,0:T(8,128)(2,1)S(1)}, u32[]{:S(2)}, u32[]{:S(2)}) collective-permute-start(bf16[8,4096]{1,0:T(8,128)(2,1)S(1)} %get-tuple-element.44), channel_id=1, source_target_pairs={{0,6},{1,7},{2,0},{3,1},{4,2},{5,3},{6,4},{7,5},{8,14},{9,15},{10,... | collective-permute-start | bytes 196616 | tf_op jit(solution)/shard_map/partials/ppermute | solution.py:238
  103.2 2.0 %collective-permute-done.7 = bf16[8,4096]{1,0:T(8,128)(2,1)S(1)} collective-permute-done((bf16[8,4096]{1,0:T(8,128)(2,1)S(1)}, bf16[8,4096]{1,0:T(8,128)(2,1)S(1)}, u32[]{:S(2)}, u32[]{:S(2)}) %collective-permute-start.7) | collective-permute-done | bytes 65568 | tf_op jit(solution)/shard_map/partials/ppermute | solution.py:238
  105.2 3.2 %collective-permute-done.6 = bf16[8,4096]{1,0:T(8,128)(2,1)S(1)} collective-permute-done((bf16[8,4096]{1,0:T(8,128)(2,1)S(1)}, bf16[8,4096]{1,0:T(8,128)(2,1)S(1)}, u32[]{:S(2)}, u32[]{:S(2)}) %collective-permute-start.6) | collective-permute-done | bytes 65568 | tf_op jit(solution)/shard_map/partials/ppermute | solution.py:238
  109.1 9.5 %all-to-all-done.1 = bf16[32,32,384]{2,1,0:T(8,128)(2,1)S(1)} async-done(((bf16[32,32,384]{2,1,0:T(8,128)(2,1)}), bf16[32,32,384]{2,1,0:T(8,128)(2,1)S(1)}, u32[]{:S(2)}, u32[]{:S(2)}) %all-to-all-start.1) | async-done | bytes 786464 | tf_op jit(solution)/shard_map/tile_sums/all_to_all | solution.py:233
  (46 shorter events, 9.7 us)
Async XLA Ops:
  0.6 2.1 %copy-start.11 = (s32[1,16]{1,0:T(1,128)S(1)}, s32[1,16]{1,0:T(1,128)}, u32[]{:S(2)}) copy-start(s32[1,16]{1,0:T(1,128)} %u_idx.5) | copy-start | bytes 196
  0.6 2.1 %copy-start.10 = (s32[1,16]{1,0:T(1,128)S(1)}, s32[1,16]{1,0:T(1,128)}, u32[]{:S(2)}) copy-start(s32[1,16]{1,0:T(1,128)} %g_idx.5) | copy-start | bytes 196
  0.7 2.1 %copy-start.12 = (s32[1,16]{1,0:T(1,128)S(1)}, s32[1,16]{1,0:T(1,128)}, u32[]{:S(2)}) copy-start(s32[1,16]{1,0:T(1,128)} %d_idx.3) | copy-start | bytes 196
  2.8 3.0 %copy-start.13 = (bf16[8,4096]{1,0:T(8,128)(2,1)S(1)}, bf16[8,4096]{1,0:T(8,128)(2,1)}, u32[]{:S(2)}) copy-start(bf16[8,4096]{1,0:T(8,128)(2,1)} %param.9) | copy-start | bytes 196612
  2.8 3.0 %copy-start.14 = (bf16[8,4096]{1,0:T(8,128)(2,1)S(1)}, bf16[8,4096]{1,0:T(8,128)(2,1)}, u32[]{:S(2)}) copy-start(bf16[8,4096]{1,0:T(8,128)(2,1)} %param.8) | copy-start | bytes 196612
  3.9 15.4 %collective-permute-start = (bf16[3,8,128,128]{3,2,1,0:T(8,128)(2,1)}, bf16[3,8,128,128]{3,2,1,0:T(8,128)(2,1)S(1)}, u32[]{:S(2)}, u32[]{:S(2)}) collective-permute-start(bf16[3,8,128,128]{3,2,1,0:T(8,128)(2,1)} %pad_maximum_fusion), channel_id=1, source_target_pairs={{0,8},{8,0},{16,792},{24,272},{256,264},{264,256},{272,24},{280,52... | collective-permute-start | bytes 2359304 | tf_op jit(solution)/shard_map/weights/ppermute | solution.py:182
  6.9 36.8 %all-to-all-start = ((bf16[8,8,8192]{2,1,0:T(8,128)(2,1)}), bf16[8,8,8192]{2,1,0:T(8,128)(2,1)S(1)}, u32[]{:S(2)}, u32[]{:S(2)}) async-start(bf16[8,8,8192]{2,1,0:T(8,128)(2,1)} %broadcast_in_dim.4), calls=%async_computation | async-start | bytes 2097152 | tf_op jit(solution)/shard_map/gather/all_to_all | solution.py:175
  13.6 30.0 %copy-start = (bf16[1,16,128,128]{3,2,1,0:T(8,128)(2,1)S(1)}, bf16[1,16,128,128]{3,2,1,0:T(8,128)(2,1)}, u32[]{:S(2)}) copy-start(bf16[1,16,128,128]{3,2,1,0:T(8,128)(2,1)} %param.10) | copy-start | bytes 1572868
  13.6 30.0 %copy-start.1 = (bf16[1,16,128,128]{3,2,1,0:T(8,128)(2,1)S(1)}, bf16[1,16,128,128]{3,2,1,0:T(8,128)(2,1)}, u32[]{:S(2)}) copy-start(bf16[1,16,128,128]{3,2,1,0:T(8,128)(2,1)} %param.11) | copy-start | bytes 1572868
  13.6 30.0 %copy-start.5 = (bf16[1,16,128,128]{3,2,1,0:T(8,128)(2,1)S(1)}, bf16[1,16,128,128]{3,2,1,0:T(8,128)(2,1)}, u32[]{:S(2)}) copy-start(bf16[1,16,128,128]{3,2,1,0:T(8,128)(2,1)} %param.12) | copy-start | bytes 1572868
  13.7 5.6 %collective-permute-start.1 = (s32[1,48]{1,0:T(1,128)S(1)}, s32[1,48]{1,0:T(1,128)S(1)}, u32[]{:S(2)}, u32[]{:S(2)}) collective-permute-start(s32[1,48]{1,0:T(1,128)S(1)} %pad_add_fusion), channel_id=1, source_target_pairs={{0,8},{8,0},{1,9},{9,1},{2,10},{10,2},{3,11},{11,3},{4,12},{12,4},... | collective-permute-start | bytes 584 | tf_op jit(solution)/shard_map/weights/ppermute | solution.py:181
  19.2 14.6 %collective-permute-start.2 = (bf16[3,8,128,128]{3,2,1,0:T(8,128)(2,1)S(1)}, bf16[3,8,128,128]{3,2,1,0:T(8,128)(2,1)S(1)}, u32[]{:S(2)}, u32[]{:S(2)}) collective-permute-start(bf16[3,8,128,128]{3,2,1,0:T(8,128)(2,1)S(1)} %collective-permute-done.ra), channel_id=1, source_target_pairs={{0,16},{16,0},{1,17},{17,1},{2,18},{18,2},{3,19},{19,3},{4,20},{20... | collective-permute-start | bytes 2359304 | tf_op jit(solution)/shard_map/weights/ppermute | solution.py:194
  47.1 8.1 %copy-start.8 = (bf16[8,64,128]{2,1,0:T(8,128)(2,1)}, bf16[8,64,128]{2,1,0:T(8,128)(2,1)S(1)}, u32[]{:S(2)}) copy-start(bf16[8,64,128]{2,1,0:T(8,128)(2,1)S(1)} %get-tuple-element.29.dup) | copy-start | bytes 393220
  49.7 5.5 %copy-start.6 = (bf16[32,32,384]{2,1,0:T(8,128)(2,1)}, bf16[32,32,384]{2,1,0:T(8,128)(2,1)S(1)}, u32[]{:S(2)}) copy-start(bf16[32,32,384]{2,1,0:T(8,128)(2,1)S(1)} %get-tuple-element.32) | copy-start | bytes 2359300
  49.7 4.3 %collective-permute-start.8 = (bf16[32,32,384]{2,1,0:T(8,128)(2,1)S(1)}, bf16[32,32,384]{2,1,0:T(8,128)(2,1)S(1)}, u32[]{:S(2)}, u32[]{:S(2)}) collective-permute-start(bf16[32,32,384]{2,1,0:T(8,128)(2,1)S(1)} %get-tuple-element.41), channel_id=1, source_target_pairs={{0,16},{16,0},{1,17},{17,1},{2,18},{18,2},{3,19},{19,3},{4,20},{20... | collective-permute-start | bytes 2359304 | tf_op jit(solution)/shard_map/cores/ppermute | solution.py:227
  51.7 12.3 %collective-permute-start.3 = (bf16[32,32,384]{2,1,0:T(8,128)(2,1)}, bf16[32,32,384]{2,1,0:T(8,128)(2,1)}, u32[]{:S(2)}, u32[]{:S(2)}) collective-permute-start(bf16[32,32,384]{2,1,0:T(8,128)(2,1)} %get-tuple-element.33), channel_id=1, source_target_pairs={{0,16},{16,0},{1,17},{17,1},{2,18},{18,2},{3,19},{19,3},{4,20},{20... | collective-permute-start | bytes 2359304 | tf_op jit(solution)/shard_map/cores/ppermute | solution.py:228
  54.1 4.5 %copy-start.4 = (bf16[3,8,128,128]{3,2,1,0:T(8,128)(2,1)S(1)}, bf16[3,8,128,128]{3,2,1,0:T(8,128)(2,1)}, u32[]{:S(2)}) copy-start(bf16[3,8,128,128]{3,2,1,0:T(8,128)(2,1)} %copy-done.2) | copy-start | bytes 2359300
  55.2 17.3 %collective-permute-start.9 = (bf16[32,32,384]{2,1,0:T(8,128)(2,1)}, bf16[32,32,384]{2,1,0:T(8,128)(2,1)}, u32[]{:S(2)}, u32[]{:S(2)}) collective-permute-start(bf16[32,32,384]{2,1,0:T(8,128)(2,1)} %add_convert_fusion.1), channel_id=1, source_target_pairs={{0,8},{8,0},{16,792},{24,272},{256,264},{264,256},{272,24},{280,52... | collective-permute-start | bytes 2359304 | tf_op jit(solution)/shard_map/layers/ppermute | solution.py:230
  59.5 4.5 %copy-start.7 = (bf16[32,32,384]{2,1,0:T(8,128)(2,1)S(1)}, bf16[32,32,384]{2,1,0:T(8,128)(2,1)}, u32[]{:S(2)}) copy-start(bf16[32,32,384]{2,1,0:T(8,128)(2,1)} %copy-done.6) | copy-start | bytes 2359300
  62.1 10.3 %collective-permute-start.4 = (bf16[4,8,4096]{2,1,0:T(8,128)(2,1)S(1)}, bf16[4,8,4096]{2,1,0:T(8,128)(2,1)S(1)}, u32[]{:S(2)}, u32[]{:S(2)}) collective-permute-start(bf16[4,8,4096]{2,1,0:T(8,128)(2,1)S(1)} %get-tuple-element.34), channel_id=1, source_target_pairs={{0,1},{1,0},{2,3},{3,2},{4,5},{5,4},{6,7},{7,6},{8,9},{9,8},{10,11... | collective-permute-start | bytes 786440 | tf_op jit(solution)/shard_map/partials/ppermute | solution.py:225
  74.7 44.0 %all-to-all-start.1 = ((bf16[32,32,384]{2,1,0:T(8,128)(2,1)}), bf16[32,32,384]{2,1,0:T(8,128)(2,1)S(1)}, u32[]{:S(2)}, u32[]{:S(2)}) async-start(bf16[32,32,384]{2,1,0:T(8,128)(2,1)} %add_convert_fusion), calls=%async_computation.1 | async-start | bytes 1572864 | tf_op jit(solution)/shard_map/tile_sums/all_to_all | solution.py:233
  93.1 10.2 %collective-permute-start.5 = (bf16[8,4096]{1,0:T(8,128)(2,1)S(1)}, bf16[8,4096]{1,0:T(8,128)(2,1)S(1)}, u32[]{:S(2)}, u32[]{:S(2)}) collective-permute-start(bf16[8,4096]{1,0:T(8,128)(2,1)S(1)} %get-tuple-element.42), channel_id=1, source_target_pairs={{0,2},{1,3},{2,4},{3,5},{4,6},{5,7},{6,0},{7,1},{8,10},{9,11},{10,... | collective-permute-start | bytes 196616 | tf_op jit(solution)/shard_map/partials/ppermute | solution.py:238
  95.2 10.1 %collective-permute-start.7 = (bf16[8,4096]{1,0:T(8,128)(2,1)S(1)}, bf16[8,4096]{1,0:T(8,128)(2,1)S(1)}, u32[]{:S(2)}, u32[]{:S(2)}) collective-permute-start(bf16[8,4096]{1,0:T(8,128)(2,1)S(1)} %get-tuple-element.43), channel_id=1, source_target_pairs={{0,4},{1,5},{2,6},{3,7},{4,0},{5,1},{6,2},{7,3},{8,12},{9,13},{10,... | collective-permute-start | bytes 196616 | tf_op jit(solution)/shard_map/partials/ppermute | solution.py:238
  99.5 8.9 %collective-permute-start.6 = (bf16[8,4096]{1,0:T(8,128)(2,1)S(1)}, bf16[8,4096]{1,0:T(8,128)(2,1)S(1)}, u32[]{:S(2)}, u32[]{:S(2)}) collective-permute-start(bf16[8,4096]{1,0:T(8,128)(2,1)S(1)} %get-tuple-element.44), channel_id=1, source_target_pairs={{0,6},{1,7},{2,0},{3,1},{4,2},{5,3},{6,4},{7,5},{8,14},{9,15},{10,... | collective-permute-start | bytes 196616 | tf_op jit(solution)/shard_map/partials/ppermute | solution.py:238
  (3 other events, 2.9 us)

commit v10 on v5

--- a/solution.py
+++ b/solution.py
@@ -209,19 +209,20 @@
     add = lambda *terms: sum(t.astype(F32) for t in terms).astype(BF16)
     with jax.named_scope("partials"):
         got = lax.ppermute(give, "x", [(i, i ^ 1) for i in range(line)])
-        pair = [add(keep[k], got[k]) for k in range(line // 2)]
-        ring = lambda d: [(i, (i + d) % line) for i in range(line)]
-        came = [lax.ppermute(pair[k], "x", ring(2 * k)) for k in (1, 3, 2)]
-        input_sum = add(*[t.astype(F32) for t in (keep[0], got[0])], *came)
-    own_mine, got = lax.optimization_barrier((own_mine, got))
     with jax.named_scope("cores"):
         far_got = lax.ppermute(far_theirs, "c", SWAP)
         own_got = lax.ppermute(own_theirs, "c", SWAP)
     with jax.named_scope("layers"):
         near = lax.ppermute(add(far_mine, far_got), LAYERS, beside())
     with jax.named_scope("tile_sums"):
-        grads = lax.all_to_all(add(own_mine, own_got, near), ("zh", "y"), 0, 0, tiled=True)
+        own_sum, give = lax.optimization_barrier((add(own_mine, own_got), give))
+        grads = lax.all_to_all(add(own_sum, near), ("zh", "y"), 0, 0, tiled=True)
         sums = jnp.sum(grads.astype(F32), axis=0)
+    with jax.named_scope("partials"):
+        pair = [add(keep[k], got[k]) for k in range(line // 2)]
+        ring = lambda d: [(i, (i + d) % line) for i in range(line)]
+        came = [lax.ppermute(pair[k], "x", ring(2 * k)) for k in (1, 3, 2)]
+        input_sum = add(*[t.astype(F32) for t in (keep[0], got[0])], *came)
     return (input_sum, sums[None])
 
 

time: 115 us -> 115 us (level)
  starting transfers between devices: 68.5 us -> 67.1 us
    ppermute x1, waiting for transfers between devices: 5.21 us -> 0.01 us  [per_device(): got = lax.ppermute(give, 'x', [(i, i ^ 1) for i in range(line)])]
    ppermute x1, waiting for transfers between devices: 0.01 us -> 3.79 us  [per_device(): near = lax.ppermute(add(far_mine, far_got), LAYERS, beside())]
    all_to_all x1, starting transfers between devices: 21.1 us -> 19.7 us  [per_device(): grads = lax.all_to_all(add(own_sum, near), ('zh', 'y'), 0, 0, tiled=True)]
    convert_element_type x4 -> x5, other arithmetic: 4.45 us -> 5.37 us  [per_device(): add = lambda *terms: sum((t.astype(F32) for t in terms)).astype(BF16)]
  transfers between devices with their start and end apart: 12 -> 12, of which waited for: 6 -> 6; matrix products, arithmetic and copies ran while one was open for 2% -> 5% of each run, Pallas kernels for 2% -> 2%
where the time goes in v10:
time: 115 us; the launch traced here: 114 us
  starting transfers between devices  67.1 us (58%)
  waiting for transfers between devices  27.3 us (24%)
  Pallas kernels  7.47 us (6%)
  other arithmetic  7.15 us (6%)
  local copies, waits for them, and re-layouts  4.11 us (4%)
    all_to_all x1, starting transfers between devices, per_device(): grads = lax.all_to_all(add(own_sum, near), ('zh', 'y'), 0, 0, tiled=True)  19.7 us
    ppermute x1, starting transfers between devices, per_device(): rb = lax.ppermute(ra, 'c', SWAP)  13.1 us
    ppermute x3, starting transfers between devices, per_device(): came = [lax.ppermute(pair[k], 'x', ring(2 * k)) for k in (1, 3, 2)]  10.4 us
    all_to_all x1, waiting for transfers between devices, per_device(): grads = lax.all_to_all(add(own_sum, near), ('zh', 'y'), 0, 0, tiled=True)  8.78 us
    ppermute x1, waiting for transfers between devices, per_device(): far = lax.ppermute(index, 'zl', SWAP)  8.09 us
    pallas_call x3, Pallas kernels, call(): pl.pallas_call(kernel, out_shape=out_shape, in_specs=[SMEM] * len(scalars...  7.47 us
    all_to_all x1, starting transfers between devices, per_device(): xa = lax.all_to_all(send, 'x', 0, 0, tiled=True).reshape(rows, 2 * width)  6.9 us
    convert_element_type x5, other arithmetic, per_device(): add = lambda *terms: sum((t.astype(F32) for t in terms)).astype(BF16)  5.37 us
  transfers between devices with their start and end apart: 12, of which 6 were waited for; matrix products, arithmetic and copies ran while one was open for 5% of the time, Pallas kernels for 2%

profile of v10, /device:TPU:16, one launch (start us, length us, event | category | flops | bytes accessed | tf_op | source)
XLA Modules:
  0.0 114.0 jit_solution(6876912302655961195)
XLA Ops:
  2.6 6.9 %all-to-all-start = ((bf16[8,8,8192]{2,1,0:T(8,128)(2,1)}), bf16[8,8,8192]{2,1,0:T(8,128)(2,1)S(1)}, u32[]{:S(2)}, u32[]{:S(2)}) async-start(bf16[8,8,8192]{2,1,0:T(8,128)(2,1)} %broadcast_in_dim.4), calls=%async_computation | async-start | bytes 2097152 | tf_op jit(solution)/shard_map/gather/all_to_all | solution.py:171
  9.8 5.2 %collective-permute-start = (bf16[3,8,128,128]{3,2,1,0:T(8,128)(2,1)S(1)}, bf16[3,8,128,128]{3,2,1,0:T(8,128)(2,1)S(1)}, u32[]{:S(2)}, u32[]{:S(2)}) collective-permute-start(bf16[3,8,128,128]{3,2,1,0:T(8,128)(2,1)S(1)} %pad_maximum_fusion), channel_id=1, source_target_pairs={{0,8},{8,0},{16,792},{24,272},{256,264},{264,256},{272,24},{280,52... | collective-permute-start | bytes 2359304 | tf_op jit(solution)/shard_map/weights/ppermute | solution.py:178
  15.0 1.9 %collective-permute-start.1 = (s32[1,48]{1,0:T(1,128)S(1)}, s32[1,48]{1,0:T(1,128)S(1)}, u32[]{:S(2)}, u32[]{:S(2)}) collective-permute-start(s32[1,48]{1,0:T(1,128)S(1)} %pad_add_fusion), channel_id=1, source_target_pairs={{0,8},{8,0},{1,9},{9,1},{2,10},{10,2},{3,11},{11,3},{4,12},{12,4},... | collective-permute-start | bytes 584 | tf_op jit(solution)/shard_map/weights/ppermute | solution.py:177
  17.0 8.1 %collective-permute-done.1.far = s32[1,48]{1,0:T(1,128)S(1)} collective-permute-done((s32[1,48]{1,0:T(1,128)S(1)}, s32[1,48]{1,0:T(1,128)S(1)}, u32[]{:S(2)}, u32[]{:S(2)}) %collective-permute-start.1) | collective-permute-done | bytes 224 | tf_op jit(solution)/shard_map/weights/ppermute | solution.py:177
  25.0 13.1 %collective-permute-start.2 = (bf16[3,8,128,128]{3,2,1,0:T(8,128)(2,1)S(1)}, bf16[3,8,128,128]{3,2,1,0:T(8,128)(2,1)S(1)}, u32[]{:S(2)}, u32[]{:S(2)}) collective-permute-start(bf16[3,8,128,128]{3,2,1,0:T(8,128)(2,1)S(1)} %collective-permute-done.ra), channel_id=1, source_target_pairs={{0,16},{16,0},{1,17},{17,1},{2,18},{18,2},{3,19},{19,3},{4,20},{20... | collective-permute-start | bytes 2359304 | tf_op jit(solution)/shard_map/weights/ppermute | solution.py:180
  38.1 1.9 %collective-permute-done.2.rb = bf16[3,8,128,128]{3,2,1,0:T(8,128)(2,1)S(1)} collective-permute-done((bf16[3,8,128,128]{3,2,1,0:T(8,128)(2,1)S(1)}, bf16[3,8,128,128]{3,2,1,0:T(8,128)(2,1)S(1)}, u32[]{:S(2)}, u32[]{:S(2)}) %collective-permute-start.2) | collective-permute-done | bytes 786464 | tf_op jit(solution)/shard_map/weights/ppermute | solution.py:180
  40.9 1.1 copy-done.3
  42.0 2.3 %forward.1 = (bf16[8,64,128]{2,1,0:T(8,128)(2,1)S(1)}, bf16[8,64,128]{2,1,0:T(8,128)(2,1)S(1)}, bf16[8,64,128]{2,1,0:T(8,128)(2,1)S(1)}) custom-call(s32[1,16]{1,0:T(1,128)S(1)} %copy-done.10, s32[1,16]{1,0:T(1,128)S(1)} %copy-done.11, s32[1,16]{1,0:T(1,128)S(1)} %copy-done.12, s32[1,48]{1,0:T(1,128)S(1)} %collective-permute-done.1.far, s32[1]{0:T(128)} %bitcast.core, ...), custom_call_target="tpu_custom_call" | custom-call | flops 201326592 | bytes 6291456 | tf_op jit(solution)/shard_map/forward/pallas_call | solution.py:145
  44.4 2.6 %tile_terms.1 = (bf16[32,32,384]{2,1,0:T(8,128)(2,1)S(1)}, bf16[32,32,384]{2,1,0:T(8,128)(2,1)}, bf16[32,32,384]{2,1,0:T(8,128)(2,1)S(1)}, bf16[32,32,384]{2,1,0:T(8,128)(2,1)S(1)}) custom-call(s32[1,16]{1,0:T(1,128)S(1)} %copy-done.10, s32[1,16]{1,0:T(1,128)S(1)} %copy-done.11, s32[1,16]{1,0:T(1,128)S(1)} %copy-done.12, ...), custom_call_target="tpu_custom_call" | custom-call | flops 201326592 | bytes 6291456 | tf_op jit(solution)/shard_map/tile_terms/pallas_call | solution.py:145
  47.0 2.3 %collective-permute-start.8 = (bf16[32,32,384]{2,1,0:T(8,128)(2,1)S(1)}, bf16[32,32,384]{2,1,0:T(8,128)(2,1)S(1)}, u32[]{:S(2)}, u32[]{:S(2)}) collective-permute-start(bf16[32,32,384]{2,1,0:T(8,128)(2,1)S(1)} %get-tuple-element.35), channel_id=1, source_target_pairs={{0,16},{16,0},{1,17},{17,1},{2,18},{18,2},{3,19},{19,3},{4,20},{20... | collective-permute-start | bytes 2359304 | tf_op jit(solution)/shard_map/cores/ppermute | solution.py:213
  49.2 2.0 %collective-permute-start.7 = (bf16[32,32,384]{2,1,0:T(8,128)(2,1)}, bf16[32,32,384]{2,1,0:T(8,128)(2,1)}, u32[]{:S(2)}, u32[]{:S(2)}) collective-permute-start(bf16[32,32,384]{2,1,0:T(8,128)(2,1)} %get-tuple-element.32), channel_id=1, source_target_pairs={{0,16},{16,0},{1,17},{17,1},{2,18},{18,2},{3,19},{19,3},{4,20},{20... | collective-permute-start | bytes 2359304 | tf_op jit(solution)/shard_map/cores/ppermute | solution.py:214
  52.4 2.5 %collective-permute-start.9 = (bf16[32,32,384]{2,1,0:T(8,128)(2,1)}, bf16[32,32,384]{2,1,0:T(8,128)(2,1)}, u32[]{:S(2)}, u32[]{:S(2)}) collective-permute-start(bf16[32,32,384]{2,1,0:T(8,128)(2,1)} %add_convert_fusion.1), channel_id=1, source_target_pairs={{0,8},{8,0},{16,792},{24,272},{256,264},{264,256},{272,24},{280,52... | collective-permute-start | bytes 2359304 | tf_op jit(solution)/shard_map/layers/ppermute | solution.py:216
  55.9 2.6 %back.1 = (bf16[4,8,4096]{2,1,0:T(8,128)(2,1)S(1)}, bf16[8,4096]{1,0:T(8,128)(2,1)S(1)}, bf16[8,4096]{1,0:T(8,128)(2,1)S(1)}, bf16[8,4096]{1,0:T(8,128)(2,1)S(1)}, bf16[8,4096]{1,0:T(8,128)(2,1)S(1)}) custom-call(s32[1,16]{1,0:T(1,128)S(1)} %copy-done.10, s32[1,16]{1,0:T(1,128)S(1)} %copy-done.11, s32[1,48]{1,0:T(1,128)S(1)} %collective-permute-done.1.far, ...), custom_call_target="tpu_custom_call" | custom-call | flops 134217728 | bytes 6291456 | tf_op jit(solution)/shard_map/back/pallas_call | solution.py:145
  58.4 3.0 %collective-permute-start.3 = (bf16[4,8,4096]{2,1,0:T(8,128)(2,1)S(1)}, bf16[4,8,4096]{2,1,0:T(8,128)(2,1)S(1)}, u32[]{:S(2)}, u32[]{:S(2)}) collective-permute-start(bf16[4,8,4096]{2,1,0:T(8,128)(2,1)S(1)} %get-tuple-element.26), channel_id=1, source_target_pairs={{0,1},{1,0},{2,3},{3,2},{4,5},{5,4},{6,7},{7,6},{8,9},{9,8},{10,11... | collective-permute-start | bytes 786440 | tf_op jit(solution)/shard_map/partials/ppermute | solution.py:211
  61.5 1.3 %add_convert_fusion.2 = bf16[32,32,384]{2,1,0:T(8,128)(2,1)S(1)} fusion(bf16[32,32,384]{2,1,0:T(8,128)(2,1)} %collective-permute-done.7, bf16[32,32,384]{2,1,0:T(8,128)(2,1)S(1)} %copy-done.7), kind=kLoop, calls=%fused_computation.3 | loop fusion | flops 1572864 | bytes 2359296 | tf_op jit(solution)/shard_map/tile_sums/convert_element_type | solution.py:209
  62.8 3.8 %collective-permute-done.9 = bf16[32,32,384]{2,1,0:T(8,128)(2,1)} collective-permute-done((bf16[32,32,384]{2,1,0:T(8,128)(2,1)}, bf16[32,32,384]{2,1,0:T(8,128)(2,1)}, u32[]{:S(2)}, u32[]{:S(2)}) %collective-permute-start.9) | collective-permute-done | bytes 786464 | tf_op jit(solution)/shard_map/layers/ppermute | solution.py:216
  66.6 2.2 %add_convert_fusion = bf16[32,32,384]{2,1,0:T(8,128)(2,1)} fusion(bf16[32,32,384]{2,1,0:T(8,128)(2,1)} %collective-permute-done.9, bf16[32,32,384]{2,1,0:T(8,128)(2,1)S(1)} %add_convert_fusion.2), kind=kLoop, calls=%fused_computation.1 | loop fusion | flops 1572864 | bytes 2359296 | tf_op jit(solution)/shard_map/tile_sums/convert_element_type | solution.py:209
  68.8 19.7 %all-to-all-start.1 = ((bf16[32,32,384]{2,1,0:T(8,128)(2,1)}), bf16[32,32,384]{2,1,0:T(8,128)(2,1)S(1)}, u32[]{:S(2)}, u32[]{:S(2)}) async-start(bf16[32,32,384]{2,1,0:T(8,128)(2,1)} %add_convert_fusion), calls=%async_computation.1 | async-start | bytes 1572864 | tf_op jit(solution)/shard_map/tile_sums/all_to_all | solution.py:219
  88.6 2.4 %collective-permute-start.4 = (bf16[8,4096]{1,0:T(8,128)(2,1)S(1)}, bf16[8,4096]{1,0:T(8,128)(2,1)S(1)}, u32[]{:S(2)}, u32[]{:S(2)}) collective-permute-start(bf16[8,4096]{1,0:T(8,128)(2,1)S(1)} %get-tuple-element.36), channel_id=1, source_target_pairs={{0,2},{1,3},{2,4},{3,5},{4,6},{5,7},{6,0},{7,1},{8,10},{9,11},{10,... | collective-permute-start | bytes 196616 | tf_op jit(solution)/shard_map/partials/ppermute | solution.py:224
  91.0 4.2 %collective-permute-start.6 = (bf16[8,4096]{1,0:T(8,128)(2,1)S(1)}, bf16[8,4096]{1,0:T(8,128)(2,1)S(1)}, u32[]{:S(2)}, u32[]{:S(2)}) collective-permute-start(bf16[8,4096]{1,0:T(8,128)(2,1)S(1)} %get-tuple-element.37), channel_id=1, source_target_pairs={{0,4},{1,5},{2,6},{3,7},{4,0},{5,1},{6,2},{7,3},{8,12},{9,13},{10,... | collective-permute-start | bytes 196616 | tf_op jit(solution)/shard_map/partials/ppermute | solution.py:224
  95.3 3.8 %collective-permute-start.5 = (bf16[8,4096]{1,0:T(8,128)(2,1)S(1)}, bf16[8,4096]{1,0:T(8,128)(2,1)S(1)}, u32[]{:S(2)}, u32[]{:S(2)}) collective-permute-start(bf16[8,4096]{1,0:T(8,128)(2,1)S(1)} %get-tuple-element.38), channel_id=1, source_target_pairs={{0,6},{1,7},{2,0},{3,1},{4,2},{5,3},{6,4},{7,5},{8,14},{9,15},{10,... | collective-permute-start | bytes 196616 | tf_op jit(solution)/shard_map/partials/ppermute | solution.py:224
  99.1 2.7 %collective-permute-done.6 = bf16[8,4096]{1,0:T(8,128)(2,1)S(1)} collective-permute-done((bf16[8,4096]{1,0:T(8,128)(2,1)S(1)}, bf16[8,4096]{1,0:T(8,128)(2,1)S(1)}, u32[]{:S(2)}, u32[]{:S(2)}) %collective-permute-start.6) | collective-permute-done | bytes 65568 | tf_op jit(solution)/shard_map/partials/ppermute | solution.py:224
  101.8 2.0 %collective-permute-done.5 = bf16[8,4096]{1,0:T(8,128)(2,1)S(1)} collective-permute-done((bf16[8,4096]{1,0:T(8,128)(2,1)S(1)}, bf16[8,4096]{1,0:T(8,128)(2,1)S(1)}, u32[]{:S(2)}, u32[]{:S(2)}) %collective-permute-start.5) | collective-permute-done | bytes 65568 | tf_op jit(solution)/shard_map/partials/ppermute | solution.py:224
  104.5 8.8 %all-to-all-done.1 = bf16[32,32,384]{2,1,0:T(8,128)(2,1)S(1)} async-done(((bf16[32,32,384]{2,1,0:T(8,128)(2,1)}), bf16[32,32,384]{2,1,0:T(8,128)(2,1)S(1)}, u32[]{:S(2)}, u32[]{:S(2)}) %all-to-all-start.1) | async-done | bytes 786464 | tf_op jit(solution)/shard_map/tile_sums/all_to_all | solution.py:219
  (41 shorter events, 6.6 us)
Async XLA Ops:
  2.6 6.9 %copy-start = (bf16[1,16,128,128]{3,2,1,0:T(8,128)(2,1)S(1)}, bf16[1,16,128,128]{3,2,1,0:T(8,128)(2,1)}, u32[]{:S(2)}) copy-start(bf16[1,16,128,128]{3,2,1,0:T(8,128)(2,1)} %param.10) | copy-start | bytes 1572868
  2.6 7.0 %copy-start.10 = (s32[1,16]{1,0:T(1,128)S(1)}, s32[1,16]{1,0:T(1,128)}, u32[]{:S(2)}) copy-start(s32[1,16]{1,0:T(1,128)} %g_idx.5) | copy-start | bytes 196
  2.6 7.0 %copy-start.11 = (s32[1,16]{1,0:T(1,128)S(1)}, s32[1,16]{1,0:T(1,128)}, u32[]{:S(2)}) copy-start(s32[1,16]{1,0:T(1,128)} %u_idx.5) | copy-start | bytes 196
  2.6 7.0 %copy-start.12 = (s32[1,16]{1,0:T(1,128)S(1)}, s32[1,16]{1,0:T(1,128)}, u32[]{:S(2)}) copy-start(s32[1,16]{1,0:T(1,128)} %d_idx.3) | copy-start | bytes 196
  2.6 7.1 %copy-start.1 = (bf16[1,16,128,128]{3,2,1,0:T(8,128)(2,1)S(1)}, bf16[1,16,128,128]{3,2,1,0:T(8,128)(2,1)}, u32[]{:S(2)}) copy-start(bf16[1,16,128,128]{3,2,1,0:T(8,128)(2,1)} %param.11) | copy-start | bytes 1572868
  2.6 7.1 %copy-start.5 = (bf16[1,16,128,128]{3,2,1,0:T(8,128)(2,1)S(1)}, bf16[1,16,128,128]{3,2,1,0:T(8,128)(2,1)}, u32[]{:S(2)}) copy-start(bf16[1,16,128,128]{3,2,1,0:T(8,128)(2,1)} %param.12) | copy-start | bytes 1572868
  2.6 38.3 %all-to-all-start = ((bf16[8,8,8192]{2,1,0:T(8,128)(2,1)}), bf16[8,8,8192]{2,1,0:T(8,128)(2,1)S(1)}, u32[]{:S(2)}, u32[]{:S(2)}) async-start(bf16[8,8,8192]{2,1,0:T(8,128)(2,1)} %broadcast_in_dim.4), calls=%async_computation | async-start | bytes 2097152 | tf_op jit(solution)/shard_map/gather/all_to_all | solution.py:171
  9.8 15.2 %collective-permute-start = (bf16[3,8,128,128]{3,2,1,0:T(8,128)(2,1)S(1)}, bf16[3,8,128,128]{3,2,1,0:T(8,128)(2,1)S(1)}, u32[]{:S(2)}, u32[]{:S(2)}) collective-permute-start(bf16[3,8,128,128]{3,2,1,0:T(8,128)(2,1)S(1)} %pad_maximum_fusion), channel_id=1, source_target_pairs={{0,8},{8,0},{16,792},{24,272},{256,264},{264,256},{272,24},{280,52... | collective-permute-start | bytes 2359304 | tf_op jit(solution)/shard_map/weights/ppermute | solution.py:178
  15.0 10.0 %collective-permute-start.1 = (s32[1,48]{1,0:T(1,128)S(1)}, s32[1,48]{1,0:T(1,128)S(1)}, u32[]{:S(2)}, u32[]{:S(2)}) collective-permute-start(s32[1,48]{1,0:T(1,128)S(1)} %pad_add_fusion), channel_id=1, source_target_pairs={{0,8},{8,0},{1,9},{9,1},{2,10},{10,2},{3,11},{11,3},{4,12},{12,4},... | collective-permute-start | bytes 584 | tf_op jit(solution)/shard_map/weights/ppermute | solution.py:177
  25.0 15.0 %collective-permute-start.2 = (bf16[3,8,128,128]{3,2,1,0:T(8,128)(2,1)S(1)}, bf16[3,8,128,128]{3,2,1,0:T(8,128)(2,1)S(1)}, u32[]{:S(2)}, u32[]{:S(2)}) collective-permute-start(bf16[3,8,128,128]{3,2,1,0:T(8,128)(2,1)S(1)} %collective-permute-done.ra), channel_id=1, source_target_pairs={{0,16},{16,0},{1,17},{17,1},{2,18},{18,2},{3,19},{19,3},{4,20},{20... | collective-permute-start | bytes 2359304 | tf_op jit(solution)/shard_map/weights/ppermute | solution.py:180
  40.9 1.1 copy-start.3
  44.4 8.0 %copy-start.8 = (bf16[8,64,128]{2,1,0:T(8,128)(2,1)}, bf16[8,64,128]{2,1,0:T(8,128)(2,1)S(1)}, u32[]{:S(2)}) copy-start(bf16[8,64,128]{2,1,0:T(8,128)(2,1)S(1)} %get-tuple-element.24.dup) | copy-start | bytes 393220
  47.0 5.4 %copy-start.6 = (bf16[32,32,384]{2,1,0:T(8,128)(2,1)}, bf16[32,32,384]{2,1,0:T(8,128)(2,1)S(1)}, u32[]{:S(2)}) copy-start(bf16[32,32,384]{2,1,0:T(8,128)(2,1)S(1)} %get-tuple-element.31) | copy-start | bytes 2359300
  47.0 4.3 %collective-permute-start.8 = (bf16[32,32,384]{2,1,0:T(8,128)(2,1)S(1)}, bf16[32,32,384]{2,1,0:T(8,128)(2,1)S(1)}, u32[]{:S(2)}, u32[]{:S(2)}) collective-permute-start(bf16[32,32,384]{2,1,0:T(8,128)(2,1)S(1)} %get-tuple-element.35), channel_id=1, source_target_pairs={{0,16},{16,0},{1,17},{17,1},{2,18},{18,2},{3,19},{19,3},{4,20},{20... | collective-permute-start | bytes 2359304 | tf_op jit(solution)/shard_map/cores/ppermute | solution.py:213
  49.2 12.2 %collective-permute-start.7 = (bf16[32,32,384]{2,1,0:T(8,128)(2,1)}, bf16[32,32,384]{2,1,0:T(8,128)(2,1)}, u32[]{:S(2)}, u32[]{:S(2)}) collective-permute-start(bf16[32,32,384]{2,1,0:T(8,128)(2,1)} %get-tuple-element.32), channel_id=1, source_target_pairs={{0,16},{16,0},{1,17},{17,1},{2,18},{18,2},{3,19},{19,3},{4,20},{20... | collective-permute-start | bytes 2359304 | tf_op jit(solution)/shard_map/cores/ppermute | solution.py:214
  51.3 3.6 %copy-start.4 = (bf16[3,8,128,128]{3,2,1,0:T(8,128)(2,1)S(1)}, bf16[3,8,128,128]{3,2,1,0:T(8,128)(2,1)}, u32[]{:S(2)}) copy-start(bf16[3,8,128,128]{3,2,1,0:T(8,128)(2,1)} %copy-done.2) | copy-start | bytes 2359300
  52.4 14.2 %collective-permute-start.9 = (bf16[32,32,384]{2,1,0:T(8,128)(2,1)}, bf16[32,32,384]{2,1,0:T(8,128)(2,1)}, u32[]{:S(2)}, u32[]{:S(2)}) collective-permute-start(bf16[32,32,384]{2,1,0:T(8,128)(2,1)} %add_convert_fusion.1), channel_id=1, source_target_pairs={{0,8},{8,0},{16,792},{24,272},{256,264},{264,256},{272,24},{280,52... | collective-permute-start | bytes 2359304 | tf_op jit(solution)/shard_map/layers/ppermute | solution.py:216
  54.9 0.9 copy-start.9
  55.9 5.6 %copy-start.7 = (bf16[32,32,384]{2,1,0:T(8,128)(2,1)S(1)}, bf16[32,32,384]{2,1,0:T(8,128)(2,1)}, u32[]{:S(2)}) copy-start(bf16[32,32,384]{2,1,0:T(8,128)(2,1)} %copy-done.6) | copy-start | bytes 2359300
  58.4 30.1 %collective-permute-start.3 = (bf16[4,8,4096]{2,1,0:T(8,128)(2,1)S(1)}, bf16[4,8,4096]{2,1,0:T(8,128)(2,1)S(1)}, u32[]{:S(2)}, u32[]{:S(2)}) collective-permute-start(bf16[4,8,4096]{2,1,0:T(8,128)(2,1)S(1)} %get-tuple-element.26), channel_id=1, source_target_pairs={{0,1},{1,0},{2,3},{3,2},{4,5},{5,4},{6,7},{7,6},{8,9},{9,8},{10,11... | collective-permute-start | bytes 786440 | tf_op jit(solution)/shard_map/partials/ppermute | solution.py:211
  68.8 44.5 %all-to-all-start.1 = ((bf16[32,32,384]{2,1,0:T(8,128)(2,1)}), bf16[32,32,384]{2,1,0:T(8,128)(2,1)S(1)}, u32[]{:S(2)}, u32[]{:S(2)}) async-start(bf16[32,32,384]{2,1,0:T(8,128)(2,1)} %add_convert_fusion), calls=%async_computation.1 | async-start | bytes 1572864 | tf_op jit(solution)/shard_map/tile_sums/all_to_all | solution.py:219
  88.6 10.5 %collective-permute-start.4 = (bf16[8,4096]{1,0:T(8,128)(2,1)S(1)}, bf16[8,4096]{1,0:T(8,128)(2,1)S(1)}, u32[]{:S(2)}, u32[]{:S(2)}) collective-permute-start(bf16[8,4096]{1,0:T(8,128)(2,1)S(1)} %get-tuple-element.36), channel_id=1, source_target_pairs={{0,2},{1,3},{2,4},{3,5},{4,6},{5,7},{6,0},{7,1},{8,10},{9,11},{10,... | collective-permute-start | bytes 196616 | tf_op jit(solution)/shard_map/partials/ppermute | solution.py:224
  91.0 10.8 %collective-permute-start.6 = (bf16[8,4096]{1,0:T(8,128)(2,1)S(1)}, bf16[8,4096]{1,0:T(8,128)(2,1)S(1)}, u32[]{:S(2)}, u32[]{:S(2)}) collective-permute-start(bf16[8,4096]{1,0:T(8,128)(2,1)S(1)} %get-tuple-element.37), channel_id=1, source_target_pairs={{0,4},{1,5},{2,6},{3,7},{4,0},{5,1},{6,2},{7,3},{8,12},{9,13},{10,... | collective-permute-start | bytes 196616 | tf_op jit(solution)/shard_map/partials/ppermute | solution.py:224
  95.3 8.6 %collective-permute-start.5 = (bf16[8,4096]{1,0:T(8,128)(2,1)S(1)}, bf16[8,4096]{1,0:T(8,128)(2,1)S(1)}, u32[]{:S(2)}, u32[]{:S(2)}) collective-permute-start(bf16[8,4096]{1,0:T(8,128)(2,1)S(1)} %get-tuple-element.38), channel_id=1, source_target_pairs={{0,6},{1,7},{2,0},{3,1},{4,2},{5,3},{6,4},{7,5},{8,14},{9,15},{10,... | collective-permute-start | bytes 196616 | tf_op jit(solution)/shard_map/partials/ppermute | solution.py:224
  (1 other events, 0.9 us)
